TPU v7x, 256 devices: a whole 4x4x8 slice. The times are simulated.
256 devices in a mesh: clip: 2 (over core), seq: 128 (over x, z, y).
Axes of the slice: x: 4, y: 4, z: 8, core: 2. Of those that a mesh axis runs over, the one named last changes fastest.
Arguments:
- latents: bfloat16 [256, 128, 1280], P(('clip', 'seq')), parts along dimension 0, may hold values from -6 to 6
- ref_hidden: bfloat16 [256, 1280], P(('clip', 'seq')), parts along dimension 0, may hold values from -6 to 6
- gain_spatial: float32 [1280], replicated, may hold values from 0.25 to 1.75
- w_qkv_spatial: bfloat16 [1280, 1920], P(None, 'seq'), may hold values from -8 to 8
- w_out_spatial: bfloat16 [640, 1280], P(None, 'seq'), may hold values from -0.25 to 0.25
- temporal_norm_gain: float32 [1280], replicated, may hold values from 0.25 to 1.75
- w_qkv_temporal: bfloat16 [1280, 1920], P(None, 'seq'), may hold values from -8 to 8
- w_out_temporal: bfloat16 [640, 1280], P(None, 'seq'), may hold values from -0.25 to 0.25
Outputs:
- mixed: bfloat16 [256, 128, 1280], P(('clip', 'seq')), parts along dimension 0
There are 2 independent parts, one for each index of `clip`. A program takes and returns all parts, laid end to end along the dimension named above; an argument that names none is the same for every part. Nothing has to cross between parts.
All inputs are finite; a program needn't handle non-finite values.
Results may differ from a plain program's by a relative error of at most 0.0095.
Values may be sent and summed in bfloat16 or wider, within the bound.
No kernel may reach another device: no remote copies, remote signals or barrier semaphores. Data moves between devices by JAX's collectives and lax.ppermute only.
A program may use at most 64 MiB of HBM per device.

v0:
```python
import jax
import jax.numpy as jnp
from jax import lax
from jax.sharding import PartitionSpec as P

D = 1280
HEADS = 10
HEAD = 64
INNER = 640


epsilon = 1e-05


def layer_norm(states, scale_gain):
    widened = states.astype(jnp.float32)
    average = jnp.mean(widened, axis=-1, keepdims=True)
    spread = jnp.mean((widened - average) ** 2, axis=-1, keepdims=True)
    return ((widened - average) * lax.rsqrt(spread + epsilon) * scale_gain).astype(jnp.bfloat16)


def attend(queries, keys_all, values):
    softmax_scale_factor = HEAD ** (-0.5)

    def one_head(operands):
        per_head_queries, per_head_keys, per_head_values = operands
        attention_logits = (
            jnp.einsum(
                "haf,hgf->hag", per_head_queries, per_head_keys, preferred_element_type=jnp.float32
            )
            * softmax_scale_factor
        )
        top = jnp.max(attention_logits, axis=-1, keepdims=True)
        expo = jnp.exp(attention_logits - top)
        attention_probabilities = (expo / jnp.sum(expo, axis=-1, keepdims=True)).astype(
            jnp.bfloat16
        )
        return jnp.einsum(
            "pzt,ptg->pzg",
            attention_probabilities,
            per_head_values,
            preferred_element_type=jnp.float32,
        ).astype(jnp.bfloat16)

    heads_first = lax.map(
        one_head,
        (
            queries.transpose(2, 0, 1, 3),
            keys_all.transpose(2, 0, 1, 3),
            values.transpose(2, 0, 1, 3),
        ),
    )
    return heads_first.transpose(1, 2, 0, 3)


def spatial_project(stacked, w_qkv_spatial):

    def project(shard_part, offset):
        return jnp.dot(stacked, shard_part, preferred_element_type=jnp.float32)

    return project(lax.all_gather(w_qkv_spatial, "seq", axis=1, tiled=True), jnp.int32(0))


def spatial_output(attn_rows, w_out_spatial):

    def project(shard_part, offset):
        return jnp.dot(attn_rows, shard_part, preferred_element_type=jnp.float32)

    return project(lax.all_gather(w_out_spatial, "seq", axis=1, tiled=True), jnp.int32(0))


def temporal_project(tnormed, w_qkv_temporal):

    def project(shard_part, offset):
        return jnp.dot(tnormed, shard_part, preferred_element_type=jnp.float32)

    return project(lax.all_gather(w_qkv_temporal, "seq", axis=1, tiled=True), jnp.int32(0)).astype(
        jnp.bfloat16
    )


def temporal_output(attn_rows, w_out_temporal):

    def project(shard_part, offset):
        return jnp.dot(attn_rows, shard_part, preferred_element_type=jnp.float32)

    return project(lax.all_gather(w_out_temporal, "seq", axis=1, tiled=True), jnp.int32(0))


def body(
    latents,
    ref_hidden,
    gain_spatial,
    w_qkv_spatial,
    w_out_spatial,
    temporal_norm_gain,
    w_qkv_temporal,
    w_out_temporal,
):
    frame_count = latents.shape[0]
    pixel_count = latents.shape[1]
    row_count = frame_count * pixel_count
    normed = layer_norm(latents, gain_spatial).reshape(row_count, D)
    ref_full = lax.all_gather(ref_hidden, "seq", axis=0, tiled=True)
    stacked = jnp.concatenate([normed, ref_full], axis=0)
    qkv_all = spatial_project(stacked, w_qkv_spatial).astype(jnp.bfloat16)
    frame_qkv = qkv_all[:row_count].reshape(frame_count, pixel_count, 3, HEADS, HEAD)
    ref_part = qkv_all[row_count:, INNER:]
    ref_kv = ref_part.reshape(pixel_count, 2, HEADS, HEAD)
    ref_keys = ref_kv[None, :, 0]
    ref_values = ref_kv[None, :, 1]
    keys_all = jnp.concatenate([frame_qkv[:, :, 1], ref_keys], axis=1)
    values_all = jnp.concatenate([frame_qkv[:, :, 2], ref_values], axis=1)
    spatial_attn = attend(frame_qkv[:, :, 0], keys_all, values_all).reshape(row_count, INNER)
    spatial_term = spatial_output(spatial_attn, w_out_spatial)
    hidden = (latents.reshape(row_count, D).astype(jnp.float32) + spatial_term).astype(jnp.bfloat16)
    hidden = hidden.reshape(frame_count, pixel_count, D)
    patches = lax.all_to_all(hidden, "seq", split_axis=1, concat_axis=0, tiled=True)
    all_frames = patches.shape[0]
    patch_count = patches.shape[1]
    tnormed = layer_norm(patches, temporal_norm_gain).reshape(all_frames * patch_count, D)
    temporal_qkv = temporal_project(tnormed, w_qkv_temporal)
    temporal_qkv = temporal_qkv.reshape(all_frames, patch_count, 3, HEADS, HEAD).transpose(
        1, 0, 2, 3, 4
    )
    temporal_attn = attend(temporal_qkv[:, :, 0], temporal_qkv[:, :, 1], temporal_qkv[:, :, 2])
    temporal_attn = temporal_attn.transpose(1, 0, 2, 3).reshape(all_frames * patch_count, INNER)
    updated = patches.reshape(all_frames * patch_count, D).astype(jnp.float32) + temporal_output(
        temporal_attn, w_out_temporal
    )
    updated = updated.astype(jnp.bfloat16).reshape(all_frames, patch_count, D)
    return lax.all_to_all(updated, "seq", split_axis=0, concat_axis=1, tiled=True)


def solution(mesh):
    in_specs = (
        P(("clip", "seq"), None, None),
        P(("clip", "seq"), None),
        P(),
        P(None, "seq"),
        P(None, "seq"),
        P(),
        P(None, "seq"),
        P(None, "seq"),
    )
    out_specs = P(("clip", "seq"), None, None)
    return jax.shard_map(body, mesh=mesh, in_specs=in_specs, out_specs=out_specs, check_vma=False)
```

profile of v0, /device:TPU:32, one launch (start us, length us, event | category | flops | bytes accessed | tf_op | source)
XLA Modules:
  0.0 531.0 jit_solution(12206717506313045455)
XLA Ops:
  6.5 0.7 all-gather.12.cloned.1.call-update
  7.3 0.7 all-gather.10.cloned.1.call-update
  8.1 0.7 all-gather.16.cloned.1.call-update
  8.8 0.5 all-gather.14.cloned.1.call-update
  9.3 342.1 %all-gather = bf16[128,1,1280]{2,1,0:T(2,128)(2,1)S(1)} all-gather(bf16[1,1,1280]{2,1,0:T(2,128)(2,1)} %bitcast.165), channel_id=1, replica_groups=mesh['clip'=2,'seq'=128] {'seq'}, dimensions={0}, use_global_device_ids=true | all-gather | bytes 330240 | tf_op jit(solution)/shard_map/all_gather | solution.py:104
  351.4 1.1 convert_reduce_fusion.1
  352.5 1.2 fusion.33
  353.8 0.9 fusion.46
  354.7 2.7 reshape.233
  357.5 7.6 %reshape.231 = bf16[1920,1280]{1,0:T(8,128)(2,1)} reshape(bf16[128,15,1280]{2,1,0:T(8,128)(2,1)} %all-gather.10.cloned.1.call-done) | data formatting | bytes 9830400
  365.1 3.9 convolution_convert_fusion.2
  369.2 0.3 copy.38
  369.4 0.2 copy.39
  369.8 7.3 %while.20 = (s32[]{:T(128)}, bf16[10,1,128,64]{2,3,1,0:T(8,128)(2,1)S(1)}, bf16[10,1,128,64]{2,3,0,1:T(8,128)(2,1)S(1)}, bf16[10,1,256,64]{2,3,0,1:T(8,128)(2,1)...) while((s32[]{:T(128)}, bf16[10,1,128,64]{2,3,1,0:T(8,128)(2,1)S(1)}, ...), condition=%wide.region_5.6_spmd, body=%wide.region_2.5_spmd.sunk | while | flops 8625922 | bytes 496197 | solution.py:45
  369.9 0.3 fusion.68
  370.1 0.2 fusion.69
  370.3 0.2 fusion.70
  370.6 0.3 fusion.68
  371.1 0.2 fusion.70
  371.3 0.3 fusion.68
  371.8 0.2 fusion.70
  372.1 0.3 fusion.68
  372.5 0.2 fusion.70
  372.8 0.3 fusion.68
  373.3 0.2 fusion.70
  373.5 0.3 fusion.68
  374.0 0.2 fusion.70
  374.3 0.3 fusion.68
  374.7 0.2 fusion.70
  375.0 0.3 fusion.68
  375.5 0.3 fusion.70
  375.7 0.3 fusion.68
  376.2 0.2 fusion.70
  376.5 0.3 fusion.68
  376.9 0.2 fusion.70
  377.2 0.6 fusion.29
  377.8 0.5 copy.64
  378.3 0.5 broadcast.101
  378.9 2.6 reduce.13
  381.4 0.8 reshape.238
  382.2 16.1 %all-to-all-start = ((bf16[128,2,640]{2,1,0:T(2,128)(2,1)}), bf16[128,2,640]{2,1,0:T(2,128)(2,1)S(1)}, u32[]{:S(2)}, u32[]{:S(2)}) async-start(bf16[128,2,640]{2,1,0:T(2,128)(2,1)} %reshape.238), calls=%async_computation | async-start | bytes 655360 | tf_op jit(solution)/shard_map/all_to_all | solution.py:118
  398.4 2.7 reshape.237
  401.1 81.4 %all-gather.14.cloned.1.call-done = bf16[128,15,1280]{2,1,0:T(8,128)(2,1)} async-done(((bf16[1,15,1280]{2,1,0:T(8,128)(2,1)}), bf16[128,15,1280]{2,1,0:T(8,128)(2,1)}) %all-gather.14.cloned.1.call-update) | async-done | bytes 4915216 | tf_op jit(solution)/shard_map/all_gather | solution.py:77
  482.5 7.6 %reshape.235 = bf16[1920,1280]{1,0:T(8,128)(2,1)} reshape(bf16[128,15,1280]{2,1,0:T(8,128)(2,1)} %all-gather.14.cloned.1.call-done) | data formatting | bytes 9830400
  490.1 0.3 reshape.239
  490.5 0.2 fusion.41
  490.8 4.1 convolution_convert_fusion.3
  494.9 0.3 copy.45
  495.3 4.3 while.21
  495.3 0.2 fusion.72
  495.7 0.2 fusion.72
  496.1 0.2 fusion.72
  496.5 0.2 fusion.72
  497.0 0.2 fusion.72
  497.4 0.2 fusion.72
  497.8 0.2 fusion.72
  498.3 0.2 fusion.72
  498.7 0.2 fusion.72
  499.1 0.2 fusion.72
  499.6 0.6 fusion.28
  500.2 0.8 reduce.14
  501.1 22.3 %all_to_all.21 = bf16[128,2,640]{2,1,0:T(2,128)(2,1)S(1)} all-to-all(bf16[128,2,640]{2,1,0:T(2,128)(2,1)S(1)} %reshape.240), channel_id=1, replica_groups=mesh['clip'=2,'seq'=128] {'seq'}, dimensions={0} | all-to-all | bytes 655360 | tf_op jit(solution)/shard_map/all_to_all | solution.py:132
  523.4 0.3 reshape.241
  523.7 0.8 copy.62
  (56 shorter events, 4.4 us)
Async XLA Ops:
  6.5 347.2 %copy-start = (bf16[1,128,1280]{2,1,0:T(8,128)(2,1)S(1)}, bf16[1,128,1280]{2,1,0:T(8,128)(2,1)}, u32[]{:S(2)}) copy-start(bf16[1,128,1280]{2,1,0:T(8,128)(2,1)} %param.12) | copy-start | bytes 983044
  6.5 348.2 %all-gather.12.cloned.1.call-start = ((), (), s32[]{:S(2)}) async-start(), calls=%async_computation.3 | async-start | bytes 2641920 | tf_op jit(solution)/shard_map/all_gather | solution.py:69
  7.3 350.2 %all-gather.10.cloned.1.call-start = ((), (), s32[]{:S(2)}) async-start(), calls=%async_computation.2 | async-start | bytes 5283840 | tf_op jit(solution)/shard_map/all_gather | solution.py:61
  8.0 390.3 %all-gather.16.cloned.1.call-start = ((), (), s32[]{:S(2)}) async-start(), calls=%async_computation.5 | async-start | bytes 2641920 | tf_op jit(solution)/shard_map/all_gather | solution.py:87
  8.7 473.8 %all-gather.14.cloned.1.call-start = ((), (), s32[]{:S(2)}) async-start(), calls=%async_computation.4 | async-start | bytes 5283840 | tf_op jit(solution)/shard_map/all_gather | solution.py:77
  382.2 107.9 %all-to-all-start = ((bf16[128,2,640]{2,1,0:T(2,128)(2,1)}), bf16[128,2,640]{2,1,0:T(2,128)(2,1)S(1)}, u32[]{:S(2)}, u32[]{:S(2)}) async-start(bf16[128,2,640]{2,1,0:T(2,128)(2,1)} %reshape.238), calls=%async_computation | async-start | bytes 655360 | tf_op jit(solution)/shard_map/all_to_all | solution.py:118
  401.1 89.7 %copy-start.1 = (f32[1280]{0:T(1024)S(1)}, f32[1280]{0:T(1024)}, u32[]{:S(2)}) copy-start(f32[1280]{0:T(1024)} %param.17) | copy-start | bytes 15364
Sparse Core Ops, SparseCore 0:
  11.0 116.3 all-gather.11
  130.8 116.2 all-gather.9
  250.7 111.6 all-gather.15
  365.7 116.7 all-gather.13
where the time goes:
time: 532 us; the launch traced here: 531 us
  blocking collectives  364 us (68%)
  waiting for transfers between devices  84.1 us (16%)
  local copies, waits for them, and re-layouts  24.9 us (5%)
  matrix products  18.4 us (3%)
  starting transfers between devices  16.2 us (3%)
  between operations  13.4 us (3%)
  other arithmetic  9.45 us (2%)
    all_gather x1, blocking collectives, body(): ref_full = lax.all_gather(ref_hidden, 'seq', axis=0, tiled=True)  342 us
    all_gather x1, waiting for transfers between devices, temporal_project(): lax.all_gather(w_qkv_temporal, 'seq', axis=1, tiled=True)  81.4 us
    unnamed x15, local copies, waits for them, and re-layouts  23.5 us
    all_to_all x1, blocking collectives, body(): lax.all_to_all(updated, 'seq', split_axis=0, concat_axis=1, tiled=True)  22.3 us
    all_to_all x1, starting transfers between devices, body(): lax.all_to_all(hidden, 'seq', split_axis=1, concat_axis=0, tiled=True)  16.1 us
  transfers between devices with their start and end apart: 5, of which 1 were waited for; matrix products, arithmetic and copies ran while one was open for 8% of the time, Pallas kernels for 0%

commit v1 on v0

v1 whole, which is shorter than its diff:
```python
import functools
import itertools

import jax
import jax.numpy as jnp
from jax import lax
from jax.experimental import pallas as pl
from jax.experimental.pallas import tpu as pltpu
from jax.sharding import PartitionSpec as P

D = 1280
HEADS = 10
HEAD = 64
INNER = 640
PIX = 128
NX, NZ, NY = 4, 8, 4
SEQ = NX * NZ * NY
EPS = 1e-05
BF = jnp.bfloat16
F32 = jnp.float32
SHIFTS = (0, 1, 3, 2)
T_S, T_O, T_T, T_U = 6, 3, 5, 3
TILES = T_S + T_O + T_T + T_U


def seq_of(x, z, y):
    return (x * NZ + z) * NY + y


Z_GROUPS = [[seq_of(x, z, y) for z in range(NZ)] for x in range(NX) for y in range(NY)]
SWAP = [(i, (i + SEQ) % (2 * SEQ)) for i in range(2 * SEQ)]


def ring_perm(k, stage):
    pairs = []
    for c, x, z, y in itertools.product(range(2), range(NX), range(NZ), range(NY)):
        if (c + stage) % 2 == 0:
            to = ((x + k) % NX, z, y)
        else:
            to = (x, z, (y + k) % NY)
        pairs.append((c * SEQ + seq_of(x, z, y), c * SEQ + seq_of(*to)))
    return pairs


def ring(block, stage):
    return [block] + [
        lax.ppermute(block, ("clip", "seq"), ring_perm(k, stage)) for k in SHIFTS[1:]
    ]


def swap(block):
    return lax.ppermute(block, ("clip", "seq"), SWAP)


def vmem(n):
    return [pl.BlockSpec(memory_space=pltpu.VMEM)] * n


PARAMS = pltpu.CompilerParams(vmem_limit_bytes=48 * 1024 * 1024)


def layer_norm(x, gain):
    mean = jnp.mean(x, axis=-1, keepdims=True)
    d = x - mean
    var = jnp.mean(d * d, axis=-1, keepdims=True)
    return (d * lax.rsqrt(var + EPS) * gain).astype(BF)


def pack_kernel(ws, ref, wo, wt, wu, out):
    c = lax.axis_index("clip")

    def tile(*rows):
        n = sum(r.shape[0] for r in rows)
        parts = [r.astype(F32) for r in rows]
        if n < 16:
            parts.append(jnp.zeros((16 - n, 128), F32))
        return jnp.concatenate(parts, axis=0).astype(BF)

    def fill(half):
        at = 0
        for t in range(5):
            out[at] = tile(ws[:, 640 * half + 128 * t : 640 * half + 128 * (t + 1)])
            at += 1
        out[at] = tile(*[ref[:, 128 * u : 128 * (u + 1)] for u in range(10)])
        at += 1
        for t in range(3):
            out[at] = tile(wo[:, 256 * half + 128 * t : 256 * half + 128 * (t + 1)])
            at += 1
        for t in range(5):
            out[at] = tile(wt[:, 640 * half + 128 * t : 640 * half + 128 * (t + 1)])
            at += 1
        for t in range(3):
            out[at] = tile(wu[:, 256 * half + 128 * t : 256 * half + 128 * (t + 1)])
            at += 1

    for half in range(2):
        pl.when(c == half)(functools.partial(fill, half))


def place():
    s = lax.axis_index("seq")
    return lax.axis_index("clip"), s // (NZ * NY), lax.rem(s, NY)


def lanes(ref, start, tiles, first):
    parts = [ref[start : start + 8, first + t].reshape(128, 128) for t in range(tiles)]
    return jnp.concatenate(parts, axis=1)


def project(own, oth, acc, xa, xb, tiles_a, tiles_b, first_b):
    c, x, y = place()
    for j in range(4):
        wa = jnp.concatenate([lanes(own[j], 8 * i, tiles_a, 0) for i in range(4)], axis=0)
        wb = jnp.concatenate([lanes(oth[i], 8 * j, tiles_b, first_b) for i in range(4)], axis=0)
        dims = (((1,), (1,)), ((), ()))
        r = lax.dot_general(wa, xa, dims, preferred_element_type=F32)
        r = r + lax.dot_general(wb, xb, dims, preferred_element_type=F32)
        for i in range(4):
            first, second = SHIFTS[i], SHIFTS[j]
            dx = jnp.where(c == 0, first, second)
            dy = jnp.where(c == 0, second, first)
            xs = lax.rem(x - dx + NX, NX)
            ys = lax.rem(y - dy + NY, NY)
            for z in range(NZ):
                at = (i * 8 + z) * 16
                acc[xs, z, ys] = r[at : at + 16]


def compact(acc, rows, count):
    for s in range(SEQ):
        x, z, y = s // 32, (s // 4) % 8, s % 4
        rows[count * s : count * (s + 1), :] = acc[x, z, y, 0:count, :]


def halves(xv, c):
    lo, hi = xv[:, :640], xv[:, 640:]
    first = c == 0
    return jnp.where(first, lo, hi), jnp.where(first, hi, lo)


def heads(rows, keys, attn):
    for h in range(HEADS):
        q = rows[64 * h : 64 * (h + 1), 0:128].astype(BF)
        k = rows[640 + 64 * h : 640 + 64 * (h + 1), 0:keys].astype(BF)
        v = rows[1280 + 64 * h : 1280 + 64 * (h + 1), 0:keys].astype(BF)
        st = lax.dot_general(k, q, (((0,), (0,)), ((), ())), preferred_element_type=F32)
        st = st * (HEAD**-0.5)
        e = jnp.exp(st - jnp.max(st, axis=0, keepdims=True))
        p = (e * (1.0 / jnp.sum(e, axis=0, keepdims=True))).astype(BF)
        attn[64 * h : 64 * (h + 1), :] = jnp.dot(v, p, preferred_element_type=F32)


def spatial_kernel(*refs):
    own, oth = refs[0:4], refs[4:8]
    latents, gain, out, acc, rows, wide, attn = refs[8:]
    c, _, _ = place()
    normed = layer_norm(latents[...].astype(F32), gain[...])
    for j in range(4):
        for i in range(4):
            wide[j * 512 + i * 128 : j * 512 + (i + 1) * 128, :] = (
                own[j][8 * i : 8 * i + 8, 5].reshape(128, 128).astype(F32)
            )
    ref_hidden = jnp.concatenate(
        [wide[pl.ds(u, 128, stride=16), :] for u in range(10)], axis=1
    ).astype(BF)
    xa, xb = halves(jnp.concatenate([normed, ref_hidden], axis=0), c)
    project(own, oth, acc, xa, xb, 5, 5, 0)
    compact(acc, rows, 15)
    heads(rows, 256, attn)
    out[...] = attn[...].T.astype(BF)


def temporal_kernel(*refs):
    own, oth = refs[0:4], refs[4:8]
    tokens, out, acc, rows, attn = refs[8:]
    c, _, _ = place()
    xa, xb = halves(tokens[...], c)
    project(own, oth, acc, xa, xb, 5, 5, 0)
    compact(acc, rows, 15)
    heads(rows, 128, attn)
    out[...] = attn[...].T.astype(BF)


def out_project(own, oth, attn, acc, rows, first):
    c, _, _ = place()
    a = attn[...]
    xa = jnp.where(c == 0, a[:, 0:384], a[:, 256:640])
    xb = jnp.where(c == 0, a[:, 384:640], a[:, 0:256])
    project(own, oth, acc, xa, xb, 3, 2, first + (1 - c))
    compact(acc, rows, 10)
    return rows[...].T


def hidden_kernel(*refs):
    own, oth = refs[0:4], refs[4:8]
    attn, latents, gain, hidden, tnormed, acc, rows = refs[8:]
    total = latents[...].astype(F32) + out_project(own, oth, attn, acc, rows, 0)
    h = total.astype(BF)
    hidden[...] = h
    tnormed[...] = layer_norm(h.astype(F32), gain[...])


def mixed_kernel(*refs):
    own, oth = refs[0:4], refs[4:8]
    attn, hidden, mixed, acc, rows = refs[8:]
    total = hidden[...].astype(F32) + out_project(own, oth, attn, acc, rows, 0)
    mixed[...] = total.astype(BF)


def call(kernel, args, outs, scratch, name, flops=0):
    shapes = [jax.ShapeDtypeStruct(s, BF) for s in outs]
    single = len(shapes) == 1
    size = sum(a.size * a.dtype.itemsize for a in args) + sum(2 * s.size for s in shapes)
    return pl.pallas_call(
        kernel,
        out_shape=shapes[0] if single else shapes,
        in_specs=vmem(len(args)),
        out_specs=vmem(1)[0] if single else vmem(len(shapes)),
        scratch_shapes=[pltpu.VMEM(s, F32) for s in scratch],
        compiler_params=PARAMS,
        cost_estimate=pl.CostEstimate(flops=flops, bytes_accessed=size, transcendentals=0),
        name=name,
    )(*args)


def body(latents, ref_hidden, gain_s, w_s, w_o, gain_t, w_t, w_u):
    latents = latents.reshape(PIX, D)
    gain_s = gain_s.reshape(1, D)
    gain_t = gain_t.reshape(1, D)
    packed = call(
        pack_kernel, [w_s.T, ref_hidden, w_o.T, w_t.T, w_u.T], [(TILES, 16, 128)], [], "pack"
    )
    along_z = lax.all_to_all(
        jnp.broadcast_to(packed[None], (NZ, TILES, 16, 128)),
        "seq",
        0,
        0,
        axis_index_groups=Z_GROUPS,
        tiled=True,
    )
    n_spatial = T_S + T_O
    first = ring(along_z[:, :n_spatial], 0)
    part_s = jnp.concatenate([b[:, :T_S] for b in first], axis=0)
    part_o = jnp.concatenate([b[:, T_S:] for b in first], axis=0)
    own_s = ring(part_s, 1)
    oth_s = [swap(b) for b in own_s]
    own_o = ring(part_o, 1)
    oth_o = [swap(b) for b in own_o]
    part_t = jnp.concatenate(ring(along_z[:, n_spatial:], 0), axis=0)
    own_t = ring(part_t, 1)
    oth_t = [swap(b) for b in own_t]

    attn = call(
        spatial_kernel,
        own_s + oth_s + [latents, gain_s],
        [(PIX, INNER)],
        [(NX, NZ, NY, 16, 256), (1920, 256), (2048, 128), (INNER, 128)],
        "spatial",
        2 * 2048 * 256 * D,
    )
    hidden, tnormed = call(
        hidden_kernel,
        own_o + oth_o + [attn, latents, gain_t],
        [(PIX, D), (PIX, D)],
        [(NX, NZ, NY, 16, 128), (D, 128)],
        "hidden",
        2 * 2048 * 128 * INNER,
    )
    tokens = lax.all_to_all(tnormed, "seq", 0, 0, tiled=True)
    tattn = call(
        temporal_kernel,
        [b[:, :T_T] for b in own_t] + [b[:, :T_T] for b in oth_t] + [tokens],
        [(PIX, INNER)],
        [(NX, NZ, NY, 16, 128), (1920, 128), (INNER, 128)],
        "temporal",
        2 * 2048 * 128 * D,
    )
    back = lax.all_to_all(tattn, "seq", 0, 0, tiled=True)
    mixed = call(
        mixed_kernel,
        [b[:, T_T:] for b in own_t] + [b[:, T_T:] for b in oth_t] + [back, hidden],
        [(PIX, D)],
        [(NX, NZ, NY, 16, 128), (D, 128)],
        "mixed",
        2 * 2048 * 128 * INNER,
    )
    return mixed.reshape(1, PIX, D)


def solution(mesh):
    in_specs = (
        P(("clip", "seq"), None, None),
        P(("clip", "seq"), None),
        P(),
        P(None, "seq"),
        P(None, "seq"),
        P(),
        P(None, "seq"),
        P(None, "seq"),
    )
    out_specs = P(("clip", "seq"), None, None)
    return jax.shard_map(body, mesh=mesh, in_specs=in_specs, out_specs=out_specs, check_vma=False)
```

time: 532 us -> 180 us (0.34)
  blocking collectives: 364 us -> 25.1 us
  waiting for transfers between devices: 84.1 us -> 54.8 us
  starting transfers between devices: 16.2 us -> 45.4 us
  matrix products: 18.4 us -> 0 us
  Pallas kernels: 0 us -> 13.1 us
  between operations: 13.4 us -> 0.32 us
  local copies, waits for them, and re-layouts: 24.9 us -> 37.3 us
  other arithmetic: 9.45 us -> 2.6 us
    all_gather x1 -> x0, blocking collectives: 342 us -> none  [body(): ref_full = lax.all_gather(ref_hidden, 'seq', axis=0, tiled=True)]
    all_gather x4 -> x0, waiting for transfers between devices: 81.5 us -> none  [the longest x1 81.4 us: temporal_project(): lax.all_gather(w_qkv_temporal, 'seq', axis=1, tiled=True)]
    ppermute x0 -> x27, waiting for transfers between devices: none -> 46.5 us  [the longest x15 46.4 us: ring(): lax.ppermute(block, ('clip', 'seq'), ring_perm(k, stage))]
    ppermute x0 -> x27, starting transfers between devices: none -> 27.3 us  [the longest x15 24.9 us: ring(): lax.ppermute(block, ('clip', 'seq'), ring_perm(k, stage))]
    slice x4 -> x29, local copies, waits for them, and re-layouts: 0.54 us -> 21.1 us  [the longest x8 11.8 us: body(): b[:, :T_T]]
    dot_general x44 -> x0, matrix products: 18.4 us -> none  [the longest x20 5.24 us: one_head(): jnp.einsum('haf,hgf->hag', per_head_queries, per_head_keys, preferred_ele...]
    pallas_call x0 -> x5, Pallas kernels: none -> 13.1 us  [call(): pl.pallas_call(kernel, out_shape=shapes[0] if single else shapes, in_spec...]
    all_to_all x1 -> x2, waiting for transfers between devices: 0.01 us -> 8.31 us  [the longest x1 4.47 us: body(): back = lax.all_to_all(tattn, 'seq', 0, 0, tiled=True)]
  transfers between devices with their start and end apart: 5 -> 29, of which waited for: 1 -> 8; matrix products, arithmetic and copies ran while one was open for 8% -> 13% of each run, Pallas kernels for 0% -> 4%
where the time goes in v1:
time: 180 us; the launch traced here: 179 us
  waiting for transfers between devices  54.8 us (30%)
  starting transfers between devices  45.4 us (25%)
  local copies, waits for them, and re-layouts  37.3 us (21%)
  blocking collectives  25.1 us (14%)
  Pallas kernels  13.1 us (7%)
  other arithmetic  2.6 us (1%)
    ppermute x15, waiting for transfers between devices, ring(): lax.ppermute(block, ('clip', 'seq'), ring_perm(k, stage))  46.4 us
    all_to_all x1, blocking collectives, body(): lax.all_to_all(jnp.broadcast_to(packed[None], (NZ, TILES, 16, 128)), 'seq...  25.1 us
    ppermute x15, starting transfers between devices, ring(): lax.ppermute(block, ('clip', 'seq'), ring_perm(k, stage))  24.9 us
    unnamed x38, local copies, waits for them, and re-layouts  15.6 us
    pallas_call x5, Pallas kernels, call(): pl.pallas_call(kernel, out_shape=shapes[0] if single else shapes, in_spec...  13.1 us
    slice x8, local copies, waits for them, and re-layouts, body(): b[:, :T_T]  11.8 us
    all_to_all x1, starting transfers between devices, body(): back = lax.all_to_all(tattn, 'seq', 0, 0, tiled=True)  10.4 us
    slice x8, local copies, waits for them, and re-layouts, body(): b[:, T_T:]  8.25 us
  transfers between devices with their start and end apart: 29, of which 8 were waited for; matrix products, arithmetic and copies ran while one was open for 13% of the time, Pallas kernels for 4%

profile of v1, /device:TPU:32, one launch (start us, length us, event | category | flops | bytes accessed | tf_op | source)
XLA Modules:
  0.0 178.6 jit_solution(8221492581351463989)
XLA Ops:
  0.0 0.7 copy-done.10
  0.7 0.8 copy-done.6
  1.5 0.8 copy-done.7
  2.3 0.7 copy-done.8
  3.0 0.7 copy-done.9
  3.8 25.1 %all_to_all.27 = bf16[8,17,16,128]{3,2,1,0:T(8,128)(2,1)S(1)} all-to-all(bf16[8,17,16,128]{3,2,1,0:T(8,128)(2,1)S(1)} %broadcast_in_dim.2), channel_id=1, replica_groups={{0,4,8,12,16,20,24,28},{1,5,9,13,17,21,25,29},{2,6,10,14,18,22,26,30},{..., dimensions={0} | all-to-all | bytes 1114112 | tf_op jit(solution)/shard_map/all_to_all | solution.py:233
  28.9 3.1 %collective-permute-start.12 = (bf16[8,9,16,128]{3,2,1,0:T(8,128)(2,1)S(1)}, bf16[8,9,16,128]{3,2,1,0:T(8,128)(2,1)S(1)}, u32[]{:S(2)}, u32[]{:S(2)}) collective-permute-start(bf16[8,9,16,128]{3,2,1,0:T(8,128)(2,1)S(1)} %slice.124), channel_id=1, source_target_pairs={{0,64},{1,65},{2,66},{3,67},{4,68},{5,69},{6,70},{7,71},{8,72},{9,... | collective-permute-start | bytes 884744 | tf_op jit(solution)/shard_map/ppermute | solution.py:47
  32.0 1.1 collective-permute-start.11
  33.2 0.9 collective-permute-start.10
  34.1 0.7 collective-permute-start.2
  34.8 2.6 %collective-permute-start.1 = (bf16[8,8,16,128]{3,2,1,0:T(8,128)(2,1)S(1)}, bf16[8,8,16,128]{3,2,1,0:T(8,128)(2,1)S(1)}, u32[]{:S(2)}, u32[]{:S(2)}) collective-permute-start(bf16[8,8,16,128]{3,2,1,0:T(8,128)(2,1)S(1)} %slice.106), channel_id=1, source_target_pairs={{0,96},{1,97},{2,98},{3,99},{4,100},{5,101},{6,102},{7,103},{8,104... | collective-permute-start | bytes 786440 | tf_op jit(solution)/shard_map/ppermute | solution.py:47
  37.5 3.1 %collective-permute-done.11 = bf16[8,9,16,128]{3,2,1,0:T(8,128)(2,1)S(1)} collective-permute-done((bf16[8,9,16,128]{3,2,1,0:T(8,128)(2,1)S(1)}, bf16[8,9,16,128]{3,2,1,0:T(8,128)(2,1)S(1)}, u32[]{:S(2)}, u32[]{:S(2)}) %collective-permute-start.11) | collective-permute-done | bytes 294944 | tf_op jit(solution)/shard_map/ppermute | solution.py:47
  40.6 3.4 %collective-permute-done.10 = bf16[8,9,16,128]{3,2,1,0:T(8,128)(2,1)S(1)} collective-permute-done((bf16[8,9,16,128]{3,2,1,0:T(8,128)(2,1)S(1)}, bf16[8,9,16,128]{3,2,1,0:T(8,128)(2,1)S(1)}, u32[]{:S(2)}, u32[]{:S(2)}) %collective-permute-start.10) | collective-permute-done | bytes 294944 | tf_op jit(solution)/shard_map/ppermute | solution.py:47
  44.1 3.3 %collective-permute-start.15 = (bf16[32,3,16,128]{3,2,1,0:T(8,128)(2,1)S(1)}, bf16[32,3,16,128]{3,2,1,0:T(8,128)(2,1)S(1)}, u32[]{:S(2)}, u32[]{:S(2)}) collective-permute-start(bf16[32,3,16,128]{3,2,1,0:T(8,128)(2,1)S(1)} %pad_maximum_fusion.2.refs_0_), channel_id=1, source_target_pairs={{0,2},{1,3},{2,0},{3,1},{4,6},{5,7},{6,4},{7,5},{8,10},{9,11},{10,... | collective-permute-start | bytes 1179656 | tf_op jit(solution)/shard_map/ppermute | solution.py:47
  47.4 1.1 collective-permute-start.14
  48.5 1.0 collective-permute-start.13
  49.6 0.9 slice-done.1
  50.7 8.7 %collective-permute-done = bf16[8,8,16,128]{3,2,1,0:T(8,128)(2,1)S(1)} collective-permute-done((bf16[8,8,16,128]{3,2,1,0:T(8,128)(2,1)S(1)}, bf16[8,8,16,128]{3,2,1,0:T(8,128)(2,1)S(1)}, u32[]{:S(2)}, u32[]{:S(2)}) %collective-permute-start) | collective-permute-done | bytes 262176 | tf_op jit(solution)/shard_map/ppermute | solution.py:47
  59.4 3.2 %collective-permute-start.22 = (bf16[32,6,16,128]{3,2,1,0:T(8,128)(2,1)S(1)}, bf16[32,6,16,128]{3,2,1,0:T(8,128)(2,1)S(1)}, u32[]{:S(2)}, u32[]{:S(2)}) collective-permute-start(bf16[32,6,16,128]{3,2,1,0:T(8,128)(2,1)S(1)} %pad_maximum_fusion.1.refs_0_), channel_id=1, source_target_pairs={{0,2},{1,3},{2,0},{3,1},{4,6},{5,7},{6,4},{7,5},{8,10},{9,11},{10,... | collective-permute-start | bytes 2359304 | tf_op jit(solution)/shard_map/ppermute | solution.py:47
  62.6 0.5 collective-permute-start.18
  63.1 1.1 pad_maximum_fusion
  64.6 2.7 %collective-permute-start.21 = (bf16[32,6,16,128]{3,2,1,0:T(8,128)(2,1)S(1)}, bf16[32,6,16,128]{3,2,1,0:T(8,128)(2,1)S(1)}, u32[]{:S(2)}, u32[]{:S(2)}) collective-permute-start(bf16[32,6,16,128]{3,2,1,0:T(8,128)(2,1)S(1)} %pad_maximum_fusion.1.refs_0_), channel_id=1, source_target_pairs={{0,3},{1,0},{2,1},{3,2},{4,7},{5,4},{6,5},{7,6},{8,11},{9,8},{10,9... | collective-permute-start | bytes 2359304 | tf_op jit(solution)/shard_map/ppermute | solution.py:47
  67.3 3.2 %collective-permute-start.4 = (bf16[32,8,16,128]{3,2,1,0:T(8,128)(2,1)}, bf16[32,8,16,128]{3,2,1,0:T(8,128)(2,1)}, u32[]{:S(2)}, u32[]{:S(2)}) collective-permute-start(bf16[32,8,16,128]{3,2,1,0:T(8,128)(2,1)} %pad_maximum_fusion), channel_id=1, source_target_pairs={{0,3},{1,0},{2,1},{3,2},{4,7},{5,4},{6,5},{7,6},{8,11},{9,8},{10,9... | collective-permute-start | bytes 3145736 | tf_op jit(solution)/shard_map/ppermute | solution.py:47
  70.5 2.5 %collective-permute-done.22.refs_3_ = bf16[32,6,16,128]{3,2,1,0:T(8,128)(2,1)S(1)} collective-permute-done((bf16[32,6,16,128]{3,2,1,0:T(8,128)(2,1)S(1)}, bf16[32,6,16,128]{3,2,1,0:T(8,128)(2,1)S(1)}, u32[]{:S(2)}, u32[]{:S(2)}) %collective-permute-start.22) | collective-permute-done | bytes 786464 | tf_op jit(solution)/shard_map/ppermute | solution.py:47
  73.0 1.6 collective-permute-start.3
  74.6 18.1 %collective-permute-done.21.refs_2_ = bf16[32,6,16,128]{3,2,1,0:T(8,128)(2,1)S(1)} collective-permute-done((bf16[32,6,16,128]{3,2,1,0:T(8,128)(2,1)S(1)}, bf16[32,6,16,128]{3,2,1,0:T(8,128)(2,1)S(1)}, u32[]{:S(2)}, u32[]{:S(2)}) %collective-permute-start.21) | collective-permute-done | bytes 786464 | tf_op jit(solution)/shard_map/ppermute | solution.py:47
  92.6 0.5 collective-permute-start.25
  93.2 10.7 %collective-permute-done.4 = bf16[32,8,16,128]{3,2,1,0:T(8,128)(2,1)} collective-permute-done((bf16[32,8,16,128]{3,2,1,0:T(8,128)(2,1)}, bf16[32,8,16,128]{3,2,1,0:T(8,128)(2,1)}, u32[]{:S(2)}, u32[]{:S(2)}) %collective-permute-start.4) | collective-permute-done | bytes 1048608 | tf_op jit(solution)/shard_map/ppermute | solution.py:47
  104.0 0.5 collective-permute-start.6
  105.4 6.1 %spatial.1.refs_8_ = bf16[128,640]{1,0:T(8,128)(2,1)S(1)} custom-call(bf16[32,6,16,128]{3,2,1,0:T(8,128)(2,1)S(1)} %pad_maximum_fusion.1.refs_0_, bf16[32,6,16,128]{3,2,1,0:T(8,128)(2,1)S(1)} %collective-permute-done.20.refs_1_, bf16[32,6,16,128]{3,2,1,0:T(8,128)(2,1)S(1)} %collective-permute-done.21.refs_2_, ...), custom_call_target="tpu_custom_call" | custom-call | flops 1342177280 | bytes 6788096 | tf_op jit(solution)/shard_map/spatial/pallas_call | solution.py:214
  111.5 1.4 hidden.1
  112.9 0.7 copy-done.4
  114.1 0.7 reduce
  114.8 0.8 reshape.21
  115.6 7.7 %all-to-all-start.1 = ((bf16[128,2,640]{2,1,0:T(2,128)(2,1)}), bf16[128,2,640]{2,1,0:T(2,128)(2,1)}, u32[]{:S(2)}, u32[]{:S(2)}) async-start(bf16[128,2,640]{2,1,0:T(2,128)(2,1)} %reshape.21), calls=%async_computation.1 | async-start | bytes 655360 | tf_op jit(solution)/shard_map/all_to_all | solution.py:269
  123.3 1.2 slice.115.refs_0_
  124.4 1.2 slice.118.refs_3_
  125.6 1.2 slice.117.refs_2_
  126.7 1.2 slice.116.refs_1_
  127.9 1.2 slice.119.refs_4_
  129.1 2.0 %slice.122.refs_7_ = bf16[32,5,16,128]{3,2,1,0:T(8,128)(2,1)} slice(bf16[32,8,16,128]{3,2,1,0:T(8,128)(2,1)} %collective-permute-done.9), slice={[0:32], [0:5], [0:16], [0:128]} | slice | bytes 1310720 | tf_op jit(solution)/shard_map/slice | solution.py:272
  131.1 2.0 %slice.121.refs_6_ = bf16[32,5,16,128]{3,2,1,0:T(8,128)(2,1)} slice(bf16[32,8,16,128]{3,2,1,0:T(8,128)(2,1)} %collective-permute-done.8), slice={[0:32], [0:5], [0:16], [0:128]} | slice | bytes 1310720 | tf_op jit(solution)/shard_map/slice | solution.py:272
  133.1 2.0 %slice.120.refs_5_ = bf16[32,5,16,128]{3,2,1,0:T(8,128)(2,1)} slice(bf16[32,8,16,128]{3,2,1,0:T(8,128)(2,1)} %collective-permute-done.7), slice={[0:32], [0:5], [0:16], [0:128]} | slice | bytes 1310720 | tf_op jit(solution)/shard_map/slice | solution.py:272
  135.1 3.8 %all-to-all-done.1 = bf16[128,2,640]{2,1,0:T(2,128)(2,1)} async-done(((bf16[128,2,640]{2,1,0:T(2,128)(2,1)}), bf16[128,2,640]{2,1,0:T(2,128)(2,1)}, u32[]{:S(2)}, u32[]{:S(2)}) %all-to-all-start.1) | async-done | bytes 327712 | tf_op jit(solution)/shard_map/all_to_all | solution.py:269
  138.9 3.2 %reshape.22 = bf16[128,1,1280]{2,1,0:T(2,128)(2,1)} reshape(bf16[128,2,640]{2,1,0:T(2,128)(2,1)} %all-to-all-done.1) | data formatting | bytes 655360
  142.1 1.2 copy.17
  143.4 1.1 copy-done.1
  144.5 1.1 copy-done.2
  145.6 3.8 %temporal.1 = bf16[128,640]{1,0:T(8,128)(2,1)S(1)} custom-call(bf16[32,5,16,128]{3,2,1,0:T(8,128)(2,1)S(1)} %slice.115.refs_0_, bf16[32,5,16,128]{3,2,1,0:T(8,128)(2,1)S(1)} %slice.116.refs_1_, bf16[32,5,16,128]{3,2,1,0:T(8,128)(2,1)S(1)} %slice.117.refs_2_, bf16[32,5,16,128]{3,2,1,0:T(8,128)(2,1)S(1)} %slice.118.refs_3_, ...), custom_call_target="tpu_custom_call" | custom-call | flops 671088640 | bytes 5734400 | tf_op jit(solution)/shard_map/temporal/pallas_call | solution.py:214
  149.5 0.6 reduce.1
  150.0 0.9 reshape.23
  150.9 10.4 %all-to-all-start.2 = ((bf16[128,2,320]{2,1,0:T(2,128)(2,1)}), bf16[128,2,320]{2,1,0:T(2,128)(2,1)}, u32[]{:S(2)}, u32[]{:S(2)}) async-start(bf16[128,2,320]{2,1,0:T(2,128)(2,1)} %reshape.23), calls=%async_computation.2 | async-start | bytes 393216 | tf_op jit(solution)/shard_map/all_to_all | solution.py:278
  161.4 1.0 slice.107.refs_0_
  162.4 1.0 slice.111.refs_4_
  163.4 1.0 slice.110.refs_3_
  164.5 1.0 slice.109.refs_2_
  165.5 1.0 slice.108.refs_1_
  166.5 1.0 slice.114.refs_7_
  167.6 1.0 slice.113.refs_6_
  168.6 1.0 slice.112.refs_5_
  169.6 4.5 %all-to-all-done.2 = bf16[128,2,320]{2,1,0:T(2,128)(2,1)} async-done(((bf16[128,2,320]{2,1,0:T(2,128)(2,1)}), bf16[128,2,320]{2,1,0:T(2,128)(2,1)}, u32[]{:S(2)}, u32[]{:S(2)}) %all-to-all-start.2) | async-done | bytes 163872 | tf_op jit(solution)/shard_map/all_to_all | solution.py:278
  174.1 1.6 reshape.24
  175.8 0.9 copy-done.5
  176.7 1.8 %mixed.1 = bf16[128,1280]{1,0:T(8,128)(2,1)} custom-call(bf16[32,3,16,128]{3,2,1,0:T(8,128)(2,1)S(1)} %slice.107.refs_0_, bf16[32,3,16,128]{3,2,1,0:T(8,128)(2,1)S(1)} %slice.108.refs_1_, bf16[32,3,16,128]{3,2,1,0:T(8,128)(2,1)S(1)} %slice.109.refs_2_, bf16[32,3,16,128]{3,2,1,0:T(8,128)(2,1)S(1)} %slice.110.refs_3_, ...), custom_call_target="tpu_custom_call" | custom-call | flops 335544320 | bytes 3964928 | tf_op jit(solution)/shard_map/mixed/pallas_call | solution.py:214
  (76 shorter events, 2.6 us)
Async XLA Ops:
  0.0 0.7 copy-start.10
  0.7 0.8 copy-start.6
  1.5 0.8 copy-start.7
  2.2 0.7 copy-start.8
  3.0 0.7 copy-start.9
  28.9 8.5 %copy-start.11 = (bf16[8,17,16,128]{3,2,1,0:T(8,128)(2,1)}, bf16[8,17,16,128]{3,2,1,0:T(8,128)(2,1)S(1)}, u32[]{:S(2)}) copy-start(bf16[8,17,16,128]{3,2,1,0:T(8,128)(2,1)S(1)} %all_to_all.27) | copy-start | bytes 1671172
  28.9 8.5 %collective-permute-start.12 = (bf16[8,9,16,128]{3,2,1,0:T(8,128)(2,1)S(1)}, bf16[8,9,16,128]{3,2,1,0:T(8,128)(2,1)S(1)}, u32[]{:S(2)}, u32[]{:S(2)}) collective-permute-start(bf16[8,9,16,128]{3,2,1,0:T(8,128)(2,1)S(1)} %slice.124), channel_id=1, source_target_pairs={{0,64},{1,65},{2,66},{3,67},{4,68},{5,69},{6,70},{7,71},{8,72},{9,... | collective-permute-start | bytes 884744 | tf_op jit(solution)/shard_map/ppermute | solution.py:47
  32.0 8.5 %collective-permute-start.11 = (bf16[8,9,16,128]{3,2,1,0:T(8,128)(2,1)S(1)}, bf16[8,9,16,128]{3,2,1,0:T(8,128)(2,1)S(1)}, u32[]{:S(2)}, u32[]{:S(2)}) collective-permute-start(bf16[8,9,16,128]{3,2,1,0:T(8,128)(2,1)S(1)} %slice.124), channel_id=1, source_target_pairs={{0,96},{1,97},{2,98},{3,99},{4,100},{5,101},{6,102},{7,103},{8,104... | collective-permute-start | bytes 884744 | tf_op jit(solution)/shard_map/ppermute | solution.py:47
  33.2 10.7 %collective-permute-start.10 = (bf16[8,9,16,128]{3,2,1,0:T(8,128)(2,1)S(1)}, bf16[8,9,16,128]{3,2,1,0:T(8,128)(2,1)S(1)}, u32[]{:S(2)}, u32[]{:S(2)}) collective-permute-start(bf16[8,9,16,128]{3,2,1,0:T(8,128)(2,1)S(1)} %slice.124), channel_id=1, source_target_pairs={{0,32},{1,33},{2,34},{3,35},{4,36},{5,37},{6,38},{7,39},{8,40},{9,... | collective-permute-start | bytes 884744 | tf_op jit(solution)/shard_map/ppermute | solution.py:47
  34.1 14.4 %collective-permute-start.2 = (bf16[8,8,16,128]{3,2,1,0:T(8,128)(2,1)S(1)}, bf16[8,8,16,128]{3,2,1,0:T(8,128)(2,1)S(1)}, u32[]{:S(2)}, u32[]{:S(2)}) collective-permute-start(bf16[8,8,16,128]{3,2,1,0:T(8,128)(2,1)S(1)} %slice.106), channel_id=1, source_target_pairs={{0,64},{1,65},{2,66},{3,67},{4,68},{5,69},{6,70},{7,71},{8,72},{9,... | collective-permute-start | bytes 786440 | tf_op jit(solution)/shard_map/ppermute | solution.py:47
  34.8 13.6 %collective-permute-start.1 = (bf16[8,8,16,128]{3,2,1,0:T(8,128)(2,1)S(1)}, bf16[8,8,16,128]{3,2,1,0:T(8,128)(2,1)S(1)}, u32[]{:S(2)}, u32[]{:S(2)}) collective-permute-start(bf16[8,8,16,128]{3,2,1,0:T(8,128)(2,1)S(1)} %slice.106), channel_id=1, source_target_pairs={{0,96},{1,97},{2,98},{3,99},{4,100},{5,101},{6,102},{7,103},{8,104... | collective-permute-start | bytes 786440 | tf_op jit(solution)/shard_map/ppermute | solution.py:47
  37.5 12.1 %copy-start.13 = (bf16[8,9,16,128]{3,2,1,0:T(8,128)(2,1)}, bf16[8,9,16,128]{3,2,1,0:T(8,128)(2,1)S(1)}, u32[]{:S(2)}) copy-start(bf16[8,9,16,128]{3,2,1,0:T(8,128)(2,1)S(1)} %collective-permute-done.12) | copy-start | bytes 884740
  40.6 3.4 %slice-start = ((bf16[8,17,16,128]{3,2,1,0:T(8,128)(2,1)}), bf16[8,3,16,128]{3,2,1,0:T(8,128)(2,1)S(1)}, s32[]{:S(2)}) async-start(bf16[8,17,16,128]{3,2,1,0:T(8,128)(2,1)} %copy-done.11), calls=%async_computation.3 | async-start | bytes 196608 | tf_op jit(solution)/shard_map/slice | solution.py:244
  44.0 15.4 %collective-permute-start.16 = (bf16[32,3,16,128]{3,2,1,0:T(8,128)(2,1)S(1)}, bf16[32,3,16,128]{3,2,1,0:T(8,128)(2,1)S(1)}, u32[]{:S(2)}, u32[]{:S(2)}) collective-permute-start(bf16[32,3,16,128]{3,2,1,0:T(8,128)(2,1)S(1)} %pad_maximum_fusion.2.refs_0_), channel_id=1, source_target_pairs={{0,128},{1,129},{2,130},{3,131},{4,132},{5,133},{6,134},{7,135},{8... | collective-permute-start | bytes 1179656 | tf_op jit(solution)/shard_map/ppermute | solution.py:52
  44.1 18.5 %collective-permute-start.15 = (bf16[32,3,16,128]{3,2,1,0:T(8,128)(2,1)S(1)}, bf16[32,3,16,128]{3,2,1,0:T(8,128)(2,1)S(1)}, u32[]{:S(2)}, u32[]{:S(2)}) collective-permute-start(bf16[32,3,16,128]{3,2,1,0:T(8,128)(2,1)S(1)} %pad_maximum_fusion.2.refs_0_), channel_id=1, source_target_pairs={{0,2},{1,3},{2,0},{3,1},{4,6},{5,7},{6,4},{7,5},{8,10},{9,11},{10,... | collective-permute-start | bytes 1179656 | tf_op jit(solution)/shard_map/ppermute | solution.py:47
  47.4 15.2 %collective-permute-start.14 = (bf16[32,3,16,128]{3,2,1,0:T(8,128)(2,1)S(1)}, bf16[32,3,16,128]{3,2,1,0:T(8,128)(2,1)S(1)}, u32[]{:S(2)}, u32[]{:S(2)}) collective-permute-start(bf16[32,3,16,128]{3,2,1,0:T(8,128)(2,1)S(1)} %pad_maximum_fusion.2.refs_0_), channel_id=1, source_target_pairs={{0,3},{1,0},{2,1},{3,2},{4,7},{5,4},{6,5},{7,6},{8,11},{9,8},{10,9... | collective-permute-start | bytes 1179656 | tf_op jit(solution)/shard_map/ppermute | solution.py:47
  48.5 10.9 %collective-permute-start = (bf16[8,8,16,128]{3,2,1,0:T(8,128)(2,1)S(1)}, bf16[8,8,16,128]{3,2,1,0:T(8,128)(2,1)S(1)}, u32[]{:S(2)}, u32[]{:S(2)}) collective-permute-start(bf16[8,8,16,128]{3,2,1,0:T(8,128)(2,1)S(1)} %slice.106), channel_id=1, source_target_pairs={{0,32},{1,33},{2,34},{3,35},{4,36},{5,37},{6,38},{7,39},{8,40},{9,... | collective-permute-start | bytes 786440 | tf_op jit(solution)/shard_map/ppermute | solution.py:47
  48.5 15.8 %collective-permute-start.13 = (bf16[32,3,16,128]{3,2,1,0:T(8,128)(2,1)S(1)}, bf16[32,3,16,128]{3,2,1,0:T(8,128)(2,1)S(1)}, u32[]{:S(2)}, u32[]{:S(2)}) collective-permute-start(bf16[32,3,16,128]{3,2,1,0:T(8,128)(2,1)S(1)} %pad_maximum_fusion.2.refs_0_), channel_id=1, source_target_pairs={{0,1},{1,2},{2,3},{3,0},{4,5},{5,6},{6,7},{7,4},{8,9},{9,10},{10,1... | collective-permute-start | bytes 1179656 | tf_op jit(solution)/shard_map/ppermute | solution.py:47
  49.5 0.9 slice-start.1
  49.5 1.0 slice-start.2
  50.7 54.5 %copy-start.14 = (f32[1280]{0:T(1024)S(1)}, f32[1280]{0:T(1024)}, u32[]{:S(2)}) copy-start(f32[1280]{0:T(1024)} %param.10) | copy-start | bytes 15364
  50.7 54.7 %copy-start.3 = (bf16[1,128,1280]{2,1,0:T(8,128)(2,1)S(1)}, bf16[1,128,1280]{2,1,0:T(8,128)(2,1)}, u32[]{:S(2)}) copy-start(bf16[1,128,1280]{2,1,0:T(8,128)(2,1)} %param.8) | copy-start | bytes 983044
  59.4 7.9 %collective-permute-start.23 = (bf16[32,6,16,128]{3,2,1,0:T(8,128)(2,1)S(1)}, bf16[32,6,16,128]{3,2,1,0:T(8,128)(2,1)S(1)}, u32[]{:S(2)}, u32[]{:S(2)}) collective-permute-start(bf16[32,6,16,128]{3,2,1,0:T(8,128)(2,1)S(1)} %pad_maximum_fusion.1.refs_0_), channel_id=1, source_target_pairs={{0,128},{1,129},{2,130},{3,131},{4,132},{5,133},{6,134},{7,135},{8... | collective-permute-start | bytes 2359304 | tf_op jit(solution)/shard_map/ppermute | solution.py:52
  59.4 13.6 %collective-permute-start.22 = (bf16[32,6,16,128]{3,2,1,0:T(8,128)(2,1)S(1)}, bf16[32,6,16,128]{3,2,1,0:T(8,128)(2,1)S(1)}, u32[]{:S(2)}, u32[]{:S(2)}) collective-permute-start(bf16[32,6,16,128]{3,2,1,0:T(8,128)(2,1)S(1)} %pad_maximum_fusion.1.refs_0_), channel_id=1, source_target_pairs={{0,2},{1,3},{2,0},{3,1},{4,6},{5,7},{6,4},{7,5},{8,10},{9,11},{10,... | collective-permute-start | bytes 2359304 | tf_op jit(solution)/shard_map/ppermute | solution.py:47
  62.6 2.0 %collective-permute-start.19 = (bf16[32,3,16,128]{3,2,1,0:T(8,128)(2,1)S(1)}, bf16[32,3,16,128]{3,2,1,0:T(8,128)(2,1)S(1)}, u32[]{:S(2)}, u32[]{:S(2)}) collective-permute-start(bf16[32,3,16,128]{3,2,1,0:T(8,128)(2,1)S(1)} %collective-permute-done.15.refs_3_), channel_id=1, source_target_pairs={{0,128},{1,129},{2,130},{3,131},{4,132},{5,133},{6,134},{7,135},{8... | collective-permute-start | bytes 1179656 | tf_op jit(solution)/shard_map/ppermute | solution.py:52
  62.6 4.7 %collective-permute-start.18 = (bf16[32,3,16,128]{3,2,1,0:T(8,128)(2,1)S(1)}, bf16[32,3,16,128]{3,2,1,0:T(8,128)(2,1)S(1)}, u32[]{:S(2)}, u32[]{:S(2)}) collective-permute-start(bf16[32,3,16,128]{3,2,1,0:T(8,128)(2,1)S(1)} %collective-permute-done.14.refs_2_), channel_id=1, source_target_pairs={{0,128},{1,129},{2,130},{3,131},{4,132},{5,133},{6,134},{7,135},{8... | collective-permute-start | bytes 1179656 | tf_op jit(solution)/shard_map/ppermute | solution.py:52
  64.2 40.9 %copy-start.15 = (f32[1280]{0:T(1024)S(1)}, f32[1280]{0:T(1024)}, u32[]{:S(2)}) copy-start(f32[1280]{0:T(1024)} %param.13) | copy-start | bytes 15364
  64.2 28.9 %collective-permute-start.5 = (bf16[32,8,16,128]{3,2,1,0:T(8,128)(2,1)}, bf16[32,8,16,128]{3,2,1,0:T(8,128)(2,1)}, u32[]{:S(2)}, u32[]{:S(2)}) collective-permute-start(bf16[32,8,16,128]{3,2,1,0:T(8,128)(2,1)} %pad_maximum_fusion), channel_id=1, source_target_pairs={{0,2},{1,3},{2,0},{3,1},{4,6},{5,7},{6,4},{7,5},{8,10},{9,11},{10,... | collective-permute-start | bytes 3145736 | tf_op jit(solution)/shard_map/ppermute | solution.py:47
  64.6 28.1 %collective-permute-start.21 = (bf16[32,6,16,128]{3,2,1,0:T(8,128)(2,1)S(1)}, bf16[32,6,16,128]{3,2,1,0:T(8,128)(2,1)S(1)}, u32[]{:S(2)}, u32[]{:S(2)}) collective-permute-start(bf16[32,6,16,128]{3,2,1,0:T(8,128)(2,1)S(1)} %pad_maximum_fusion.1.refs_0_), channel_id=1, source_target_pairs={{0,3},{1,0},{2,1},{3,2},{4,7},{5,4},{6,5},{7,6},{8,11},{9,8},{10,9... | collective-permute-start | bytes 2359304 | tf_op jit(solution)/shard_map/ppermute | solution.py:47
  67.3 25.4 %collective-permute-start.20 = (bf16[32,6,16,128]{3,2,1,0:T(8,128)(2,1)S(1)}, bf16[32,6,16,128]{3,2,1,0:T(8,128)(2,1)S(1)}, u32[]{:S(2)}, u32[]{:S(2)}) collective-permute-start(bf16[32,6,16,128]{3,2,1,0:T(8,128)(2,1)S(1)} %pad_maximum_fusion.1.refs_0_), channel_id=1, source_target_pairs={{0,1},{1,2},{2,3},{3,0},{4,5},{5,6},{6,7},{7,4},{8,9},{9,10},{10,1... | collective-permute-start | bytes 2359304 | tf_op jit(solution)/shard_map/ppermute | solution.py:47
  67.3 36.7 %collective-permute-start.4 = (bf16[32,8,16,128]{3,2,1,0:T(8,128)(2,1)}, bf16[32,8,16,128]{3,2,1,0:T(8,128)(2,1)}, u32[]{:S(2)}, u32[]{:S(2)}) collective-permute-start(bf16[32,8,16,128]{3,2,1,0:T(8,128)(2,1)} %pad_maximum_fusion), channel_id=1, source_target_pairs={{0,3},{1,0},{2,1},{3,2},{4,7},{5,4},{6,5},{7,6},{8,11},{9,8},{10,9... | collective-permute-start | bytes 3145736 | tf_op jit(solution)/shard_map/ppermute | solution.py:47
  73.0 31.0 %collective-permute-start.3 = (bf16[32,8,16,128]{3,2,1,0:T(8,128)(2,1)}, bf16[32,8,16,128]{3,2,1,0:T(8,128)(2,1)}, u32[]{:S(2)}, u32[]{:S(2)}) collective-permute-start(bf16[32,8,16,128]{3,2,1,0:T(8,128)(2,1)} %pad_maximum_fusion), channel_id=1, source_target_pairs={{0,1},{1,2},{2,3},{3,0},{4,5},{5,6},{6,7},{7,4},{8,9},{9,10},{10,1... | collective-permute-start | bytes 3145736 | tf_op jit(solution)/shard_map/ppermute | solution.py:47
  92.6 11.9 %collective-permute-start.26 = (bf16[32,6,16,128]{3,2,1,0:T(8,128)(2,1)S(1)}, bf16[32,6,16,128]{3,2,1,0:T(8,128)(2,1)S(1)}, u32[]{:S(2)}, u32[]{:S(2)}) collective-permute-start(bf16[32,6,16,128]{3,2,1,0:T(8,128)(2,1)S(1)} %collective-permute-done.22.refs_3_), channel_id=1, source_target_pairs={{0,128},{1,129},{2,130},{3,131},{4,132},{5,133},{6,134},{7,135},{8... | collective-permute-start | bytes 2359304 | tf_op jit(solution)/shard_map/ppermute | solution.py:52
  92.6 12.0 %collective-permute-start.25 = (bf16[32,6,16,128]{3,2,1,0:T(8,128)(2,1)S(1)}, bf16[32,6,16,128]{3,2,1,0:T(8,128)(2,1)S(1)}, u32[]{:S(2)}, u32[]{:S(2)}) collective-permute-start(bf16[32,6,16,128]{3,2,1,0:T(8,128)(2,1)S(1)} %collective-permute-done.21.refs_2_), channel_id=1, source_target_pairs={{0,128},{1,129},{2,130},{3,131},{4,132},{5,133},{6,134},{7,135},{8... | collective-permute-start | bytes 2359304 | tf_op jit(solution)/shard_map/ppermute | solution.py:52
  93.2 11.9 %collective-permute-start.24 = (bf16[32,6,16,128]{3,2,1,0:T(8,128)(2,1)S(1)}, bf16[32,6,16,128]{3,2,1,0:T(8,128)(2,1)S(1)}, u32[]{:S(2)}, u32[]{:S(2)}) collective-permute-start(bf16[32,6,16,128]{3,2,1,0:T(8,128)(2,1)S(1)} %collective-permute-done.20.refs_1_), channel_id=1, source_target_pairs={{0,128},{1,129},{2,130},{3,131},{4,132},{5,133},{6,134},{7,135},{8... | collective-permute-start | bytes 2359304 | tf_op jit(solution)/shard_map/ppermute | solution.py:52
  104.0 7.5 %collective-permute-start.17 = (bf16[32,3,16,128]{3,2,1,0:T(8,128)(2,1)S(1)}, bf16[32,3,16,128]{3,2,1,0:T(8,128)(2,1)S(1)}, u32[]{:S(2)}, u32[]{:S(2)}) collective-permute-start(bf16[32,3,16,128]{3,2,1,0:T(8,128)(2,1)S(1)} %collective-permute-done.13.refs_1_), channel_id=1, source_target_pairs={{0,128},{1,129},{2,130},{3,131},{4,132},{5,133},{6,134},{7,135},{8... | collective-permute-start | bytes 1179656 | tf_op jit(solution)/shard_map/ppermute | solution.py:52
  104.0 23.9 %collective-permute-start.6 = (bf16[32,8,16,128]{3,2,1,0:T(8,128)(2,1)}, bf16[32,8,16,128]{3,2,1,0:T(8,128)(2,1)}, u32[]{:S(2)}, u32[]{:S(2)}) collective-permute-start(bf16[32,8,16,128]{3,2,1,0:T(8,128)(2,1)} %pad_maximum_fusion), channel_id=1, source_target_pairs={{0,128},{1,129},{2,130},{3,131},{4,132},{5,133},{6,134},{7,135},{8... | collective-permute-start | bytes 3145736 | tf_op jit(solution)/shard_map/ppermute | solution.py:52
  104.5 0.9 copy-start.12
  104.5 24.6 %collective-permute-start.9 = (bf16[32,8,16,128]{3,2,1,0:T(8,128)(2,1)}, bf16[32,8,16,128]{3,2,1,0:T(8,128)(2,1)}, u32[]{:S(2)}, u32[]{:S(2)}) collective-permute-start(bf16[32,8,16,128]{3,2,1,0:T(8,128)(2,1)} %collective-permute-done.5), channel_id=1, source_target_pairs={{0,128},{1,129},{2,130},{3,131},{4,132},{5,133},{6,134},{7,135},{8... | collective-permute-start | bytes 3145736 | tf_op jit(solution)/shard_map/ppermute | solution.py:52
  104.6 26.5 %collective-permute-start.8 = (bf16[32,8,16,128]{3,2,1,0:T(8,128)(2,1)}, bf16[32,8,16,128]{3,2,1,0:T(8,128)(2,1)}, u32[]{:S(2)}, u32[]{:S(2)}) collective-permute-start(bf16[32,8,16,128]{3,2,1,0:T(8,128)(2,1)} %collective-permute-done.4), channel_id=1, source_target_pairs={{0,128},{1,129},{2,130},{3,131},{4,132},{5,133},{6,134},{7,135},{8... | collective-permute-start | bytes 3145736 | tf_op jit(solution)/shard_map/ppermute | solution.py:52
  105.0 28.1 %collective-permute-start.7 = (bf16[32,8,16,128]{3,2,1,0:T(8,128)(2,1)}, bf16[32,8,16,128]{3,2,1,0:T(8,128)(2,1)}, u32[]{:S(2)}, u32[]{:S(2)}) collective-permute-start(bf16[32,8,16,128]{3,2,1,0:T(8,128)(2,1)} %collective-permute-done.3), channel_id=1, source_target_pairs={{0,128},{1,129},{2,130},{3,131},{4,132},{5,133},{6,134},{7,135},{8... | collective-permute-start | bytes 3145736 | tf_op jit(solution)/shard_map/ppermute | solution.py:52
  112.8 0.7 copy-start.4
  115.6 23.3 %all-to-all-start.1 = ((bf16[128,2,640]{2,1,0:T(2,128)(2,1)}), bf16[128,2,640]{2,1,0:T(2,128)(2,1)}, u32[]{:S(2)}, u32[]{:S(2)}) async-start(bf16[128,2,640]{2,1,0:T(2,128)(2,1)} %reshape.21), calls=%async_computation.1 | async-start | bytes 655360 | tf_op jit(solution)/shard_map/all_to_all | solution.py:269
  142.1 1.3 copy-start
  143.4 1.1 copy-start.1
  144.5 1.1 copy-start.2
  150.9 23.2 %all-to-all-start.2 = ((bf16[128,2,320]{2,1,0:T(2,128)(2,1)}), bf16[128,2,320]{2,1,0:T(2,128)(2,1)}, u32[]{:S(2)}, u32[]{:S(2)}) async-start(bf16[128,2,320]{2,1,0:T(2,128)(2,1)} %reshape.23), calls=%async_computation.2 | async-start | bytes 393216 | tf_op jit(solution)/shard_map/all_to_all | solution.py:278
  175.8 1.0 copy-start.5

commit v2 on v1

v2 whole, which is shorter than its diff:
```python
import functools
import itertools

import jax
import jax.numpy as jnp
from jax import lax
from jax.experimental import pallas as pl
from jax.experimental.pallas import tpu as pltpu
from jax.sharding import PartitionSpec as P

D = 1280
HEADS = 10
HEAD = 64
INNER = 640
PIX = 128
NX, NZ, NY = 4, 8, 4
SEQ = NX * NZ * NY
EPS = 1e-05
BF = jnp.bfloat16
F32 = jnp.float32
SHIFTS = (0, 1, 3, 2)
GROUP = 7
TILES = 2 * GROUP


def seq_of(x, z, y):
    return (x * NZ + z) * NY + y


Z_GROUPS = [[seq_of(x, z, y) for z in range(NZ)] for x in range(NX) for y in range(NY)]
SWAP = [(i, (i + SEQ) % (2 * SEQ)) for i in range(2 * SEQ)]


def ring_perm(k, stage):
    pairs = []
    for c, x, z, y in itertools.product(range(2), range(NX), range(NZ), range(NY)):
        if (c + stage) % 2 == 0:
            to = ((x + k) % NX, z, y)
        else:
            to = (x, z, (y + k) % NY)
        pairs.append((c * SEQ + seq_of(x, z, y), c * SEQ + seq_of(*to)))
    return pairs


def ring(block, stage):
    return [block] + [
        lax.ppermute(block, ("clip", "seq"), ring_perm(k, stage)) for k in SHIFTS[1:]
    ]


def ring_by_halves(pair, stage):
    def shift(part, k):
        return lax.ppermute(part, ("clip", "seq"), ring_perm(k, stage))

    one, two = pair
    up_one, down_two = shift(one, 1), shift(two, 3)
    up_two, down_one = shift(two, 1), shift(one, 3)
    far_one, far_two = shift(up_one, 1), shift(down_two, 3)
    return [one, two, up_one, up_two, down_one, down_two, far_one, far_two]


def swap(block):
    return lax.ppermute(block, ("clip", "seq"), SWAP)


def vmem(n):
    return [pl.BlockSpec(memory_space=pltpu.VMEM)] * n


ANY = pl.BlockSpec(memory_space=pl.ANY)


def small(mib):
    return pltpu.CompilerParams(vmem_limit_bytes=mib * 1024 * 1024)


def layer_norm(x, gain):
    mean = jnp.mean(x, axis=-1, keepdims=True)
    d = x - mean
    var = jnp.mean(d * d, axis=-1, keepdims=True)
    return (d * lax.rsqrt(var + EPS) * gain).astype(BF)


def pack_kernel(ws_in, ref_in, wo_in, wt_in, wu_in, out, ws, ref, wo, wt, wu, sems):
    c = lax.axis_index("clip")
    pairs = ((ws_in, ws), (ref_in, ref), (wo_in, wo), (wt_in, wt), (wu_in, wu))
    copies = [pltpu.make_async_copy(src, dst, sems.at[i]) for i, (src, dst) in enumerate(pairs)]
    for copy in copies:
        copy.start()
    for copy in copies:
        copy.wait()

    def tile(*rows):
        n = sum(r.shape[0] for r in rows)
        parts = [r.astype(F32) for r in rows]
        if n < 16:
            parts.append(jnp.zeros((16 - n, 128), F32))
        return jnp.concatenate(parts, axis=0).astype(BF)

    def lane(ref, t):
        return ref[:, 128 * t : 128 * (t + 1)]

    def fill(half):
        refs = [lane(ref, u) for u in range(10)]
        for t in range(5):
            out[t] = tile(lane(ws, 5 * half + t), refs[t])
            out[GROUP + t] = tile(lane(wt, 5 * half + t))
        for at, w, extra in ((5, wo, refs[5:]), (GROUP + 5, wu, [])):
            middle = lane(w, 2).astype(F32)[5 * half : 5 * half + 5]
            out[at] = tile(lane(w, 3 * half), middle)
            out[at + 1] = tile(lane(w, 3 * half + 1), *extra)

    for half in range(2):
        pl.when(c == half)(functools.partial(fill, half))


def halves_kernel(along_z, p1, p2, p3, one, two):
    spatial = (along_z, p1, p2, p3)
    for half, out in enumerate((one, two)):
        for i in range(2):
            out[8 * i : 8 * i + 8] = spatial[2 * half + i][:, 0:GROUP]
        out[16:20] = along_z[4 * half : 4 * half + 4, GROUP : 2 * GROUP]


def temporal_blocks_kernel(*refs):
    out = refs[-1]
    for i, piece in enumerate(refs[:-1]):
        out[4 * i : 4 * i + 4] = piece[16:20]


def gate_kernel(*refs):
    pass


def gate(values, after):
    n = len(values)
    return list(
        pl.pallas_call(
            gate_kernel,
            out_shape=[jax.ShapeDtypeStruct(v.shape, v.dtype) for v in values],
            in_specs=vmem(n + 1),
            out_specs=vmem(n),
            input_output_aliases={i: i for i in range(n)},
            compiler_params=small(1),
            name="gate",
        )(*values, after)
    )


def reorder(kernel, args, outs, name):
    return pl.pallas_call(
        kernel,
        out_shape=[jax.ShapeDtypeStruct((n, GROUP, 16, 128), BF) for n in outs],
        in_specs=vmem(len(args)),
        out_specs=vmem(len(outs)),
        compiler_params=small(4),
        name=name,
    )(*args)


def to_rows(value, out, rows, n):
    wide = 2 * out.shape[1]
    for t in range(wide):
        at = pl.ds(t, 128, stride=wide)
        rows[at, :] = value[:, 128 * t : 128 * (t + 1)] if t < n else jnp.zeros((128, 128), F32)
    out.reshape(128 * wide, 128)[...] = rows[...].astype(BF)


def from_rows(ref, rows, n):
    wide = 2 * ref.shape[1]
    rows[...] = ref.reshape(128 * wide, 128)[...].astype(F32)
    return jnp.concatenate(
        [rows[pl.ds(t, 128, stride=wide), :] for t in range(n)], axis=1
    ).astype(BF)


def place():
    s = lax.axis_index("seq")
    return lax.axis_index("clip"), s // (NZ * NY), lax.rem(s, NY)


def blocks(refs, j, i):
    per_shift = len(refs) // 4
    at = 4 // per_shift
    return refs[per_shift * j + i // at], 8 * (i % at)


def lanes(refs, j, i, first, count):
    ref, start = blocks(refs, j, i)
    parts = [ref[start : start + 8, first + t].reshape(128, 128) for t in range(count)]
    return jnp.concatenate(parts, axis=1)


def pieces_of(own, oth, j, first, count):
    wa = [lanes(own, j, i, first, count) for i in range(4)]
    wb = [lanes(oth, i, j, first, count) for i in range(4)]
    return jnp.concatenate(wa, axis=0), jnp.concatenate(wb, axis=0)


def spread(acc, r, j, row, x_core):
    c, x, y = place()
    for i in range(4):
        dx = jnp.where(c == x_core, SHIFTS[i], SHIFTS[j])
        dy = jnp.where(c == x_core, SHIFTS[j], SHIFTS[i])
        xs = lax.rem(x - dx + NX, NX)
        ys = lax.rem(y - dy + NY, NY)
        for z in range(NZ):
            at = (i * 8 + z) * 16
            acc[xs, z, ys, row : row + 16, :] = r[at : at + 16]


NT = (((1,), (1,)), ((), ()))
NN = (((1,), (0,)), ((), ()))


def dot(a, b, dims):
    return lax.dot_general(a, b, dims, preferred_element_type=F32)


def qkv_project(own, oth, acc, rows, tokens, x_core):
    c, _, _ = place()
    xa, xb = halves(tokens, c)
    for j in range(4):
        wa, wb = pieces_of(own, oth, j, 0, 5)
        spread(acc, dot(wa, xa, NT) + dot(wb, xb, NT), j, 0, x_core)
    for s in range(SEQ):
        x, z, y = s // 32, (s // 4) % 8, s % 4
        rows[15 * s : 15 * s + 15, :] = acc[x, z, y, 0:15, :]


def out_project(own, oth, acc, rows, part, dims, x_core):
    c, _, _ = place()
    lo, mid, hi = part(0, 256), part(256, 384), part(384, 640)
    xa = jnp.where(c == 0, lo, hi)
    xb = jnp.where(c == 0, hi, lo)
    for j in range(4):
        wa, wb = pieces_of(own, oth, j, 5, 2)
        spread(acc, dot(wa, xa, dims) + dot(wb, xb, dims), j, 0, x_core)
        ma, mb = dot(wa[:, :128], mid, dims), dot(wb[:, :128], mid, dims)
        spread(acc, jnp.where(c == 0, ma, mb), j, 16, x_core)
        spread(acc, jnp.where(c == 0, mb, ma), j, 32, x_core)
    for s in range(SEQ):
        x, z, y = s // 32, (s // 4) % 8, s % 4
        m0 = acc[x, z, y, 26:31, :]
        m1 = acc[x, z, y, 42:47, :]
        rows[10 * s : 10 * s + 10, :] = acc[x, z, y, 0:10, :] + jnp.concatenate([m0, m1], axis=0)


def halves(xv, c):
    lo, hi = xv[:, :640], xv[:, 640:]
    first = c == 0
    return jnp.where(first, lo, hi), jnp.where(first, hi, lo)


def heads(rows, keys, attn):
    for h in range(HEADS):
        q = rows[64 * h : 64 * (h + 1), 0:128].astype(BF)
        k = rows[640 + 64 * h : 640 + 64 * (h + 1), 0:keys].astype(BF)
        v = rows[1280 + 64 * h : 1280 + 64 * (h + 1), 0:keys].astype(BF)
        st = lax.dot_general(k, q, (((0,), (0,)), ((), ())), preferred_element_type=F32)
        st = st * (HEAD**-0.5)
        e = jnp.exp(st - jnp.max(st, axis=0, keepdims=True))
        p = (e * (1.0 / jnp.sum(e, axis=0, keepdims=True))).astype(BF)
        attn[64 * h : 64 * (h + 1), :] = jnp.dot(v, p, preferred_element_type=F32)


def reference_tokens(own, last):
    parts = []
    for t in (0, 1, 2, 3, 4, 6):
        for j in range(4):
            for i in range(4):
                at = (j * 4 + i) * 64
                ref, start = blocks(own, j, i)
                tail = ref[start : start + 8, t].astype(F32)[:, 8:16, :]
                last[t, at : at + 64, :] = tail.reshape(64, 128)
        at = (7,) if t < 5 else (2, 3, 4, 5, 6)
        parts += [last[t, pl.ds(r, 128, stride=8), :] for r in at]
    return jnp.concatenate(parts, axis=1).astype(BF)


def spatial_kernel(*refs):
    own, oth = refs[0:8], refs[8:16]
    latents, gain_s, gain_t, hidden, tnormed, acc, rows, last, attn, acc_out, rows_out = refs[16:]
    normed = layer_norm(latents[...].astype(F32), gain_s[...])
    tokens = jnp.concatenate([normed, reference_tokens(own, last)], axis=0)
    qkv_project(own, oth, acc, rows, tokens, 0)
    heads(rows, 256, attn)
    part = lambda a, b: attn[a:b, :].astype(BF)
    out_project(own, oth, acc_out, rows_out, part, NN, 0)
    h = (latents[...].astype(F32) + rows_out[...].T).astype(BF)
    hidden[...] = h
    to_rows(layer_norm(h.astype(F32), gain_t[...]).astype(F32), tnormed, rows_out, 10)


def temporal_kernel(*refs):
    own, oth = refs[0:4], refs[4:8]
    tokens, out, acc, rows, attn, wide, wide_out = refs[8:]
    qkv_project(own, oth, acc, rows, from_rows(tokens, wide, 10), 1)
    heads(rows, 128, attn)
    to_rows(attn[...].T, out, wide_out, 5)


def mixed_kernel(*refs):
    own, oth = refs[0:4], refs[4:8]
    attn, hidden, mixed, acc, rows, wide = refs[8:]
    a = from_rows(attn, wide, 5)
    out_project(own, oth, acc, rows, lambda first, last: a[:, first:last], NT, 1)
    mixed[...] = (hidden[...].astype(F32) + rows[...].T).astype(BF)


def call(kernel, args, outs, scratch, name, flops, mib):
    shapes = [jax.ShapeDtypeStruct(s, BF) for s in outs]
    single = len(shapes) == 1
    size = sum(a.size * a.dtype.itemsize for a in args) + sum(2 * s.size for s in shapes)
    return pl.pallas_call(
        kernel,
        out_shape=shapes[0] if single else shapes,
        in_specs=vmem(len(args)),
        out_specs=vmem(1)[0] if single else vmem(len(shapes)),
        scratch_shapes=[pltpu.VMEM(s, F32) for s in scratch],
        compiler_params=small(mib),
        cost_estimate=pl.CostEstimate(flops=flops, bytes_accessed=size, transcendentals=0),
        name=name,
    )(*args)


def body(latents, ref_hidden, gain_s, w_s, w_o, gain_t, w_t, w_u):
    latents = latents.reshape(PIX, D)
    gain_s = gain_s.reshape(1, D)
    gain_t = gain_t.reshape(1, D)
    shards = [w_s.T, ref_hidden, w_o.T, w_t.T, w_u.T]
    packed = pl.pallas_call(
        pack_kernel,
        out_shape=jax.ShapeDtypeStruct((TILES, 16, 128), BF),
        in_specs=[ANY] * 5,
        out_specs=vmem(1)[0],
        scratch_shapes=[pltpu.VMEM(a.shape, BF) for a in shards] + [pltpu.SemaphoreType.DMA((5,))],
        compiler_params=small(60),
        name="pack",
    )(*shards)
    along_z = lax.all_to_all(
        jnp.broadcast_to(packed[None], (NZ, TILES, 16, 128)),
        "seq",
        0,
        0,
        axis_index_groups=Z_GROUPS,
        tiled=True,
    )
    first = ring(along_z[:, :GROUP], 0)
    own_s = ring_by_halves(reorder(halves_kernel, [along_z] + first[1:], [20, 20], "halves"), 1)
    oth_s = [swap(b) for b in own_s]
    (part_t,) = reorder(temporal_blocks_kernel, own_s, [32], "temporal_blocks")
    ring_t = ring(part_t, 0)

    hidden, tnormed = call(
        spatial_kernel,
        own_s + oth_s + [latents, gain_s, gain_t],
        [(PIX, D), (PIX, 5, 2, 128)],
        [
            (NX, NZ, NY, 16, 256),
            (1920, 256),
            (GROUP, 1024, 128),
            (INNER, 128),
            (NX, NZ, NY, 48, 128),
            (D, 128),
        ],
        "spatial",
        9 * 10**9,
        24,
    )
    tokens = lax.all_to_all(tnormed, "seq", 0, 0, tiled=True)
    own_t = ring_t[:1] + gate(ring_t[1:], tokens)
    oth_t = [swap(ring_t[0])] + [swap(b) for b in own_t[1:]]
    tattn = call(
        temporal_kernel,
        own_t + oth_t + [tokens],
        [(PIX, 3, 2, 128)],
        [(NX, NZ, NY, 16, 128), (1920, 128), (INNER, 128), (D, 128), (768, 128)],
        "temporal",
        5 * 10**9,
        16,
    )
    back = lax.all_to_all(tattn, "seq", 0, 0, tiled=True)
    mixed = call(
        mixed_kernel,
        own_t + oth_t + [back, hidden],
        [(PIX, D)],
        [(NX, NZ, NY, 48, 128), (D, 128), (768, 128)],
        "mixed",
        3 * 10**9,
        16,
    )
    return mixed.reshape(1, PIX, D)


def solution(mesh):
    in_specs = (
        P(("clip", "seq"), None, None),
        P(("clip", "seq"), None),
        P(),
        P(None, "seq"),
        P(None, "seq"),
        P(),
        P(None, "seq"),
        P(None, "seq"),
    )
    out_specs = P(("clip", "seq"), None, None)
    return jax.shard_map(body, mesh=mesh, in_specs=in_specs, out_specs=out_specs, check_vma=False)
```

time: 180 us -> 136 us (0.76)
  local copies, waits for them, and re-layouts: 37.3 us -> 0.92 us
  blocking collectives: 25.1 us -> 42.7 us
  starting transfers between devices: 45.4 us -> 29.7 us
  waiting for transfers between devices: 54.8 us -> 42.3 us
  Pallas kernels: 13.1 us -> 19.5 us
  other arithmetic: 2.6 us -> 0 us
    ppermute x15 -> x6, waiting for transfers between devices: 46.4 us -> 11.5 us  [ring(): lax.ppermute(block, ('clip', 'seq'), ring_perm(k, stage))]
    slice x29 -> x1, local copies, waits for them, and re-layouts: 21.1 us -> 0.02 us  [body(): first = ring(along_z[:, :GROUP], 0)]
    all_to_all x0 -> x1, blocking collectives: none -> 19.7 us  [body(): back = lax.all_to_all(tattn, 'seq', 0, 0, tiled=True)]
    ppermute x0 -> x6, waiting for transfers between devices: none -> 16.7 us  [shift(): return lax.ppermute(part, ('clip', 'seq'), ring_perm(k, stage))]
    ppermute x15 -> x6, starting transfers between devices: 24.9 us -> 8.77 us  [ring(): lax.ppermute(block, ('clip', 'seq'), ring_perm(k, stage))]
    unnamed x38 -> x6, local copies, waits for them, and re-layouts: 15.6 us -> 0.02 us
    all_to_all x1 -> x0, starting transfers between devices: 10.4 us -> none  [body(): back = lax.all_to_all(tattn, 'seq', 0, 0, tiled=True)]
    ppermute x0 -> x6, starting transfers between devices: none -> 10 us  [shift(): return lax.ppermute(part, ('clip', 'seq'), ring_perm(k, stage))]
  transfers between devices with their start and end apart: 29 -> 25, of which waited for: 8 -> 14; matrix products, arithmetic and copies ran while one was open for 13% -> 0% of each run, Pallas kernels for 4% -> 6%
where the time goes in v2:
time: 136 us; the launch traced here: 135 us
  blocking collectives  42.7 us (31%)
  waiting for transfers between devices  42.3 us (31%)
  starting transfers between devices  29.7 us (22%)
  Pallas kernels  19.5 us (14%)
    all_to_all x1, blocking collectives, body(): lax.all_to_all(jnp.broadcast_to(packed[None], (NZ, TILES, 16, 128)), 'seq...  23 us
    all_to_all x1, blocking collectives, body(): back = lax.all_to_all(tattn, 'seq', 0, 0, tiled=True)  19.7 us
    pallas_call x3, Pallas kernels, call(): pl.pallas_call(kernel, out_shape=shapes[0] if single else shapes, in_spec...  16.9 us
    ppermute x6, waiting for transfers between devices, shift(): return lax.ppermute(part, ('clip', 'seq'), ring_perm(k, stage))  16.7 us
    ppermute x6, waiting for transfers between devices, ring(): lax.ppermute(block, ('clip', 'seq'), ring_perm(k, stage))  11.5 us
    ppermute x6, starting transfers between devices, shift(): return lax.ppermute(part, ('clip', 'seq'), ring_perm(k, stage))  10 us
    all_to_all x1, starting transfers between devices, body(): tokens = lax.all_to_all(tnormed, 'seq', 0, 0, tiled=True)  9.59 us
    all_to_all x1, waiting for transfers between devices, body(): tokens = lax.all_to_all(tnormed, 'seq', 0, 0, tiled=True)  9.41 us
  transfers between devices with their start and end apart: 25, of which 14 were waited for; matrix products, arithmetic and copies ran while one was open for 0% of the time, Pallas kernels for 6%

profile of v2, /device:TPU:32, one launch (start us, length us, event | category | flops | bytes accessed | tf_op | source)
XLA Modules:
  0.0 135.2 jit_solution(12193310933992961593)
XLA Ops:
  0.0 1.5 %pack.1 = bf16[14,16,128]{2,1,0:T(8,128)(2,1)} custom-call(bf16[15,1280]{1,0:T(8,128)(2,1)} %bitcast.7, bf16[1,1280]{1,0:T(2,128)(2,1)} %ref_in.1, bf16[10,640]{1,0:T(8,128)(2,1)} %bitcast.9, bf16[15,1280]{1,0:T(8,128)(2,1)} %bitcast.8, bf16[10,640]{1,0:T(8,128)(2,1)} %bitcast.10), custom_call_target="tpu_custom_call" | custom-call | tf_op jit(solution)/shard_map/pack/pallas_call | solution.py:332
  1.5 0.9 broadcast_in_dim.2
  2.4 23.0 %all_to_all.15.along_z = bf16[8,14,16,128]{3,2,1,0:T(8,128)(2,1)S(1)} all-to-all(bf16[8,14,16,128]{3,2,1,0:T(8,128)(2,1)S(1)} %broadcast_in_dim.2), channel_id=1, replica_groups={{0,4,8,12,16,20,24,28},{1,5,9,13,17,21,25,29},{2,6,10,14,18,22,26,30},{..., dimensions={0} | all-to-all | bytes 917504 | tf_op jit(solution)/shard_map/all_to_all | solution.py:341
  25.4 3.1 %collective-permute-start.2 = (bf16[8,7,16,128]{3,2,1,0:T(8,128)(2,1)S(1)}, bf16[8,7,16,128]{3,2,1,0:T(8,128)(2,1)S(1)}, u32[]{:S(2)}, u32[]{:S(2)}) collective-permute-start(bf16[8,7,16,128]{3,2,1,0:T(8,128)(2,1)S(1)} %slice.4), channel_id=1, source_target_pairs={{0,64},{1,65},{2,66},{3,67},{4,68},{5,69},{6,70},{7,71},{8,72},{9,... | collective-permute-start | bytes 688136 | tf_op jit(solution)/shard_map/ppermute | solution.py:47
  28.5 1.1 collective-permute-start.1
  29.7 0.9 collective-permute-start
  30.6 2.5 %collective-permute-done.2.p3 = bf16[8,7,16,128]{3,2,1,0:T(8,128)(2,1)S(1)} collective-permute-done((bf16[8,7,16,128]{3,2,1,0:T(8,128)(2,1)S(1)}, bf16[8,7,16,128]{3,2,1,0:T(8,128)(2,1)S(1)}, u32[]{:S(2)}, u32[]{:S(2)}) %collective-permute-start.2) | collective-permute-done | bytes 229408 | tf_op jit(solution)/shard_map/ppermute | solution.py:47
  33.0 2.5 %collective-permute-done.1.p2 = bf16[8,7,16,128]{3,2,1,0:T(8,128)(2,1)S(1)} collective-permute-done((bf16[8,7,16,128]{3,2,1,0:T(8,128)(2,1)S(1)}, bf16[8,7,16,128]{3,2,1,0:T(8,128)(2,1)S(1)}, u32[]{:S(2)}, u32[]{:S(2)}) %collective-permute-start.1) | collective-permute-done | bytes 229408 | tf_op jit(solution)/shard_map/ppermute | solution.py:47
  35.6 1.3 collective-permute-done.p1
  36.9 0.1 halves.1
  37.0 0.0 copy-start.2
  37.0 0.1 collective-permute-start.12
  37.1 3.1 %collective-permute-start.5 = (bf16[20,7,16,128]{3,2,1,0:T(8,128)(2,1)S(1)}, bf16[20,7,16,128]{3,2,1,0:T(8,128)(2,1)S(1)}, u32[]{:S(2)}, u32[]{:S(2)}) collective-permute-start(bf16[20,7,16,128]{3,2,1,0:T(8,128)(2,1)S(1)} %get-tuple-element.12.refs_0_), channel_id=1, source_target_pairs={{0,3},{1,0},{2,1},{3,2},{4,7},{5,4},{6,5},{7,6},{8,11},{9,8},{10,9... | collective-permute-start | bytes 1720328 | tf_op jit(solution)/shard_map/ppermute | solution.py:53
  40.2 0.0 collective-permute-start.3
  40.2 3.2 %collective-permute-start.6 = (bf16[20,7,16,128]{3,2,1,0:T(8,128)(2,1)S(1)}, bf16[20,7,16,128]{3,2,1,0:T(8,128)(2,1)S(1)}, u32[]{:S(2)}, u32[]{:S(2)}) collective-permute-start(bf16[20,7,16,128]{3,2,1,0:T(8,128)(2,1)S(1)} %get-tuple-element.13.refs_1_), channel_id=1, source_target_pairs={{0,3},{1,0},{2,1},{3,2},{4,7},{5,4},{6,5},{7,6},{8,11},{9,8},{10,9... | collective-permute-start | bytes 1720328 | tf_op jit(solution)/shard_map/ppermute | solution.py:53
  43.4 0.0 collective-permute-start.13
  43.4 0.0 collective-permute-done.12.refs_8_
  43.4 0.0 collective-permute-start.4
  43.4 4.0 %collective-permute-done.5.refs_4_ = bf16[20,7,16,128]{3,2,1,0:T(8,128)(2,1)S(1)} collective-permute-done((bf16[20,7,16,128]{3,2,1,0:T(8,128)(2,1)S(1)}, bf16[20,7,16,128]{3,2,1,0:T(8,128)(2,1)S(1)}, u32[]{:S(2)}, u32[]{:S(2)}) %collective-permute-start.5) | collective-permute-done | bytes 573472 | tf_op jit(solution)/shard_map/ppermute | solution.py:53
  47.4 0.0 collective-permute-start.16
  47.4 3.7 %collective-permute-done.3.refs_2_ = bf16[20,7,16,128]{3,2,1,0:T(8,128)(2,1)S(1)} collective-permute-done((bf16[20,7,16,128]{3,2,1,0:T(8,128)(2,1)S(1)}, bf16[20,7,16,128]{3,2,1,0:T(8,128)(2,1)S(1)}, u32[]{:S(2)}, u32[]{:S(2)}) %collective-permute-start.3) | collective-permute-done | bytes 573472 | tf_op jit(solution)/shard_map/ppermute | solution.py:53
  51.1 0.0 collective-permute-start.7
  51.1 2.4 %collective-permute-done.6.refs_5_ = bf16[20,7,16,128]{3,2,1,0:T(8,128)(2,1)S(1)} collective-permute-done((bf16[20,7,16,128]{3,2,1,0:T(8,128)(2,1)S(1)}, bf16[20,7,16,128]{3,2,1,0:T(8,128)(2,1)S(1)}, u32[]{:S(2)}, u32[]{:S(2)}) %collective-permute-start.6) | collective-permute-done | bytes 573472 | tf_op jit(solution)/shard_map/ppermute | solution.py:53
  53.6 3.7 %collective-permute-start.8 = (bf16[20,7,16,128]{3,2,1,0:T(8,128)(2,1)S(1)}, bf16[20,7,16,128]{3,2,1,0:T(8,128)(2,1)S(1)}, u32[]{:S(2)}, u32[]{:S(2)}) collective-permute-start(bf16[20,7,16,128]{3,2,1,0:T(8,128)(2,1)S(1)} %collective-permute-done.6.refs_5_), channel_id=1, source_target_pairs={{0,3},{1,0},{2,1},{3,2},{4,7},{5,4},{6,5},{7,6},{8,11},{9,8},{10,9... | collective-permute-start | bytes 1720328 | tf_op jit(solution)/shard_map/ppermute | solution.py:53
  57.3 0.0 collective-permute-done.13.refs_9_
  57.3 0.0 collective-permute-start.14
  57.3 0.0 collective-permute-done.4.refs_3_
  57.3 0.5 collective-permute-start.17
  57.8 0.0 collective-permute-done.16.refs_12_
  57.8 0.1 collective-permute-start.15
  57.9 5.5 %collective-permute-done.7.refs_6_ = bf16[20,7,16,128]{3,2,1,0:T(8,128)(2,1)S(1)} collective-permute-done((bf16[20,7,16,128]{3,2,1,0:T(8,128)(2,1)S(1)}, bf16[20,7,16,128]{3,2,1,0:T(8,128)(2,1)S(1)}, u32[]{:S(2)}, u32[]{:S(2)}) %collective-permute-start.7) | collective-permute-done | bytes 573472 | tf_op jit(solution)/shard_map/ppermute | solution.py:53
  63.4 0.0 collective-permute-start.18
  63.4 1.1 collective-permute-done.8.refs_7_
  64.5 0.0 collective-permute-start.19
  64.5 0.0 copy-done.1
  64.5 0.0 copy-done.2
  64.5 0.0 copy-start
  64.5 1.0 temporal_blocks.1.refs_0_
  65.5 0.0 collective-permute-done.14.refs_10_
  65.5 1.6 %collective-permute-start.11 = (bf16[32,7,16,128]{3,2,1,0:T(8,128)(2,1)}, bf16[32,7,16,128]{3,2,1,0:T(8,128)(2,1)S(1)}, u32[]{:S(2)}, u32[]{:S(2)}) collective-permute-start(bf16[32,7,16,128]{3,2,1,0:T(8,128)(2,1)} %temporal_blocks.1.refs_0_), channel_id=1, source_target_pairs={{0,64},{1,65},{2,66},{3,67},{4,68},{5,69},{6,70},{7,71},{8,72},{9,... | collective-permute-start | bytes 2752520 | tf_op jit(solution)/shard_map/ppermute | solution.py:47
  67.1 0.0 collective-permute-done.17.refs_13_
  67.2 1.2 collective-permute-start.10
  68.3 0.0 collective-permute-done.15.refs_11_
  68.3 0.9 collective-permute-start.9
  69.2 0.0 collective-permute-done.18.refs_14_
  69.2 0.0 collective-permute-done.19.refs_15_
  69.2 0.0 copy-done
  69.2 7.5 %spatial.1 = (bf16[128,1280]{1,0:T(8,128)(2,1)S(1)}, bf16[128,5,2,128]{3,2,1,0:T(2,128)(2,1)}) custom-call(bf16[20,7,16,128]{3,2,1,0:T(8,128)(2,1)S(1)} %get-tuple-element.12.refs_0_, bf16[20,7,16,128]{3,2,1,0:T(8,128)(2,1)S(1)} %get-tuple-element.13.refs_1_, bf16[20,7,16,128]{3,2,1,0:T(8,128)(2,1)S(1)} %collective-permute-done.3.refs_2_, ...), custom_call_target="tpu_custom_call" | custom-call | flops 8999999488 | bytes 10168320 | tf_op jit(solution)/shard_map/spatial/pallas_call | solution.py:315
  76.7 9.6 %all-to-all-start.1 = ((bf16[128,5,2,128]{3,2,1,0:T(2,128)(2,1)}), bf16[128,5,2,128]{3,2,1,0:T(2,128)(2,1)S(1)}, u32[]{:S(2)}, u32[]{:S(2)}) async-start(bf16[128,5,2,128]{3,2,1,0:T(2,128)(2,1)} %get-tuple-element.14), calls=%async_computation.1 | async-start | bytes 655360 | tf_op jit(solution)/shard_map/all_to_all | solution.py:371
  86.3 0.1 collective-permute-start.20
  86.4 0.0 collective-permute-done.11.refs_2_
  86.4 4.1 %collective-permute-done.10.refs_1_ = bf16[32,7,16,128]{3,2,1,0:T(8,128)(2,1)S(1)} collective-permute-done((bf16[32,7,16,128]{3,2,1,0:T(8,128)(2,1)}, bf16[32,7,16,128]{3,2,1,0:T(8,128)(2,1)S(1)}, u32[]{:S(2)}, u32[]{:S(2)}) %collective-permute-start.10) | collective-permute-done | bytes 917536 | tf_op jit(solution)/shard_map/ppermute | solution.py:47
  90.5 1.1 collective-permute-done.9.refs_0_
  91.6 9.4 %all-to-all-done.1.refs_3_.refs_8_ = bf16[128,5,2,128]{3,2,1,0:T(2,128)(2,1)S(1)} async-done(((bf16[128,5,2,128]{3,2,1,0:T(2,128)(2,1)}), bf16[128,5,2,128]{3,2,1,0:T(2,128)(2,1)S(1)}, u32[]{:S(2)}, u32[]{:S(2)}) %all-to-all-start.1) | async-done | bytes 327712 | tf_op jit(solution)/shard_map/all_to_all | solution.py:371
  101.0 0.0 collective-permute-start.21
  101.0 0.5 collective-permute-start.22
  101.5 0.0 collective-permute-start.23
  101.5 0.0 collective-permute-done.20.refs_4_
  101.5 2.0 %collective-permute-done.21.refs_5_ = bf16[32,7,16,128]{3,2,1,0:T(8,128)(2,1)S(1)} collective-permute-done((bf16[32,7,16,128]{3,2,1,0:T(8,128)(2,1)S(1)}, bf16[32,7,16,128]{3,2,1,0:T(8,128)(2,1)S(1)}, u32[]{:S(2)}, u32[]{:S(2)}) %collective-permute-start.21) | collective-permute-done | bytes 917536 | tf_op jit(solution)/shard_map/ppermute | solution.py:63
  103.5 1.3 collective-permute-done.22.refs_6_
  104.8 1.3 collective-permute-done.23.refs_7_
  106.1 5.6 %temporal.1 = bf16[128,3,2,128]{3,2,1,0:T(2,128)(2,1)S(1)} custom-call(bf16[32,7,16,128]{3,2,1,0:T(8,128)(2,1)} %temporal_blocks.1.refs_0_, bf16[32,7,16,128]{3,2,1,0:T(8,128)(2,1)S(1)} %get-tuple-element.15.refs_1_, bf16[32,7,16,128]{3,2,1,0:T(8,128)(2,1)S(1)} %get-tuple-element.16.refs_2_, bf16[32,7,16,128]{3,2,1,0:T(8,128)(2,1)S(1)} %get-tuple-element.17.refs_3_, ...), custom_call_target="tpu_custom_call" | custom-call | flops 5000000000 | bytes 7864320 | tf_op jit(solution)/shard_map/temporal/pallas_call | solution.py:315
  111.7 19.7 %all_to_all.16.refs_8_ = bf16[128,3,2,128]{3,2,1,0:T(2,128)(2,1)S(1)} all-to-all(bf16[128,3,2,128]{3,2,1,0:T(2,128)(2,1)S(1)} %temporal.1), channel_id=1, replica_groups=mesh['clip'=2,'seq'=128] {'seq'}, dimensions={0} | all-to-all | bytes 393216 | tf_op jit(solution)/shard_map/all_to_all | solution.py:383
  131.5 3.8 %mixed.1 = bf16[128,1280]{1,0:T(8,128)(2,1)} custom-call(bf16[32,7,16,128]{3,2,1,0:T(8,128)(2,1)} %temporal_blocks.1.refs_0_, bf16[32,7,16,128]{3,2,1,0:T(8,128)(2,1)S(1)} %get-tuple-element.15.refs_1_, bf16[32,7,16,128]{3,2,1,0:T(8,128)(2,1)S(1)} %get-tuple-element.16.refs_2_, bf16[32,7,16,128]{3,2,1,0:T(8,128)(2,1)S(1)} %get-tuple-element.17.refs_3_, ...), custom_call_target="tpu_custom_call" | custom-call | flops 3000000000 | bytes 8192000 | tf_op jit(solution)/shard_map/mixed/pallas_call | solution.py:315
  (5 shorter events, 0.0 us)
Async XLA Ops:
  25.4 7.6 %collective-permute-start.2 = (bf16[8,7,16,128]{3,2,1,0:T(8,128)(2,1)S(1)}, bf16[8,7,16,128]{3,2,1,0:T(8,128)(2,1)S(1)}, u32[]{:S(2)}, u32[]{:S(2)}) collective-permute-start(bf16[8,7,16,128]{3,2,1,0:T(8,128)(2,1)S(1)} %slice.4), channel_id=1, source_target_pairs={{0,64},{1,65},{2,66},{3,67},{4,68},{5,69},{6,70},{7,71},{8,72},{9,... | collective-permute-start | bytes 688136 | tf_op jit(solution)/shard_map/ppermute | solution.py:47
  28.5 7.0 %collective-permute-start.1 = (bf16[8,7,16,128]{3,2,1,0:T(8,128)(2,1)S(1)}, bf16[8,7,16,128]{3,2,1,0:T(8,128)(2,1)S(1)}, u32[]{:S(2)}, u32[]{:S(2)}) collective-permute-start(bf16[8,7,16,128]{3,2,1,0:T(8,128)(2,1)S(1)} %slice.4), channel_id=1, source_target_pairs={{0,96},{1,97},{2,98},{3,99},{4,100},{5,101},{6,102},{7,103},{8,104... | collective-permute-start | bytes 688136 | tf_op jit(solution)/shard_map/ppermute | solution.py:47
  29.7 7.2 %collective-permute-start = (bf16[8,7,16,128]{3,2,1,0:T(8,128)(2,1)S(1)}, bf16[8,7,16,128]{3,2,1,0:T(8,128)(2,1)S(1)}, u32[]{:S(2)}, u32[]{:S(2)}) collective-permute-start(bf16[8,7,16,128]{3,2,1,0:T(8,128)(2,1)S(1)} %slice.4), channel_id=1, source_target_pairs={{0,32},{1,33},{2,34},{3,35},{4,36},{5,37},{6,38},{7,39},{8,40},{9,... | collective-permute-start | bytes 688136 | tf_op jit(solution)/shard_map/ppermute | solution.py:47
  36.9 27.6 %copy-start.1 = (f32[1280]{0:T(1024)S(1)}, f32[1280]{0:T(1024)}, u32[]{:S(2)}) copy-start(f32[1280]{0:T(1024)} %param.10) | copy-start | bytes 15364
  37.0 27.5 %copy-start.2 = (f32[1280]{0:T(1024)S(1)}, f32[1280]{0:T(1024)}, u32[]{:S(2)}) copy-start(f32[1280]{0:T(1024)} %param.13) | copy-start | bytes 15364
  37.0 6.4 %collective-permute-start.12 = (bf16[20,7,16,128]{3,2,1,0:T(8,128)(2,1)S(1)}, bf16[20,7,16,128]{3,2,1,0:T(8,128)(2,1)S(1)}, u32[]{:S(2)}, u32[]{:S(2)}) collective-permute-start(bf16[20,7,16,128]{3,2,1,0:T(8,128)(2,1)S(1)} %get-tuple-element.12.refs_0_), channel_id=1, source_target_pairs={{0,128},{1,129},{2,130},{3,131},{4,132},{5,133},{6,134},{7,135},{8... | collective-permute-start | bytes 1720328 | tf_op jit(solution)/shard_map/ppermute | solution.py:63
  37.1 10.3 %collective-permute-start.5 = (bf16[20,7,16,128]{3,2,1,0:T(8,128)(2,1)S(1)}, bf16[20,7,16,128]{3,2,1,0:T(8,128)(2,1)S(1)}, u32[]{:S(2)}, u32[]{:S(2)}) collective-permute-start(bf16[20,7,16,128]{3,2,1,0:T(8,128)(2,1)S(1)} %get-tuple-element.12.refs_0_), channel_id=1, source_target_pairs={{0,3},{1,0},{2,1},{3,2},{4,7},{5,4},{6,5},{7,6},{8,11},{9,8},{10,9... | collective-permute-start | bytes 1720328 | tf_op jit(solution)/shard_map/ppermute | solution.py:53
  40.2 10.9 %collective-permute-start.3 = (bf16[20,7,16,128]{3,2,1,0:T(8,128)(2,1)S(1)}, bf16[20,7,16,128]{3,2,1,0:T(8,128)(2,1)S(1)}, u32[]{:S(2)}, u32[]{:S(2)}) collective-permute-start(bf16[20,7,16,128]{3,2,1,0:T(8,128)(2,1)S(1)} %get-tuple-element.12.refs_0_), channel_id=1, source_target_pairs={{0,1},{1,2},{2,3},{3,0},{4,5},{5,6},{6,7},{7,4},{8,9},{9,10},{10,1... | collective-permute-start | bytes 1720328 | tf_op jit(solution)/shard_map/ppermute | solution.py:53
  40.2 13.4 %collective-permute-start.6 = (bf16[20,7,16,128]{3,2,1,0:T(8,128)(2,1)S(1)}, bf16[20,7,16,128]{3,2,1,0:T(8,128)(2,1)S(1)}, u32[]{:S(2)}, u32[]{:S(2)}) collective-permute-start(bf16[20,7,16,128]{3,2,1,0:T(8,128)(2,1)S(1)} %get-tuple-element.13.refs_1_), channel_id=1, source_target_pairs={{0,3},{1,0},{2,1},{3,2},{4,7},{5,4},{6,5},{7,6},{8,11},{9,8},{10,9... | collective-permute-start | bytes 1720328 | tf_op jit(solution)/shard_map/ppermute | solution.py:53
  43.4 13.8 %collective-permute-start.13 = (bf16[20,7,16,128]{3,2,1,0:T(8,128)(2,1)S(1)}, bf16[20,7,16,128]{3,2,1,0:T(8,128)(2,1)S(1)}, u32[]{:S(2)}, u32[]{:S(2)}) collective-permute-start(bf16[20,7,16,128]{3,2,1,0:T(8,128)(2,1)S(1)} %get-tuple-element.13.refs_1_), channel_id=1, source_target_pairs={{0,128},{1,129},{2,130},{3,131},{4,132},{5,133},{6,134},{7,135},{8... | collective-permute-start | bytes 1720328 | tf_op jit(solution)/shard_map/ppermute | solution.py:63
  43.4 13.8 %collective-permute-start.4 = (bf16[20,7,16,128]{3,2,1,0:T(8,128)(2,1)S(1)}, bf16[20,7,16,128]{3,2,1,0:T(8,128)(2,1)S(1)}, u32[]{:S(2)}, u32[]{:S(2)}) collective-permute-start(bf16[20,7,16,128]{3,2,1,0:T(8,128)(2,1)S(1)} %get-tuple-element.13.refs_1_), channel_id=1, source_target_pairs={{0,1},{1,2},{2,3},{3,0},{4,5},{5,6},{6,7},{7,4},{8,9},{9,10},{10,1... | collective-permute-start | bytes 1720328 | tf_op jit(solution)/shard_map/ppermute | solution.py:53
  47.4 10.4 %collective-permute-start.16 = (bf16[20,7,16,128]{3,2,1,0:T(8,128)(2,1)S(1)}, bf16[20,7,16,128]{3,2,1,0:T(8,128)(2,1)S(1)}, u32[]{:S(2)}, u32[]{:S(2)}) collective-permute-start(bf16[20,7,16,128]{3,2,1,0:T(8,128)(2,1)S(1)} %collective-permute-done.5.refs_4_), channel_id=1, source_target_pairs={{0,128},{1,129},{2,130},{3,131},{4,132},{5,133},{6,134},{7,135},{8... | collective-permute-start | bytes 1720328 | tf_op jit(solution)/shard_map/ppermute | solution.py:63
  51.1 12.3 %collective-permute-start.7 = (bf16[20,7,16,128]{3,2,1,0:T(8,128)(2,1)S(1)}, bf16[20,7,16,128]{3,2,1,0:T(8,128)(2,1)S(1)}, u32[]{:S(2)}, u32[]{:S(2)}) collective-permute-start(bf16[20,7,16,128]{3,2,1,0:T(8,128)(2,1)S(1)} %collective-permute-done.3.refs_2_), channel_id=1, source_target_pairs={{0,1},{1,2},{2,3},{3,0},{4,5},{5,6},{6,7},{7,4},{8,9},{9,10},{10,1... | collective-permute-start | bytes 1720328 | tf_op jit(solution)/shard_map/ppermute | solution.py:53
  53.6 10.9 %collective-permute-start.8 = (bf16[20,7,16,128]{3,2,1,0:T(8,128)(2,1)S(1)}, bf16[20,7,16,128]{3,2,1,0:T(8,128)(2,1)S(1)}, u32[]{:S(2)}, u32[]{:S(2)}) collective-permute-start(bf16[20,7,16,128]{3,2,1,0:T(8,128)(2,1)S(1)} %collective-permute-done.6.refs_5_), channel_id=1, source_target_pairs={{0,3},{1,0},{2,1},{3,2},{4,7},{5,4},{6,5},{7,6},{8,11},{9,8},{10,9... | collective-permute-start | bytes 1720328 | tf_op jit(solution)/shard_map/ppermute | solution.py:53
  57.3 8.3 %collective-permute-start.14 = (bf16[20,7,16,128]{3,2,1,0:T(8,128)(2,1)S(1)}, bf16[20,7,16,128]{3,2,1,0:T(8,128)(2,1)S(1)}, u32[]{:S(2)}, u32[]{:S(2)}) collective-permute-start(bf16[20,7,16,128]{3,2,1,0:T(8,128)(2,1)S(1)} %collective-permute-done.3.refs_2_), channel_id=1, source_target_pairs={{0,128},{1,129},{2,130},{3,131},{4,132},{5,133},{6,134},{7,135},{8... | collective-permute-start | bytes 1720328 | tf_op jit(solution)/shard_map/ppermute | solution.py:63
  57.3 9.9 %collective-permute-start.17 = (bf16[20,7,16,128]{3,2,1,0:T(8,128)(2,1)S(1)}, bf16[20,7,16,128]{3,2,1,0:T(8,128)(2,1)S(1)}, u32[]{:S(2)}, u32[]{:S(2)}) collective-permute-start(bf16[20,7,16,128]{3,2,1,0:T(8,128)(2,1)S(1)} %collective-permute-done.6.refs_5_), channel_id=1, source_target_pairs={{0,128},{1,129},{2,130},{3,131},{4,132},{5,133},{6,134},{7,135},{8... | collective-permute-start | bytes 1720328 | tf_op jit(solution)/shard_map/ppermute | solution.py:63
  57.8 10.5 %collective-permute-start.15 = (bf16[20,7,16,128]{3,2,1,0:T(8,128)(2,1)S(1)}, bf16[20,7,16,128]{3,2,1,0:T(8,128)(2,1)S(1)}, u32[]{:S(2)}, u32[]{:S(2)}) collective-permute-start(bf16[20,7,16,128]{3,2,1,0:T(8,128)(2,1)S(1)} %collective-permute-done.4.refs_3_), channel_id=1, source_target_pairs={{0,128},{1,129},{2,130},{3,131},{4,132},{5,133},{6,134},{7,135},{8... | collective-permute-start | bytes 1720328 | tf_op jit(solution)/shard_map/ppermute | solution.py:63
  63.4 5.8 %collective-permute-start.18 = (bf16[20,7,16,128]{3,2,1,0:T(8,128)(2,1)S(1)}, bf16[20,7,16,128]{3,2,1,0:T(8,128)(2,1)S(1)}, u32[]{:S(2)}, u32[]{:S(2)}) collective-permute-start(bf16[20,7,16,128]{3,2,1,0:T(8,128)(2,1)S(1)} %collective-permute-done.7.refs_6_), channel_id=1, source_target_pairs={{0,128},{1,129},{2,130},{3,131},{4,132},{5,133},{6,134},{7,135},{8... | collective-permute-start | bytes 1720328 | tf_op jit(solution)/shard_map/ppermute | solution.py:63
  64.5 4.7 %collective-permute-start.19 = (bf16[20,7,16,128]{3,2,1,0:T(8,128)(2,1)S(1)}, bf16[20,7,16,128]{3,2,1,0:T(8,128)(2,1)S(1)}, u32[]{:S(2)}, u32[]{:S(2)}) collective-permute-start(bf16[20,7,16,128]{3,2,1,0:T(8,128)(2,1)S(1)} %collective-permute-done.8.refs_7_), channel_id=1, source_target_pairs={{0,128},{1,129},{2,130},{3,131},{4,132},{5,133},{6,134},{7,135},{8... | collective-permute-start | bytes 1720328 | tf_op jit(solution)/shard_map/ppermute | solution.py:63
  64.5 4.7 %copy-start = (bf16[1,128,1280]{2,1,0:T(8,128)(2,1)S(1)}, bf16[1,128,1280]{2,1,0:T(8,128)(2,1)}, u32[]{:S(2)}) copy-start(bf16[1,128,1280]{2,1,0:T(8,128)(2,1)} %param.8) | copy-start | bytes 983044
  65.5 20.8 %collective-permute-start.11 = (bf16[32,7,16,128]{3,2,1,0:T(8,128)(2,1)}, bf16[32,7,16,128]{3,2,1,0:T(8,128)(2,1)S(1)}, u32[]{:S(2)}, u32[]{:S(2)}) collective-permute-start(bf16[32,7,16,128]{3,2,1,0:T(8,128)(2,1)} %temporal_blocks.1.refs_0_), channel_id=1, source_target_pairs={{0,64},{1,65},{2,66},{3,67},{4,68},{5,69},{6,70},{7,71},{8,72},{9,... | collective-permute-start | bytes 2752520 | tf_op jit(solution)/shard_map/ppermute | solution.py:47
  67.2 23.4 %collective-permute-start.10 = (bf16[32,7,16,128]{3,2,1,0:T(8,128)(2,1)}, bf16[32,7,16,128]{3,2,1,0:T(8,128)(2,1)S(1)}, u32[]{:S(2)}, u32[]{:S(2)}) collective-permute-start(bf16[32,7,16,128]{3,2,1,0:T(8,128)(2,1)} %temporal_blocks.1.refs_0_), channel_id=1, source_target_pairs={{0,96},{1,97},{2,98},{3,99},{4,100},{5,101},{6,102},{7,103},{8,104... | collective-permute-start | bytes 2752520 | tf_op jit(solution)/shard_map/ppermute | solution.py:47
  68.3 23.2 %collective-permute-start.9 = (bf16[32,7,16,128]{3,2,1,0:T(8,128)(2,1)}, bf16[32,7,16,128]{3,2,1,0:T(8,128)(2,1)S(1)}, u32[]{:S(2)}, u32[]{:S(2)}) collective-permute-start(bf16[32,7,16,128]{3,2,1,0:T(8,128)(2,1)} %temporal_blocks.1.refs_0_), channel_id=1, source_target_pairs={{0,32},{1,33},{2,34},{3,35},{4,36},{5,37},{6,38},{7,39},{8,40},{9,... | collective-permute-start | bytes 2752520 | tf_op jit(solution)/shard_map/ppermute | solution.py:47
  76.7 24.3 %all-to-all-start.1 = ((bf16[128,5,2,128]{3,2,1,0:T(2,128)(2,1)}), bf16[128,5,2,128]{3,2,1,0:T(2,128)(2,1)S(1)}, u32[]{:S(2)}, u32[]{:S(2)}) async-start(bf16[128,5,2,128]{3,2,1,0:T(2,128)(2,1)} %get-tuple-element.14), calls=%async_computation.1 | async-start | bytes 655360 | tf_op jit(solution)/shard_map/all_to_all | solution.py:371
  86.3 15.2 %collective-permute-start.20 = (bf16[32,7,16,128]{3,2,1,0:T(8,128)(2,1)}, bf16[32,7,16,128]{3,2,1,0:T(8,128)(2,1)}, u32[]{:S(2)}, u32[]{:S(2)}) collective-permute-start(bf16[32,7,16,128]{3,2,1,0:T(8,128)(2,1)} %temporal_blocks.1.refs_0_), channel_id=1, source_target_pairs={{0,128},{1,129},{2,130},{3,131},{4,132},{5,133},{6,134},{7,135},{8... | collective-permute-start | bytes 2752520 | tf_op jit(solution)/shard_map/ppermute | solution.py:63
  101.0 2.5 %collective-permute-start.21 = (bf16[32,7,16,128]{3,2,1,0:T(8,128)(2,1)S(1)}, bf16[32,7,16,128]{3,2,1,0:T(8,128)(2,1)S(1)}, u32[]{:S(2)}, u32[]{:S(2)}) collective-permute-start(bf16[32,7,16,128]{3,2,1,0:T(8,128)(2,1)S(1)} %get-tuple-element.15.refs_1_), channel_id=1, source_target_pairs={{0,128},{1,129},{2,130},{3,131},{4,132},{5,133},{6,134},{7,135},{8... | collective-permute-start | bytes 2752520 | tf_op jit(solution)/shard_map/ppermute | solution.py:63
  101.0 3.8 %collective-permute-start.22 = (bf16[32,7,16,128]{3,2,1,0:T(8,128)(2,1)S(1)}, bf16[32,7,16,128]{3,2,1,0:T(8,128)(2,1)S(1)}, u32[]{:S(2)}, u32[]{:S(2)}) collective-permute-start(bf16[32,7,16,128]{3,2,1,0:T(8,128)(2,1)S(1)} %get-tuple-element.16.refs_2_), channel_id=1, source_target_pairs={{0,128},{1,129},{2,130},{3,131},{4,132},{5,133},{6,134},{7,135},{8... | collective-permute-start | bytes 2752520 | tf_op jit(solution)/shard_map/ppermute | solution.py:63
  101.5 4.6 %collective-permute-start.23 = (bf16[32,7,16,128]{3,2,1,0:T(8,128)(2,1)S(1)}, bf16[32,7,16,128]{3,2,1,0:T(8,128)(2,1)S(1)}, u32[]{:S(2)}, u32[]{:S(2)}) collective-permute-start(bf16[32,7,16,128]{3,2,1,0:T(8,128)(2,1)S(1)} %get-tuple-element.17.refs_3_), channel_id=1, source_target_pairs={{0,128},{1,129},{2,130},{3,131},{4,132},{5,133},{6,134},{7,135},{8... | collective-permute-start | bytes 2752520 | tf_op jit(solution)/shard_map/ppermute | solution.py:63

commit v3 on v2

--- a/solution.py
+++ b/solution.py
@@ -102,13 +102,17 @@
 
     def fill(half):
         refs = [lane(ref, u) for u in range(10)]
+        def put(at, value):
+            for z in range(NZ):
+                out[z, at] = value
+
         for t in range(5):
-            out[t] = tile(lane(ws, 5 * half + t), refs[t])
-            out[GROUP + t] = tile(lane(wt, 5 * half + t))
+            put(t, tile(lane(ws, 5 * half + t), refs[t]))
+            put(GROUP + t, tile(lane(wt, 5 * half + t)))
         for at, w, extra in ((5, wo, refs[5:]), (GROUP + 5, wu, [])):
             middle = lane(w, 2).astype(F32)[5 * half : 5 * half + 5]
-            out[at] = tile(lane(w, 3 * half), middle)
-            out[at + 1] = tile(lane(w, 3 * half + 1), *extra)
+            put(at, tile(lane(w, 3 * half), middle))
+            put(at + 1, tile(lane(w, 3 * half + 1), *extra))
 
     for half in range(2):
         pl.when(c == half)(functools.partial(fill, half))
@@ -141,7 +145,7 @@
             in_specs=vmem(n + 1),
             out_specs=vmem(n),
             input_output_aliases={i: i for i in range(n)},
-            compiler_params=small(1),
+            compiler_params=small(4),
             name="gate",
         )(*values, after)
     )
@@ -150,10 +154,10 @@
 def reorder(kernel, args, outs, name):
     return pl.pallas_call(
         kernel,
-        out_shape=[jax.ShapeDtypeStruct((n, GROUP, 16, 128), BF) for n in outs],
+        out_shape=[jax.ShapeDtypeStruct(n + (16, 128), BF) for n in outs],
         in_specs=vmem(len(args)),
         out_specs=vmem(len(outs)),
-        compiler_params=small(4),
+        compiler_params=small(8),
         name=name,
     )(*args)
 
@@ -180,9 +184,9 @@
 
 
 def blocks(refs, j, i):
-    per_shift = len(refs) // 4
-    at = 4 // per_shift
-    return refs[per_shift * j + i // at], 8 * (i % at)
+    each = 16 // len(refs)
+    at = 4 * j + i
+    return refs[at // each], 8 * (at % each)
 
 
 def lanes(refs, j, i, first, count):
@@ -217,15 +221,19 @@
     return lax.dot_general(a, b, dims, preferred_element_type=F32)
 
 
+def compact(acc, rows):
+    for s in range(SEQ):
+        x, z, y = s // 32, (s // 4) % 8, s % 4
+        rows[15 * s : 15 * s + 15, :] = acc[x, z, y, 0:15, :]
+
+
 def qkv_project(own, oth, acc, rows, tokens, x_core):
     c, _, _ = place()
     xa, xb = halves(tokens, c)
     for j in range(4):
         wa, wb = pieces_of(own, oth, j, 0, 5)
         spread(acc, dot(wa, xa, NT) + dot(wb, xb, NT), j, 0, x_core)
-    for s in range(SEQ):
-        x, z, y = s // 32, (s // 4) % 8, s % 4
-        rows[15 * s : 15 * s + 15, :] = acc[x, z, y, 0:15, :]
+    compact(acc, rows)
 
 
 def out_project(own, oth, acc, rows, part, dims, x_core):
@@ -292,24 +300,56 @@
     to_rows(layer_norm(h.astype(F32), gain_t[...]).astype(F32), tnormed, rows_out, 10)
 
 
+def half_kernel(*refs):
+    own, (tokens, out, for_out, wide) = refs[0:4], refs[4:]
+    c, _, _ = place()
+    xa, _ = halves(from_rows(tokens, wide, 10), c)
+    for j in range(4):
+        wa = jnp.concatenate([lanes(own, j, i, 0, 5) for i in range(4)], axis=0)
+        out[512 * j : 512 * (j + 1), :] = dot(wa, xa, NT)
+        for_out[32 * j : 32 * (j + 1)] = own[j][:, 5:7]
+
+
 def temporal_kernel(*refs):
-    own, oth = refs[0:4], refs[4:8]
-    tokens, out, acc, rows, attn, wide, wide_out = refs[8:]
-    qkv_project(own, oth, acc, rows, from_rows(tokens, wide, 10), 1)
+    oth = refs[0:4]
+    half, tokens, out, for_out, acc, rows, attn, wide, wide_out = refs[4:]
+    c, _, _ = place()
+    _, xb = halves(from_rows(tokens, wide, 10), c)
+    for j in range(4):
+        wb = jnp.concatenate([lanes(oth, i, j, 0, 5) for i in range(4)], axis=0)
+        spread(acc, half[512 * j : 512 * (j + 1), :] + dot(wb, xb, NT), j, 0, 1)
+        for_out[32 * j : 32 * (j + 1)] = oth[j][:, 5:7]
+    compact(acc, rows)
     heads(rows, 128, attn)
     to_rows(attn[...].T, out, wide_out, 5)
 
 
-def mixed_kernel(*refs):
-    own, oth = refs[0:4], refs[4:8]
-    attn, hidden, mixed, acc, rows, wide = refs[8:]
+def weights_kernel(*refs):
+    own, oth, out, acc, rows = refs
+    c, _, _ = place()
+    for j in range(4):
+        wa, wb = pieces_of([own], [oth], j, 0, 2)
+        lo = jnp.where(c == 0, wa, wb).astype(F32)
+        hi = jnp.where(c == 0, wb, wa).astype(F32)
+        spread(acc, jnp.concatenate([lo, hi], axis=1), j, 0, 1)
+    for s in range(SEQ):
+        x, z, y = s // 32, (s // 4) % 8, s % 4
+        at = slice(10 * s, 10 * s + 10)
+        rows[at, 0:256] = acc[x, z, y, 0:10, 0:256]
+        rows[at, 384:640] = acc[x, z, y, 0:10, 256:512]
+        rows[at, 256:384] = jnp.concatenate(
+            [acc[x, z, y, 10:15, 0:128], acc[x, z, y, 10:15, 256:384]], axis=0
+        )
+    out[...] = rows[...].astype(BF)
+
+
+def mixed_kernel(weights, attn, hidden, mixed, wide):
     a = from_rows(attn, wide, 5)
-    out_project(own, oth, acc, rows, lambda first, last: a[:, first:last], NT, 1)
-    mixed[...] = (hidden[...].astype(F32) + rows[...].T).astype(BF)
-
-
-def call(kernel, args, outs, scratch, name, flops, mib):
-    shapes = [jax.ShapeDtypeStruct(s, BF) for s in outs]
+    mixed[...] = (hidden[...].astype(F32) + dot(a, weights[...], NT)).astype(BF)
+
+
+def call(kernel, args, outs, scratch, name, flops, mib, dtypes=(BF, BF)):
+    shapes = [jax.ShapeDtypeStruct(s, d) for s, d in zip(outs, dtypes)]
     single = len(shapes) == 1
     size = sum(a.size * a.dtype.itemsize for a in args) + sum(2 * s.size for s in shapes)
     return pl.pallas_call(
@@ -331,7 +371,7 @@
     shards = [w_s.T, ref_hidden, w_o.T, w_t.T, w_u.T]
     packed = pl.pallas_call(
         pack_kernel,
-        out_shape=jax.ShapeDtypeStruct((TILES, 16, 128), BF),
+        out_shape=jax.ShapeDtypeStruct((NZ, TILES, 16, 128), BF),
         in_specs=[ANY] * 5,
         out_specs=vmem(1)[0],
         scratch_shapes=[pltpu.VMEM(a.shape, BF) for a in shards] + [pltpu.SemaphoreType.DMA((5,))],
@@ -339,7 +379,7 @@
         name="pack",
     )(*shards)
     along_z = lax.all_to_all(
-        jnp.broadcast_to(packed[None], (NZ, TILES, 16, 128)),
+        packed,
         "seq",
         0,
         0,
@@ -347,9 +387,9 @@
         tiled=True,
     )
     first = ring(along_z[:, :GROUP], 0)
-    own_s = ring_by_halves(reorder(halves_kernel, [along_z] + first[1:], [20, 20], "halves"), 1)
+    own_s = ring_by_halves(reorder(halves_kernel, [along_z] + first[1:], [(20, GROUP)] * 2, "halves"), 1)
     oth_s = [swap(b) for b in own_s]
-    (part_t,) = reorder(temporal_blocks_kernel, own_s, [32], "temporal_blocks")
+    (part_t,) = reorder(temporal_blocks_kernel, own_s, [(32, GROUP)], "temporal_blocks")
     ring_t = ring(part_t, 0)
 
     hidden, tnormed = call(
@@ -366,29 +406,48 @@
         ],
         "spatial",
         9 * 10**9,
-        24,
+        32,
     )
     tokens = lax.all_to_all(tnormed, "seq", 0, 0, tiled=True)
     own_t = ring_t[:1] + gate(ring_t[1:], tokens)
     oth_t = [swap(ring_t[0])] + [swap(b) for b in own_t[1:]]
-    tattn = call(
+    half_t, own_u = call(
+        half_kernel,
+        own_t + [tokens],
+        [(2048, 128), (SEQ, 2, 16, 128)],
+        [(D, 128)],
+        "half",
+        3 * 10**9,
+        16,
+        [F32, BF],
+    )
+    tattn, oth_u = call(
         temporal_kernel,
-        own_t + oth_t + [tokens],
-        [(PIX, 3, 2, 128)],
+        oth_t + [half_t, tokens],
+        [(PIX, 3, 2, 128), (SEQ, 2, 16, 128)],
         [(NX, NZ, NY, 16, 128), (1920, 128), (INNER, 128), (D, 128), (768, 128)],
         "temporal",
         5 * 10**9,
         16,
     )
+    weights_u = call(
+        weights_kernel,
+        [own_u, oth_u],
+        [(D, INNER)],
+        [(NX, NZ, NY, 16, 512), (D, INNER)],
+        "weights",
+        3 * 10**9,
+        16,
+    )
     back = lax.all_to_all(tattn, "seq", 0, 0, tiled=True)
     mixed = call(
         mixed_kernel,
-        own_t + oth_t + [back, hidden],
+        [weights_u, back, hidden],
         [(PIX, D)],
-        [(NX, NZ, NY, 48, 128), (D, 128), (768, 128)],
+        [(768, 128)],
         "mixed",
-        3 * 10**9,
-        16,
+        10**9,
+        8,
     )
     return mixed.reshape(1, PIX, D)
 

time: 136 us -> 133 us (0.978)
  blocking collectives: 42.7 us -> 23.2 us
  starting transfers between devices: 29.7 us -> 36.8 us
  waiting for transfers between devices: 42.3 us -> 48.4 us
  local copies, waits for them, and re-layouts: 0.92 us -> 3.21 us
    all_to_all x2 -> x1, blocking collectives: 42.7 us -> 23.2 us  [body(): lax.all_to_all(packed, 'seq', 0, 0, axis_index_groups=Z_GROUPS, tiled=True)]
    all_to_all x0 -> x1, waiting for transfers between devices: none -> 11.1 us  [body(): back = lax.all_to_all(tattn, 'seq', 0, 0, tiled=True)]
    all_to_all x0 -> x1, starting transfers between devices: none -> 6.68 us  [body(): back = lax.all_to_all(tattn, 'seq', 0, 0, tiled=True)]
    all_to_all x1, waiting for transfers between devices: 9.41 us -> 5.16 us  [body(): tokens = lax.all_to_all(tnormed, 'seq', 0, 0, tiled=True)]
    ppermute x12, waiting for transfers between devices: 4.6 us -> 1.27 us  [swap(): return lax.ppermute(block, ('clip', 'seq'), SWAP)]
    unnamed x6 -> x14, local copies, waits for them, and re-layouts: 0.02 us -> 3.18 us
    ppermute x6, waiting for transfers between devices: 11.5 us -> 14.7 us  [ring(): lax.ppermute(block, ('clip', 'seq'), ring_perm(k, stage))]
    pallas_call x3 -> x5, Pallas kernels: 16.9 us -> 17.8 us  [call(): pl.pallas_call(kernel, out_shape=shapes[0] if single else shapes, in_spec...]
  transfers between devices with their start and end apart: 25 -> 26, of which waited for: 14 -> 13; matrix products, arithmetic and copies ran while one was open for 0% -> 0% of each run, Pallas kernels for 6% -> 9%
where the time goes in v3:
time: 133 us; the launch traced here: 132 us
  waiting for transfers between devices  48.4 us (36%)
  starting transfers between devices  36.8 us (28%)
  blocking collectives  23.2 us (17%)
  Pallas kernels  20.5 us (15%)
  local copies, waits for them, and re-layouts  3.21 us (2%)
    all_to_all x1, blocking collectives, body(): lax.all_to_all(packed, 'seq', 0, 0, axis_index_groups=Z_GROUPS, tiled=True)  23.2 us
    pallas_call x5, Pallas kernels, call(): pl.pallas_call(kernel, out_shape=shapes[0] if single else shapes, in_spec...  17.8 us
    ppermute x6, waiting for transfers between devices, shift(): return lax.ppermute(part, ('clip', 'seq'), ring_perm(k, stage))  16.2 us
    ppermute x6, waiting for transfers between devices, ring(): lax.ppermute(block, ('clip', 'seq'), ring_perm(k, stage))  14.7 us
    all_to_all x1, waiting for transfers between devices, body(): back = lax.all_to_all(tattn, 'seq', 0, 0, tiled=True)  11.1 us
    ppermute x6, starting transfers between devices, shift(): return lax.ppermute(part, ('clip', 'seq'), ring_perm(k, stage))  10 us
    all_to_all x1, starting transfers between devices, body(): tokens = lax.all_to_all(tnormed, 'seq', 0, 0, tiled=True)  9.72 us
    ppermute x6, starting transfers between devices, ring(): lax.ppermute(block, ('clip', 'seq'), ring_perm(k, stage))  8.6 us
  transfers between devices with their start and end apart: 26, of which 13 were waited for; matrix products, arithmetic and copies ran while one was open for 0% of the time, Pallas kernels for 9%

profile of v3, /device:TPU:32, one launch (start us, length us, event | category | flops | bytes accessed | tf_op | source)
XLA Modules:
  0.0 132.3 jit_solution(4417903923718045790)
XLA Ops:
  0.0 1.7 %pack.1 = bf16[8,14,16,128]{3,2,1,0:T(8,128)(2,1)} custom-call(bf16[15,1280]{1,0:T(8,128)(2,1)} %bitcast.7, bf16[1,1280]{1,0:T(2,128)(2,1)} %ref_in.1, bf16[10,640]{1,0:T(8,128)(2,1)} %bitcast.9, bf16[15,1280]{1,0:T(8,128)(2,1)} %bitcast.8, bf16[10,640]{1,0:T(8,128)(2,1)} %bitcast.10), custom_call_target="tpu_custom_call" | custom-call | tf_op jit(solution)/shard_map/pack/pallas_call | solution.py:372
  1.7 23.2 %all_to_all.15.along_z = bf16[8,14,16,128]{3,2,1,0:T(8,128)(2,1)S(1)} all-to-all(bf16[8,14,16,128]{3,2,1,0:T(8,128)(2,1)} %pack.1), channel_id=1, replica_groups={{0,4,8,12,16,20,24,28},{1,5,9,13,17,21,25,29},{2,6,10,14,18,22,26,30},{..., dimensions={0} | all-to-all | bytes 917504 | tf_op jit(solution)/shard_map/all_to_all | solution.py:381
  24.9 1.6 %collective-permute-start = (bf16[8,7,16,128]{3,2,1,0:T(8,128)(2,1)S(1)}, bf16[8,7,16,128]{3,2,1,0:T(8,128)(2,1)S(1)}, u32[]{:S(2)}, u32[]{:S(2)}) collective-permute-start(bf16[8,7,16,128]{3,2,1,0:T(8,128)(2,1)S(1)} %slice.4), channel_id=1, source_target_pairs={{0,32},{1,33},{2,34},{3,35},{4,36},{5,37},{6,38},{7,39},{8,40},{9,... | collective-permute-start | bytes 688136 | tf_op jit(solution)/shard_map/ppermute | solution.py:47
  26.5 1.7 %collective-permute-start.1 = (bf16[8,7,16,128]{3,2,1,0:T(8,128)(2,1)S(1)}, bf16[8,7,16,128]{3,2,1,0:T(8,128)(2,1)S(1)}, u32[]{:S(2)}, u32[]{:S(2)}) collective-permute-start(bf16[8,7,16,128]{3,2,1,0:T(8,128)(2,1)S(1)} %slice.4), channel_id=1, source_target_pairs={{0,96},{1,97},{2,98},{3,99},{4,100},{5,101},{6,102},{7,103},{8,104... | collective-permute-start | bytes 688136 | tf_op jit(solution)/shard_map/ppermute | solution.py:47
  28.3 1.8 %collective-permute-start.2 = (bf16[8,7,16,128]{3,2,1,0:T(8,128)(2,1)S(1)}, bf16[8,7,16,128]{3,2,1,0:T(8,128)(2,1)S(1)}, u32[]{:S(2)}, u32[]{:S(2)}) collective-permute-start(bf16[8,7,16,128]{3,2,1,0:T(8,128)(2,1)S(1)} %slice.4), channel_id=1, source_target_pairs={{0,64},{1,65},{2,66},{3,67},{4,68},{5,69},{6,70},{7,71},{8,72},{9,... | collective-permute-start | bytes 688136 | tf_op jit(solution)/shard_map/ppermute | solution.py:47
  30.1 2.2 %collective-permute-done.p1 = bf16[8,7,16,128]{3,2,1,0:T(8,128)(2,1)S(1)} collective-permute-done((bf16[8,7,16,128]{3,2,1,0:T(8,128)(2,1)S(1)}, bf16[8,7,16,128]{3,2,1,0:T(8,128)(2,1)S(1)}, u32[]{:S(2)}, u32[]{:S(2)}) %collective-permute-start) | collective-permute-done | bytes 229408 | tf_op jit(solution)/shard_map/ppermute | solution.py:47
  32.2 2.0 %collective-permute-done.1.p2 = bf16[8,7,16,128]{3,2,1,0:T(8,128)(2,1)S(1)} collective-permute-done((bf16[8,7,16,128]{3,2,1,0:T(8,128)(2,1)S(1)}, bf16[8,7,16,128]{3,2,1,0:T(8,128)(2,1)S(1)}, u32[]{:S(2)}, u32[]{:S(2)}) %collective-permute-start.1) | collective-permute-done | bytes 229408 | tf_op jit(solution)/shard_map/ppermute | solution.py:47
  34.3 1.5 %collective-permute-done.2.p3 = bf16[8,7,16,128]{3,2,1,0:T(8,128)(2,1)S(1)} collective-permute-done((bf16[8,7,16,128]{3,2,1,0:T(8,128)(2,1)S(1)}, bf16[8,7,16,128]{3,2,1,0:T(8,128)(2,1)S(1)}, u32[]{:S(2)}, u32[]{:S(2)}) %collective-permute-start.2) | collective-permute-done | bytes 229408 | tf_op jit(solution)/shard_map/ppermute | solution.py:47
  35.8 0.1 halves.1
  35.9 1.7 %collective-permute-start.3 = (bf16[20,7,16,128]{3,2,1,0:T(8,128)(2,1)S(1)}, bf16[20,7,16,128]{3,2,1,0:T(8,128)(2,1)S(1)}, u32[]{:S(2)}, u32[]{:S(2)}) collective-permute-start(bf16[20,7,16,128]{3,2,1,0:T(8,128)(2,1)S(1)} %get-tuple-element.16.refs_0_), channel_id=1, source_target_pairs={{0,1},{1,2},{2,3},{3,0},{4,5},{5,6},{6,7},{7,4},{8,9},{9,10},{10,1... | collective-permute-start | bytes 1720328 | tf_op jit(solution)/shard_map/ppermute | solution.py:53
  37.5 1.7 %collective-permute-start.6 = (bf16[20,7,16,128]{3,2,1,0:T(8,128)(2,1)S(1)}, bf16[20,7,16,128]{3,2,1,0:T(8,128)(2,1)S(1)}, u32[]{:S(2)}, u32[]{:S(2)}) collective-permute-start(bf16[20,7,16,128]{3,2,1,0:T(8,128)(2,1)S(1)} %get-tuple-element.17.refs_1_), channel_id=1, source_target_pairs={{0,3},{1,0},{2,1},{3,2},{4,7},{5,4},{6,5},{7,6},{8,11},{9,8},{10,9... | collective-permute-start | bytes 1720328 | tf_op jit(solution)/shard_map/ppermute | solution.py:53
  39.2 0.4 collective-permute-start.4
  39.5 2.9 %collective-permute-start.5 = (bf16[20,7,16,128]{3,2,1,0:T(8,128)(2,1)S(1)}, bf16[20,7,16,128]{3,2,1,0:T(8,128)(2,1)S(1)}, u32[]{:S(2)}, u32[]{:S(2)}) collective-permute-start(bf16[20,7,16,128]{3,2,1,0:T(8,128)(2,1)S(1)} %get-tuple-element.16.refs_0_), channel_id=1, source_target_pairs={{0,3},{1,0},{2,1},{3,2},{4,7},{5,4},{6,5},{7,6},{8,11},{9,8},{10,9... | collective-permute-start | bytes 1720328 | tf_op jit(solution)/shard_map/ppermute | solution.py:53
  42.4 0.0 collective-permute-start.12
  42.4 4.4 %collective-permute-done.3.refs_2_ = bf16[20,7,16,128]{3,2,1,0:T(8,128)(2,1)S(1)} collective-permute-done((bf16[20,7,16,128]{3,2,1,0:T(8,128)(2,1)S(1)}, bf16[20,7,16,128]{3,2,1,0:T(8,128)(2,1)S(1)}, u32[]{:S(2)}, u32[]{:S(2)}) %collective-permute-start.3) | collective-permute-done | bytes 573472 | tf_op jit(solution)/shard_map/ppermute | solution.py:53
  46.9 0.0 collective-permute-start.13
  46.9 0.4 collective-permute-done.6.refs_5_
  47.2 1.7 %collective-permute-start.7 = (bf16[20,7,16,128]{3,2,1,0:T(8,128)(2,1)S(1)}, bf16[20,7,16,128]{3,2,1,0:T(8,128)(2,1)S(1)}, u32[]{:S(2)}, u32[]{:S(2)}) collective-permute-start(bf16[20,7,16,128]{3,2,1,0:T(8,128)(2,1)S(1)} %collective-permute-done.3.refs_2_), channel_id=1, source_target_pairs={{0,1},{1,2},{2,3},{3,0},{4,5},{5,6},{6,7},{7,4},{8,9},{9,10},{10,1... | collective-permute-start | bytes 1720328 | tf_op jit(solution)/shard_map/ppermute | solution.py:53
  48.9 4.1 %collective-permute-done.4.refs_3_ = bf16[20,7,16,128]{3,2,1,0:T(8,128)(2,1)S(1)} collective-permute-done((bf16[20,7,16,128]{3,2,1,0:T(8,128)(2,1)S(1)}, bf16[20,7,16,128]{3,2,1,0:T(8,128)(2,1)S(1)}, u32[]{:S(2)}, u32[]{:S(2)}) %collective-permute-start.4) | collective-permute-done | bytes 573472 | tf_op jit(solution)/shard_map/ppermute | solution.py:53
  53.0 1.8 %collective-permute-start.8 = (bf16[20,7,16,128]{3,2,1,0:T(8,128)(2,1)S(1)}, bf16[20,7,16,128]{3,2,1,0:T(8,128)(2,1)S(1)}, u32[]{:S(2)}, u32[]{:S(2)}) collective-permute-start(bf16[20,7,16,128]{3,2,1,0:T(8,128)(2,1)S(1)} %collective-permute-done.6.refs_5_), channel_id=1, source_target_pairs={{0,3},{1,0},{2,1},{3,2},{4,7},{5,4},{6,5},{7,6},{8,11},{9,8},{10,9... | collective-permute-start | bytes 1720328 | tf_op jit(solution)/shard_map/ppermute | solution.py:53
  54.8 0.0 collective-permute-done.5.refs_4_
  54.8 0.0 collective-permute-start.14
  54.8 0.0 collective-permute-done.12.refs_8_
  54.8 0.5 collective-permute-start.17
  55.3 0.0 collective-permute-done.13.refs_9_
  55.3 0.1 collective-permute-start.15
  55.4 3.7 %collective-permute-done.7.refs_6_ = bf16[20,7,16,128]{3,2,1,0:T(8,128)(2,1)S(1)} collective-permute-done((bf16[20,7,16,128]{3,2,1,0:T(8,128)(2,1)S(1)}, bf16[20,7,16,128]{3,2,1,0:T(8,128)(2,1)S(1)}, u32[]{:S(2)}, u32[]{:S(2)}) %collective-permute-start.7) | collective-permute-done | bytes 573472 | tf_op jit(solution)/shard_map/ppermute | solution.py:53
  59.1 0.0 collective-permute-start.16
  59.1 3.6 %collective-permute-done.8.refs_7_ = bf16[20,7,16,128]{3,2,1,0:T(8,128)(2,1)S(1)} collective-permute-done((bf16[20,7,16,128]{3,2,1,0:T(8,128)(2,1)S(1)}, bf16[20,7,16,128]{3,2,1,0:T(8,128)(2,1)S(1)}, u32[]{:S(2)}, u32[]{:S(2)}) %collective-permute-start.8) | collective-permute-done | bytes 573472 | tf_op jit(solution)/shard_map/ppermute | solution.py:53
  62.7 0.0 collective-permute-start.18
  62.7 0.0 collective-permute-done.14.refs_10_
  62.7 0.5 collective-permute-start.19
  63.2 0.0 copy-start
  63.3 1.0 temporal_blocks.1.refs_0_
  64.2 0.0 collective-permute-done.17.refs_13_
  64.3 2.2 %collective-permute-start.10 = (bf16[32,7,16,128]{3,2,1,0:T(8,128)(2,1)}, bf16[32,7,16,128]{3,2,1,0:T(8,128)(2,1)S(1)}, u32[]{:S(2)}, u32[]{:S(2)}) collective-permute-start(bf16[32,7,16,128]{3,2,1,0:T(8,128)(2,1)} %temporal_blocks.1.refs_0_), channel_id=1, source_target_pairs={{0,96},{1,97},{2,98},{3,99},{4,100},{5,101},{6,102},{7,103},{8,104... | collective-permute-start | bytes 2752520 | tf_op jit(solution)/shard_map/ppermute | solution.py:47
  66.4 0.0 collective-permute-done.15.refs_11_
  66.4 1.2 collective-permute-start.11
  67.7 0.0 collective-permute-done.16.refs_12_
  67.7 0.1 collective-permute-start.9
  67.7 0.0 collective-permute-done.18.refs_14_
  67.7 7.5 %spatial.1 = (bf16[128,1280]{1,0:T(8,128)(2,1)S(1)}, bf16[128,5,2,128]{3,2,1,0:T(2,128)(2,1)}) custom-call(bf16[20,7,16,128]{3,2,1,0:T(8,128)(2,1)S(1)} %get-tuple-element.16.refs_0_, bf16[20,7,16,128]{3,2,1,0:T(8,128)(2,1)S(1)} %get-tuple-element.17.refs_1_, bf16[20,7,16,128]{3,2,1,0:T(8,128)(2,1)S(1)} %collective-permute-done.3.refs_2_, ...), custom_call_target="tpu_custom_call" | custom-call | flops 8999999488 | bytes 10168320 | tf_op jit(solution)/shard_map/spatial/pallas_call | solution.py:355
  75.2 9.7 %all-to-all-start.1 = ((bf16[128,5,2,128]{3,2,1,0:T(2,128)(2,1)}), bf16[128,5,2,128]{3,2,1,0:T(2,128)(2,1)S(1)}, u32[]{:S(2)}, u32[]{:S(2)}) async-start(bf16[128,5,2,128]{3,2,1,0:T(2,128)(2,1)} %get-tuple-element.18), calls=%async_computation.1 | async-start | bytes 655360 | tf_op jit(solution)/shard_map/all_to_all | solution.py:411
  85.0 0.1 collective-permute-start.20
  85.1 4.9 %collective-permute-done.10.refs_1_ = bf16[32,7,16,128]{3,2,1,0:T(8,128)(2,1)S(1)} collective-permute-done((bf16[32,7,16,128]{3,2,1,0:T(8,128)(2,1)}, bf16[32,7,16,128]{3,2,1,0:T(8,128)(2,1)S(1)}, u32[]{:S(2)}, u32[]{:S(2)}) %collective-permute-start.10) | collective-permute-done | bytes 917536 | tf_op jit(solution)/shard_map/ppermute | solution.py:47
  89.9 0.0 collective-permute-done.11.refs_2_
  89.9 4.1 %collective-permute-done.9.refs_0_ = bf16[32,7,16,128]{3,2,1,0:T(8,128)(2,1)S(1)} collective-permute-done((bf16[32,7,16,128]{3,2,1,0:T(8,128)(2,1)}, bf16[32,7,16,128]{3,2,1,0:T(8,128)(2,1)S(1)}, u32[]{:S(2)}, u32[]{:S(2)}) %collective-permute-start.9) | collective-permute-done | bytes 917536 | tf_op jit(solution)/shard_map/ppermute | solution.py:47
  94.0 5.2 %all-to-all-done.1.refs_3_.refs_4_.refs_5_ = bf16[128,5,2,128]{3,2,1,0:T(2,128)(2,1)S(1)} async-done(((bf16[128,5,2,128]{3,2,1,0:T(2,128)(2,1)}), bf16[128,5,2,128]{3,2,1,0:T(2,128)(2,1)S(1)}, u32[]{:S(2)}, u32[]{:S(2)}) %all-to-all-start.1) | async-done | bytes 327712 | tf_op jit(solution)/shard_map/all_to_all | solution.py:411
  99.2 0.0 collective-permute-start.21
  99.2 0.5 collective-permute-start.22
  99.7 0.0 collective-permute-start.23
  99.7 2.3 %half.1 = (f32[2048,128]{1,0:T(8,128)S(1)}, bf16[128,2,16,128]{3,2,1,0:T(8,128)(2,1)S(1)}) custom-call(bf16[32,7,16,128]{3,2,1,0:T(8,128)(2,1)} %temporal_blocks.1.refs_0_, bf16[32,7,16,128]{3,2,1,0:T(8,128)(2,1)S(1)} %get-tuple-element.19.refs_1_, bf16[32,7,16,128]{3,2,1,0:T(8,128)(2,1)S(1)} %get-tuple-element.20.refs_2_, ...), custom_call_target="tpu_custom_call" | custom-call | flops 3000000000 | bytes 5570560 | tf_op jit(solution)/shard_map/half/pallas_call | solution.py:355
  102.1 1.0 copy-done.1
  103.1 0.0 collective-permute-done.20.refs_0_
  103.1 0.0 collective-permute-done.21.refs_1_
  103.1 0.0 collective-permute-done.22.refs_2_
  103.1 1.2 collective-permute-done.23.refs_3_
  104.3 5.5 %temporal.1 = (bf16[128,3,2,128]{3,2,1,0:T(2,128)(2,1)}, bf16[128,2,16,128]{3,2,1,0:T(8,128)(2,1)S(1)}) custom-call(bf16[32,7,16,128]{3,2,1,0:T(8,128)(2,1)} %collective-permute-done.20.refs_0_, bf16[32,7,16,128]{3,2,1,0:T(8,128)(2,1)S(1)} %collective-permute-done.21.refs_1_, bf16[32,7,16,128]{3,2,1,0:T(8,128)(2,1)S(1)} %collective-permute-done.22.refs_2_, ...), custom_call_target="tpu_custom_call" | custom-call | flops 5000000000 | bytes 6291456 | tf_op jit(solution)/shard_map/temporal/pallas_call | solution.py:355
  109.8 1.0 copy-done.3
  110.8 6.7 %all-to-all-start.2 = ((bf16[128,3,2,128]{3,2,1,0:T(2,128)(2,1)}), bf16[128,3,2,128]{3,2,1,0:T(2,128)(2,1)S(1)}, u32[]{:S(2)}, u32[]{:S(2)}) async-start(bf16[128,3,2,128]{3,2,1,0:T(2,128)(2,1)} %get-tuple-element.25), calls=%async_computation.2 | async-start | bytes 393216 | tf_op jit(solution)/shard_map/all_to_all | solution.py:442
  117.5 1.2 copy-done.4
  118.7 1.0 weights.1
  119.8 11.1 %all-to-all-done.2.attn = bf16[128,3,2,128]{3,2,1,0:T(2,128)(2,1)S(1)} async-done(((bf16[128,3,2,128]{3,2,1,0:T(2,128)(2,1)}), bf16[128,3,2,128]{3,2,1,0:T(2,128)(2,1)S(1)}, u32[]{:S(2)}, u32[]{:S(2)}) %all-to-all-start.2) | async-done | bytes 196640 | tf_op jit(solution)/shard_map/all_to_all | solution.py:442
  130.9 1.4 %mixed.1 = bf16[128,1280]{1,0:T(8,128)(2,1)} custom-call(bf16[1280,640]{1,0:T(8,128)(2,1)S(1)} %weights.1, bf16[128,3,2,128]{3,2,1,0:T(2,128)(2,1)S(1)} %all-to-all-done.2.attn, bf16[128,1280]{1,0:T(8,128)(2,1)S(1)} %get-tuple-element.26.hidden), custom_call_target="tpu_custom_call" | custom-call | flops 1000000000 | bytes 2490368 | tf_op jit(solution)/shard_map/mixed/pallas_call | solution.py:355
  (15 shorter events, 0.0 us)
Async XLA Ops:
  0.0 63.2 %copy-start.5 = (f32[1280]{0:T(1024)S(1)}, f32[1280]{0:T(1024)}, u32[]{:S(2)}) copy-start(f32[1280]{0:T(1024)} %param.10) | copy-start | bytes 15364
  0.0 63.2 %copy-start.6 = (f32[1280]{0:T(1024)S(1)}, f32[1280]{0:T(1024)}, u32[]{:S(2)}) copy-start(f32[1280]{0:T(1024)} %param.13) | copy-start | bytes 15364
  24.9 7.3 %collective-permute-start = (bf16[8,7,16,128]{3,2,1,0:T(8,128)(2,1)S(1)}, bf16[8,7,16,128]{3,2,1,0:T(8,128)(2,1)S(1)}, u32[]{:S(2)}, u32[]{:S(2)}) collective-permute-start(bf16[8,7,16,128]{3,2,1,0:T(8,128)(2,1)S(1)} %slice.4), channel_id=1, source_target_pairs={{0,32},{1,33},{2,34},{3,35},{4,36},{5,37},{6,38},{7,39},{8,40},{9,... | collective-permute-start | bytes 688136 | tf_op jit(solution)/shard_map/ppermute | solution.py:47
  26.5 7.8 %collective-permute-start.1 = (bf16[8,7,16,128]{3,2,1,0:T(8,128)(2,1)S(1)}, bf16[8,7,16,128]{3,2,1,0:T(8,128)(2,1)S(1)}, u32[]{:S(2)}, u32[]{:S(2)}) collective-permute-start(bf16[8,7,16,128]{3,2,1,0:T(8,128)(2,1)S(1)} %slice.4), channel_id=1, source_target_pairs={{0,96},{1,97},{2,98},{3,99},{4,100},{5,101},{6,102},{7,103},{8,104... | collective-permute-start | bytes 688136 | tf_op jit(solution)/shard_map/ppermute | solution.py:47
  28.3 7.5 %collective-permute-start.2 = (bf16[8,7,16,128]{3,2,1,0:T(8,128)(2,1)S(1)}, bf16[8,7,16,128]{3,2,1,0:T(8,128)(2,1)S(1)}, u32[]{:S(2)}, u32[]{:S(2)}) collective-permute-start(bf16[8,7,16,128]{3,2,1,0:T(8,128)(2,1)S(1)} %slice.4), channel_id=1, source_target_pairs={{0,64},{1,65},{2,66},{3,67},{4,68},{5,69},{6,70},{7,71},{8,72},{9,... | collective-permute-start | bytes 688136 | tf_op jit(solution)/shard_map/ppermute | solution.py:47
  35.9 11.0 %collective-permute-start.3 = (bf16[20,7,16,128]{3,2,1,0:T(8,128)(2,1)S(1)}, bf16[20,7,16,128]{3,2,1,0:T(8,128)(2,1)S(1)}, u32[]{:S(2)}, u32[]{:S(2)}) collective-permute-start(bf16[20,7,16,128]{3,2,1,0:T(8,128)(2,1)S(1)} %get-tuple-element.16.refs_0_), channel_id=1, source_target_pairs={{0,1},{1,2},{2,3},{3,0},{4,5},{5,6},{6,7},{7,4},{8,9},{9,10},{10,1... | collective-permute-start | bytes 1720328 | tf_op jit(solution)/shard_map/ppermute | solution.py:53
  37.5 9.7 %collective-permute-start.6 = (bf16[20,7,16,128]{3,2,1,0:T(8,128)(2,1)S(1)}, bf16[20,7,16,128]{3,2,1,0:T(8,128)(2,1)S(1)}, u32[]{:S(2)}, u32[]{:S(2)}) collective-permute-start(bf16[20,7,16,128]{3,2,1,0:T(8,128)(2,1)S(1)} %get-tuple-element.17.refs_1_), channel_id=1, source_target_pairs={{0,3},{1,0},{2,1},{3,2},{4,7},{5,4},{6,5},{7,6},{8,11},{9,8},{10,9... | collective-permute-start | bytes 1720328 | tf_op jit(solution)/shard_map/ppermute | solution.py:53
  39.2 13.8 %collective-permute-start.4 = (bf16[20,7,16,128]{3,2,1,0:T(8,128)(2,1)S(1)}, bf16[20,7,16,128]{3,2,1,0:T(8,128)(2,1)S(1)}, u32[]{:S(2)}, u32[]{:S(2)}) collective-permute-start(bf16[20,7,16,128]{3,2,1,0:T(8,128)(2,1)S(1)} %get-tuple-element.17.refs_1_), channel_id=1, source_target_pairs={{0,1},{1,2},{2,3},{3,0},{4,5},{5,6},{6,7},{7,4},{8,9},{9,10},{10,1... | collective-permute-start | bytes 1720328 | tf_op jit(solution)/shard_map/ppermute | solution.py:53
  39.5 15.3 %collective-permute-start.5 = (bf16[20,7,16,128]{3,2,1,0:T(8,128)(2,1)S(1)}, bf16[20,7,16,128]{3,2,1,0:T(8,128)(2,1)S(1)}, u32[]{:S(2)}, u32[]{:S(2)}) collective-permute-start(bf16[20,7,16,128]{3,2,1,0:T(8,128)(2,1)S(1)} %get-tuple-element.16.refs_0_), channel_id=1, source_target_pairs={{0,3},{1,0},{2,1},{3,2},{4,7},{5,4},{6,5},{7,6},{8,11},{9,8},{10,9... | collective-permute-start | bytes 1720328 | tf_op jit(solution)/shard_map/ppermute | solution.py:53
  42.4 12.4 %collective-permute-start.12 = (bf16[20,7,16,128]{3,2,1,0:T(8,128)(2,1)S(1)}, bf16[20,7,16,128]{3,2,1,0:T(8,128)(2,1)S(1)}, u32[]{:S(2)}, u32[]{:S(2)}) collective-permute-start(bf16[20,7,16,128]{3,2,1,0:T(8,128)(2,1)S(1)} %get-tuple-element.16.refs_0_), channel_id=1, source_target_pairs={{0,128},{1,129},{2,130},{3,131},{4,132},{5,133},{6,134},{7,135},{8... | collective-permute-start | bytes 1720328 | tf_op jit(solution)/shard_map/ppermute | solution.py:63
  46.9 8.5 %collective-permute-start.13 = (bf16[20,7,16,128]{3,2,1,0:T(8,128)(2,1)S(1)}, bf16[20,7,16,128]{3,2,1,0:T(8,128)(2,1)S(1)}, u32[]{:S(2)}, u32[]{:S(2)}) collective-permute-start(bf16[20,7,16,128]{3,2,1,0:T(8,128)(2,1)S(1)} %get-tuple-element.17.refs_1_), channel_id=1, source_target_pairs={{0,128},{1,129},{2,130},{3,131},{4,132},{5,133},{6,134},{7,135},{8... | collective-permute-start | bytes 1720328 | tf_op jit(solution)/shard_map/ppermute | solution.py:63
  47.2 11.9 %collective-permute-start.7 = (bf16[20,7,16,128]{3,2,1,0:T(8,128)(2,1)S(1)}, bf16[20,7,16,128]{3,2,1,0:T(8,128)(2,1)S(1)}, u32[]{:S(2)}, u32[]{:S(2)}) collective-permute-start(bf16[20,7,16,128]{3,2,1,0:T(8,128)(2,1)S(1)} %collective-permute-done.3.refs_2_), channel_id=1, source_target_pairs={{0,1},{1,2},{2,3},{3,0},{4,5},{5,6},{6,7},{7,4},{8,9},{9,10},{10,1... | collective-permute-start | bytes 1720328 | tf_op jit(solution)/shard_map/ppermute | solution.py:53
  53.0 9.7 %collective-permute-start.8 = (bf16[20,7,16,128]{3,2,1,0:T(8,128)(2,1)S(1)}, bf16[20,7,16,128]{3,2,1,0:T(8,128)(2,1)S(1)}, u32[]{:S(2)}, u32[]{:S(2)}) collective-permute-start(bf16[20,7,16,128]{3,2,1,0:T(8,128)(2,1)S(1)} %collective-permute-done.6.refs_5_), channel_id=1, source_target_pairs={{0,3},{1,0},{2,1},{3,2},{4,7},{5,4},{6,5},{7,6},{8,11},{9,8},{10,9... | collective-permute-start | bytes 1720328 | tf_op jit(solution)/shard_map/ppermute | solution.py:53
  54.8 7.9 %collective-permute-start.14 = (bf16[20,7,16,128]{3,2,1,0:T(8,128)(2,1)S(1)}, bf16[20,7,16,128]{3,2,1,0:T(8,128)(2,1)S(1)}, u32[]{:S(2)}, u32[]{:S(2)}) collective-permute-start(bf16[20,7,16,128]{3,2,1,0:T(8,128)(2,1)S(1)} %collective-permute-done.3.refs_2_), channel_id=1, source_target_pairs={{0,128},{1,129},{2,130},{3,131},{4,132},{5,133},{6,134},{7,135},{8... | collective-permute-start | bytes 1720328 | tf_op jit(solution)/shard_map/ppermute | solution.py:63
  54.8 9.4 %collective-permute-start.17 = (bf16[20,7,16,128]{3,2,1,0:T(8,128)(2,1)S(1)}, bf16[20,7,16,128]{3,2,1,0:T(8,128)(2,1)S(1)}, u32[]{:S(2)}, u32[]{:S(2)}) collective-permute-start(bf16[20,7,16,128]{3,2,1,0:T(8,128)(2,1)S(1)} %collective-permute-done.6.refs_5_), channel_id=1, source_target_pairs={{0,128},{1,129},{2,130},{3,131},{4,132},{5,133},{6,134},{7,135},{8... | collective-permute-start | bytes 1720328 | tf_op jit(solution)/shard_map/ppermute | solution.py:63
  55.3 11.1 %collective-permute-start.15 = (bf16[20,7,16,128]{3,2,1,0:T(8,128)(2,1)S(1)}, bf16[20,7,16,128]{3,2,1,0:T(8,128)(2,1)S(1)}, u32[]{:S(2)}, u32[]{:S(2)}) collective-permute-start(bf16[20,7,16,128]{3,2,1,0:T(8,128)(2,1)S(1)} %collective-permute-done.4.refs_3_), channel_id=1, source_target_pairs={{0,128},{1,129},{2,130},{3,131},{4,132},{5,133},{6,134},{7,135},{8... | collective-permute-start | bytes 1720328 | tf_op jit(solution)/shard_map/ppermute | solution.py:63
  59.1 8.5 %collective-permute-start.16 = (bf16[20,7,16,128]{3,2,1,0:T(8,128)(2,1)S(1)}, bf16[20,7,16,128]{3,2,1,0:T(8,128)(2,1)S(1)}, u32[]{:S(2)}, u32[]{:S(2)}) collective-permute-start(bf16[20,7,16,128]{3,2,1,0:T(8,128)(2,1)S(1)} %collective-permute-done.5.refs_4_), channel_id=1, source_target_pairs={{0,128},{1,129},{2,130},{3,131},{4,132},{5,133},{6,134},{7,135},{8... | collective-permute-start | bytes 1720328 | tf_op jit(solution)/shard_map/ppermute | solution.py:63
  62.7 5.0 %collective-permute-start.18 = (bf16[20,7,16,128]{3,2,1,0:T(8,128)(2,1)S(1)}, bf16[20,7,16,128]{3,2,1,0:T(8,128)(2,1)S(1)}, u32[]{:S(2)}, u32[]{:S(2)}) collective-permute-start(bf16[20,7,16,128]{3,2,1,0:T(8,128)(2,1)S(1)} %collective-permute-done.7.refs_6_), channel_id=1, source_target_pairs={{0,128},{1,129},{2,130},{3,131},{4,132},{5,133},{6,134},{7,135},{8... | collective-permute-start | bytes 1720328 | tf_op jit(solution)/shard_map/ppermute | solution.py:63
  62.7 5.0 %collective-permute-start.19 = (bf16[20,7,16,128]{3,2,1,0:T(8,128)(2,1)S(1)}, bf16[20,7,16,128]{3,2,1,0:T(8,128)(2,1)S(1)}, u32[]{:S(2)}, u32[]{:S(2)}) collective-permute-start(bf16[20,7,16,128]{3,2,1,0:T(8,128)(2,1)S(1)} %collective-permute-done.8.refs_7_), channel_id=1, source_target_pairs={{0,128},{1,129},{2,130},{3,131},{4,132},{5,133},{6,134},{7,135},{8... | collective-permute-start | bytes 1720328 | tf_op jit(solution)/shard_map/ppermute | solution.py:63
  63.2 4.5 %copy-start = (bf16[1,128,1280]{2,1,0:T(8,128)(2,1)S(1)}, bf16[1,128,1280]{2,1,0:T(8,128)(2,1)}, u32[]{:S(2)}) copy-start(bf16[1,128,1280]{2,1,0:T(8,128)(2,1)} %param.8) | copy-start | bytes 983044
  64.3 25.7 %collective-permute-start.10 = (bf16[32,7,16,128]{3,2,1,0:T(8,128)(2,1)}, bf16[32,7,16,128]{3,2,1,0:T(8,128)(2,1)S(1)}, u32[]{:S(2)}, u32[]{:S(2)}) collective-permute-start(bf16[32,7,16,128]{3,2,1,0:T(8,128)(2,1)} %temporal_blocks.1.refs_0_), channel_id=1, source_target_pairs={{0,96},{1,97},{2,98},{3,99},{4,100},{5,101},{6,102},{7,103},{8,104... | collective-permute-start | bytes 2752520 | tf_op jit(solution)/shard_map/ppermute | solution.py:47
  66.4 23.5 %collective-permute-start.11 = (bf16[32,7,16,128]{3,2,1,0:T(8,128)(2,1)}, bf16[32,7,16,128]{3,2,1,0:T(8,128)(2,1)S(1)}, u32[]{:S(2)}, u32[]{:S(2)}) collective-permute-start(bf16[32,7,16,128]{3,2,1,0:T(8,128)(2,1)} %temporal_blocks.1.refs_0_), channel_id=1, source_target_pairs={{0,64},{1,65},{2,66},{3,67},{4,68},{5,69},{6,70},{7,71},{8,72},{9,... | collective-permute-start | bytes 2752520 | tf_op jit(solution)/shard_map/ppermute | solution.py:47
  67.7 26.4 %collective-permute-start.9 = (bf16[32,7,16,128]{3,2,1,0:T(8,128)(2,1)}, bf16[32,7,16,128]{3,2,1,0:T(8,128)(2,1)S(1)}, u32[]{:S(2)}, u32[]{:S(2)}) collective-permute-start(bf16[32,7,16,128]{3,2,1,0:T(8,128)(2,1)} %temporal_blocks.1.refs_0_), channel_id=1, source_target_pairs={{0,32},{1,33},{2,34},{3,35},{4,36},{5,37},{6,38},{7,39},{8,40},{9,... | collective-permute-start | bytes 2752520 | tf_op jit(solution)/shard_map/ppermute | solution.py:47
  75.2 24.0 %all-to-all-start.1 = ((bf16[128,5,2,128]{3,2,1,0:T(2,128)(2,1)}), bf16[128,5,2,128]{3,2,1,0:T(2,128)(2,1)S(1)}, u32[]{:S(2)}, u32[]{:S(2)}) async-start(bf16[128,5,2,128]{3,2,1,0:T(2,128)(2,1)} %get-tuple-element.18), calls=%async_computation.1 | async-start | bytes 655360 | tf_op jit(solution)/shard_map/all_to_all | solution.py:411
  85.0 18.1 %collective-permute-start.20 = (bf16[32,7,16,128]{3,2,1,0:T(8,128)(2,1)}, bf16[32,7,16,128]{3,2,1,0:T(8,128)(2,1)}, u32[]{:S(2)}, u32[]{:S(2)}) collective-permute-start(bf16[32,7,16,128]{3,2,1,0:T(8,128)(2,1)} %temporal_blocks.1.refs_0_), channel_id=1, source_target_pairs={{0,128},{1,129},{2,130},{3,131},{4,132},{5,133},{6,134},{7,135},{8... | collective-permute-start | bytes 2752520 | tf_op jit(solution)/shard_map/ppermute | solution.py:63
  99.2 3.8 %collective-permute-start.21 = (bf16[32,7,16,128]{3,2,1,0:T(8,128)(2,1)S(1)}, bf16[32,7,16,128]{3,2,1,0:T(8,128)(2,1)S(1)}, u32[]{:S(2)}, u32[]{:S(2)}) collective-permute-start(bf16[32,7,16,128]{3,2,1,0:T(8,128)(2,1)S(1)} %get-tuple-element.19.refs_1_), channel_id=1, source_target_pairs={{0,128},{1,129},{2,130},{3,131},{4,132},{5,133},{6,134},{7,135},{8... | collective-permute-start | bytes 2752520 | tf_op jit(solution)/shard_map/ppermute | solution.py:63
  99.2 3.8 %collective-permute-start.22 = (bf16[32,7,16,128]{3,2,1,0:T(8,128)(2,1)S(1)}, bf16[32,7,16,128]{3,2,1,0:T(8,128)(2,1)S(1)}, u32[]{:S(2)}, u32[]{:S(2)}) collective-permute-start(bf16[32,7,16,128]{3,2,1,0:T(8,128)(2,1)S(1)} %get-tuple-element.20.refs_2_), channel_id=1, source_target_pairs={{0,128},{1,129},{2,130},{3,131},{4,132},{5,133},{6,134},{7,135},{8... | collective-permute-start | bytes 2752520 | tf_op jit(solution)/shard_map/ppermute | solution.py:63
  99.7 4.6 %collective-permute-start.23 = (bf16[32,7,16,128]{3,2,1,0:T(8,128)(2,1)S(1)}, bf16[32,7,16,128]{3,2,1,0:T(8,128)(2,1)S(1)}, u32[]{:S(2)}, u32[]{:S(2)}) collective-permute-start(bf16[32,7,16,128]{3,2,1,0:T(8,128)(2,1)S(1)} %get-tuple-element.21.refs_3_), channel_id=1, source_target_pairs={{0,128},{1,129},{2,130},{3,131},{4,132},{5,133},{6,134},{7,135},{8... | collective-permute-start | bytes 2752520 | tf_op jit(solution)/shard_map/ppermute | solution.py:63
  102.1 1.0 copy-start.1
  104.3 13.2 %copy-start.2 = (bf16[128,2,16,128]{3,2,1,0:T(8,128)(2,1)S(1)}, bf16[128,2,16,128]{3,2,1,0:T(8,128)(2,1)}, u32[]{:S(2)}) copy-start(bf16[128,2,16,128]{3,2,1,0:T(8,128)(2,1)} %copy-done.1) | copy-start | bytes 3145732
  109.8 1.0 copy-start.3
  110.8 20.1 %all-to-all-start.2 = ((bf16[128,3,2,128]{3,2,1,0:T(2,128)(2,1)}), bf16[128,3,2,128]{3,2,1,0:T(2,128)(2,1)S(1)}, u32[]{:S(2)}, u32[]{:S(2)}) async-start(bf16[128,3,2,128]{3,2,1,0:T(2,128)(2,1)} %get-tuple-element.25), calls=%async_computation.2 | async-start | bytes 393216 | tf_op jit(solution)/shard_map/all_to_all | solution.py:442
  117.5 1.2 copy-start.4

commit v4 on v3

--- a/solution.py
+++ b/solution.py
@@ -68,6 +68,7 @@
 
 
 ANY = pl.BlockSpec(memory_space=pl.ANY)
+HBM = pl.BlockSpec(memory_space=pltpu.HBM)
 
 
 def small(mib):
@@ -239,18 +240,20 @@
 def out_project(own, oth, acc, rows, part, dims, x_core):
     c, _, _ = place()
     lo, mid, hi = part(0, 256), part(256, 384), part(384, 640)
+    upper = lax.rem(lax.broadcasted_iota(jnp.int32, (512, 128), 0), 16) < 10
     xa = jnp.where(c == 0, lo, hi)
     xb = jnp.where(c == 0, hi, lo)
     for j in range(4):
         wa, wb = pieces_of(own, oth, j, 5, 2)
-        spread(acc, dot(wa, xa, dims) + dot(wb, xb, dims), j, 0, x_core)
+        both = dot(wa, xa, dims) + dot(wb, xb, dims)
         ma, mb = dot(wa[:, :128], mid, dims), dot(wb[:, :128], mid, dims)
-        spread(acc, jnp.where(c == 0, ma, mb), j, 16, x_core)
-        spread(acc, jnp.where(c == 0, mb, ma), j, 32, x_core)
+        m0, m1 = jnp.where(c == 0, ma, mb), jnp.where(c == 0, mb, ma)
+        spread(acc, jnp.where(upper, both, m0), j, 0, x_core)
+        spread(acc, m1, j, 16, x_core)
     for s in range(SEQ):
         x, z, y = s // 32, (s // 4) % 8, s % 4
-        m0 = acc[x, z, y, 26:31, :]
-        m1 = acc[x, z, y, 42:47, :]
+        m0 = acc[x, z, y, 10:15, :]
+        m1 = acc[x, z, y, 26:31, :]
         rows[10 * s : 10 * s + 10, :] = acc[x, z, y, 0:10, :] + jnp.concatenate([m0, m1], axis=0)
 
 
@@ -260,16 +263,18 @@
     return jnp.where(first, lo, hi), jnp.where(first, hi, lo)
 
 
-def heads(rows, keys, attn):
+def heads(rows, scores, attn):
+    keys = scores.shape[1]
     for h in range(HEADS):
         q = rows[64 * h : 64 * (h + 1), 0:128].astype(BF)
         k = rows[640 + 64 * h : 640 + 64 * (h + 1), 0:keys].astype(BF)
-        v = rows[1280 + 64 * h : 1280 + 64 * (h + 1), 0:keys].astype(BF)
-        st = lax.dot_general(k, q, (((0,), (0,)), ((), ())), preferred_element_type=F32)
-        st = st * (HEAD**-0.5)
+        scores[h] = dot(k, q, (((0,), (0,)), ((), ())))
+    for h in range(HEADS):
+        st = scores[h] * (HEAD**-0.5)
         e = jnp.exp(st - jnp.max(st, axis=0, keepdims=True))
         p = (e * (1.0 / jnp.sum(e, axis=0, keepdims=True))).astype(BF)
-        attn[64 * h : 64 * (h + 1), :] = jnp.dot(v, p, preferred_element_type=F32)
+        v = rows[1280 + 64 * h : 1280 + 64 * (h + 1), 0:keys].astype(BF)
+        attn[64 * h : 64 * (h + 1), :] = dot(v, p, NN)
 
 
 def reference_tokens(own, last):
@@ -288,11 +293,11 @@
 
 def spatial_kernel(*refs):
     own, oth = refs[0:8], refs[8:16]
-    latents, gain_s, gain_t, hidden, tnormed, acc, rows, last, attn, acc_out, rows_out = refs[16:]
+    latents, gain_s, gain_t, hidden, tnormed, acc, rows, last, attn, scores, acc_out, rows_out = refs[16:]
     normed = layer_norm(latents[...].astype(F32), gain_s[...])
     tokens = jnp.concatenate([normed, reference_tokens(own, last)], axis=0)
     qkv_project(own, oth, acc, rows, tokens, 0)
-    heads(rows, 256, attn)
+    heads(rows, scores, attn)
     part = lambda a, b: attn[a:b, :].astype(BF)
     out_project(own, oth, acc_out, rows_out, part, NN, 0)
     h = (latents[...].astype(F32) + rows_out[...].T).astype(BF)
@@ -300,28 +305,42 @@
     to_rows(layer_norm(h.astype(F32), gain_t[...]).astype(F32), tnormed, rows_out, 10)
 
 
+def output_tiles(pieces, out, sems):
+    copies = [
+        pltpu.make_async_copy(p.at[:, pl.ds(5, 2)], out.at[pl.ds(32 * j, 32)], sems.at[j])
+        for j, p in enumerate(pieces)
+    ]
+    for copy in copies:
+        copy.start()
+    return copies
+
+
 def half_kernel(*refs):
-    own, (tokens, out, for_out, wide) = refs[0:4], refs[4:]
+    own, (tokens, out, for_out, wide, sems) = refs[0:4], refs[4:]
     c, _, _ = place()
+    copies = output_tiles(own, for_out, sems)
     xa, _ = halves(from_rows(tokens, wide, 10), c)
     for j in range(4):
         wa = jnp.concatenate([lanes(own, j, i, 0, 5) for i in range(4)], axis=0)
         out[512 * j : 512 * (j + 1), :] = dot(wa, xa, NT)
-        for_out[32 * j : 32 * (j + 1)] = own[j][:, 5:7]
+    for copy in copies:
+        copy.wait()
 
 
 def temporal_kernel(*refs):
     oth = refs[0:4]
-    half, tokens, out, for_out, acc, rows, attn, wide, wide_out = refs[4:]
+    half, tokens, out, for_out, acc, rows, attn, scores, wide, wide_out, sems = refs[4:]
     c, _, _ = place()
+    copies = output_tiles(oth, for_out, sems)
     _, xb = halves(from_rows(tokens, wide, 10), c)
     for j in range(4):
         wb = jnp.concatenate([lanes(oth, i, j, 0, 5) for i in range(4)], axis=0)
         spread(acc, half[512 * j : 512 * (j + 1), :] + dot(wb, xb, NT), j, 0, 1)
-        for_out[32 * j : 32 * (j + 1)] = oth[j][:, 5:7]
     compact(acc, rows)
-    heads(rows, 128, attn)
+    heads(rows, scores, attn)
     to_rows(attn[...].T, out, wide_out, 5)
+    for copy in copies:
+        copy.wait()
 
 
 def weights_kernel(*refs):
@@ -356,8 +375,8 @@
         kernel,
         out_shape=shapes[0] if single else shapes,
         in_specs=vmem(len(args)),
-        out_specs=vmem(1)[0] if single else vmem(len(shapes)),
-        scratch_shapes=[pltpu.VMEM(s, F32) for s in scratch],
+        out_specs=vmem(1)[0] if single else [HBM if s == (SEQ, 2, 16, 128) else vmem(1)[0] for s in outs],
+        scratch_shapes=[pltpu.VMEM(s, F32) if isinstance(s, tuple) else s for s in scratch],
         compiler_params=small(mib),
         cost_estimate=pl.CostEstimate(flops=flops, bytes_accessed=size, transcendentals=0),
         name=name,
@@ -401,7 +420,8 @@
             (1920, 256),
             (GROUP, 1024, 128),
             (INNER, 128),
-            (NX, NZ, NY, 48, 128),
+            (HEADS, 256, 128),
+            (NX, NZ, NY, 32, 128),
             (D, 128),
         ],
         "spatial",
@@ -415,7 +435,7 @@
         half_kernel,
         own_t + [tokens],
         [(2048, 128), (SEQ, 2, 16, 128)],
-        [(D, 128)],
+        [(D, 128), pltpu.SemaphoreType.DMA((4,))],
         "half",
         3 * 10**9,
         16,
@@ -425,7 +445,15 @@
         temporal_kernel,
         oth_t + [half_t, tokens],
         [(PIX, 3, 2, 128), (SEQ, 2, 16, 128)],
-        [(NX, NZ, NY, 16, 128), (1920, 128), (INNER, 128), (D, 128), (768, 128)],
+        [
+            (NX, NZ, NY, 16, 128),
+            (1920, 128),
+            (INNER, 128),
+            (HEADS, 128, 128),
+            (D, 128),
+            (768, 128),
+            pltpu.SemaphoreType.DMA((4,)),
+        ],
         "temporal",
         5 * 10**9,
         16,

time: 133 us -> 130 us (0.977)
  Pallas kernels: 20.5 us -> 17.1 us
    pallas_call x5, Pallas kernels: 17.8 us -> 14.3 us  [call(): pl.pallas_call(kernel, out_shape=shapes[0] if single else shapes, in_spec...]
    ppermute x6, waiting for transfers between devices: 14.7 us -> 17.1 us  [ring(): lax.ppermute(block, ('clip', 'seq'), ring_perm(k, stage))]
    all_to_all x1, waiting for transfers between devices: 5.16 us -> 2.77 us  [body(): tokens = lax.all_to_all(tnormed, 'seq', 0, 0, tiled=True)]
  transfers between devices with their start and end apart: 26 -> 26, of which waited for: 13 -> 13; matrix products, arithmetic and copies ran while one was open for 0% -> 0% of each run, Pallas kernels for 9% -> 8%
where the time goes in v4:
time: 130 us; the launch traced here: 129 us
  waiting for transfers between devices  48.5 us (37%)
  starting transfers between devices  36.8 us (28%)
  blocking collectives  23.2 us (18%)
  Pallas kernels  17.1 us (13%)
  local copies, waits for them, and re-layouts  3.2 us (2%)
    all_to_all x1, blocking collectives, body(): lax.all_to_all(packed, 'seq', 0, 0, axis_index_groups=Z_GROUPS, tiled=True)  23.2 us
    ppermute x6, waiting for transfers between devices, ring(): lax.ppermute(block, ('clip', 'seq'), ring_perm(k, stage))  17.1 us
    ppermute x6, waiting for transfers between devices, shift(): return lax.ppermute(part, ('clip', 'seq'), ring_perm(k, stage))  16.2 us
    pallas_call x5, Pallas kernels, call(): pl.pallas_call(kernel, out_shape=shapes[0] if single else shapes, in_spec...  14.3 us
    all_to_all x1, waiting for transfers between devices, body(): back = lax.all_to_all(tattn, 'seq', 0, 0, tiled=True)  11.3 us
    ppermute x6, starting transfers between devices, shift(): return lax.ppermute(part, ('clip', 'seq'), ring_perm(k, stage))  10 us
    all_to_all x1, starting transfers between devices, body(): tokens = lax.all_to_all(tnormed, 'seq', 0, 0, tiled=True)  9.73 us
    ppermute x6, starting transfers between devices, ring(): lax.ppermute(block, ('clip', 'seq'), ring_perm(k, stage))  8.6 us
  transfers between devices with their start and end apart: 26, of which 13 were waited for; matrix products, arithmetic and copies ran while one was open for 0% of the time, Pallas kernels for 8%

profile of v4, /device:TPU:32, one launch (start us, length us, event | category | flops | bytes accessed | tf_op | source)
XLA Modules:
  0.0 129.0 jit_solution(10522798208556915759)
XLA Ops:
  0.0 1.7 %pack.1 = bf16[8,14,16,128]{3,2,1,0:T(8,128)(2,1)} custom-call(bf16[15,1280]{1,0:T(8,128)(2,1)} %bitcast.7, bf16[1,1280]{1,0:T(2,128)(2,1)} %ref_in.1, bf16[10,640]{1,0:T(8,128)(2,1)} %bitcast.9, bf16[15,1280]{1,0:T(8,128)(2,1)} %bitcast.8, bf16[10,640]{1,0:T(8,128)(2,1)} %bitcast.10), custom_call_target="tpu_custom_call" | custom-call | tf_op jit(solution)/shard_map/pack/pallas_call | solution.py:391
  1.7 23.2 %all_to_all.15.along_z = bf16[8,14,16,128]{3,2,1,0:T(8,128)(2,1)S(1)} all-to-all(bf16[8,14,16,128]{3,2,1,0:T(8,128)(2,1)} %pack.1), channel_id=1, replica_groups={{0,4,8,12,16,20,24,28},{1,5,9,13,17,21,25,29},{2,6,10,14,18,22,26,30},{..., dimensions={0} | all-to-all | bytes 917504 | tf_op jit(solution)/shard_map/all_to_all | solution.py:400
  24.9 1.6 %collective-permute-start = (bf16[8,7,16,128]{3,2,1,0:T(8,128)(2,1)S(1)}, bf16[8,7,16,128]{3,2,1,0:T(8,128)(2,1)S(1)}, u32[]{:S(2)}, u32[]{:S(2)}) collective-permute-start(bf16[8,7,16,128]{3,2,1,0:T(8,128)(2,1)S(1)} %slice.4), channel_id=1, source_target_pairs={{0,32},{1,33},{2,34},{3,35},{4,36},{5,37},{6,38},{7,39},{8,40},{9,... | collective-permute-start | bytes 688136 | tf_op jit(solution)/shard_map/ppermute | solution.py:47
  26.5 1.7 %collective-permute-start.1 = (bf16[8,7,16,128]{3,2,1,0:T(8,128)(2,1)S(1)}, bf16[8,7,16,128]{3,2,1,0:T(8,128)(2,1)S(1)}, u32[]{:S(2)}, u32[]{:S(2)}) collective-permute-start(bf16[8,7,16,128]{3,2,1,0:T(8,128)(2,1)S(1)} %slice.4), channel_id=1, source_target_pairs={{0,96},{1,97},{2,98},{3,99},{4,100},{5,101},{6,102},{7,103},{8,104... | collective-permute-start | bytes 688136 | tf_op jit(solution)/shard_map/ppermute | solution.py:47
  28.3 1.8 %collective-permute-start.2 = (bf16[8,7,16,128]{3,2,1,0:T(8,128)(2,1)S(1)}, bf16[8,7,16,128]{3,2,1,0:T(8,128)(2,1)S(1)}, u32[]{:S(2)}, u32[]{:S(2)}) collective-permute-start(bf16[8,7,16,128]{3,2,1,0:T(8,128)(2,1)S(1)} %slice.4), channel_id=1, source_target_pairs={{0,64},{1,65},{2,66},{3,67},{4,68},{5,69},{6,70},{7,71},{8,72},{9,... | collective-permute-start | bytes 688136 | tf_op jit(solution)/shard_map/ppermute | solution.py:47
  30.1 2.2 %collective-permute-done.p1 = bf16[8,7,16,128]{3,2,1,0:T(8,128)(2,1)S(1)} collective-permute-done((bf16[8,7,16,128]{3,2,1,0:T(8,128)(2,1)S(1)}, bf16[8,7,16,128]{3,2,1,0:T(8,128)(2,1)S(1)}, u32[]{:S(2)}, u32[]{:S(2)}) %collective-permute-start) | collective-permute-done | bytes 229408 | tf_op jit(solution)/shard_map/ppermute | solution.py:47
  32.2 2.0 %collective-permute-done.1.p2 = bf16[8,7,16,128]{3,2,1,0:T(8,128)(2,1)S(1)} collective-permute-done((bf16[8,7,16,128]{3,2,1,0:T(8,128)(2,1)S(1)}, bf16[8,7,16,128]{3,2,1,0:T(8,128)(2,1)S(1)}, u32[]{:S(2)}, u32[]{:S(2)}) %collective-permute-start.1) | collective-permute-done | bytes 229408 | tf_op jit(solution)/shard_map/ppermute | solution.py:47
  34.3 1.5 %collective-permute-done.2.p3 = bf16[8,7,16,128]{3,2,1,0:T(8,128)(2,1)S(1)} collective-permute-done((bf16[8,7,16,128]{3,2,1,0:T(8,128)(2,1)S(1)}, bf16[8,7,16,128]{3,2,1,0:T(8,128)(2,1)S(1)}, u32[]{:S(2)}, u32[]{:S(2)}) %collective-permute-start.2) | collective-permute-done | bytes 229408 | tf_op jit(solution)/shard_map/ppermute | solution.py:47
  35.8 0.1 halves.1
  35.9 1.7 %collective-permute-start.3 = (bf16[20,7,16,128]{3,2,1,0:T(8,128)(2,1)S(1)}, bf16[20,7,16,128]{3,2,1,0:T(8,128)(2,1)S(1)}, u32[]{:S(2)}, u32[]{:S(2)}) collective-permute-start(bf16[20,7,16,128]{3,2,1,0:T(8,128)(2,1)S(1)} %get-tuple-element.16.refs_0_), channel_id=1, source_target_pairs={{0,1},{1,2},{2,3},{3,0},{4,5},{5,6},{6,7},{7,4},{8,9},{9,10},{10,1... | collective-permute-start | bytes 1720328 | tf_op jit(solution)/shard_map/ppermute | solution.py:53
  37.5 1.7 %collective-permute-start.6 = (bf16[20,7,16,128]{3,2,1,0:T(8,128)(2,1)S(1)}, bf16[20,7,16,128]{3,2,1,0:T(8,128)(2,1)S(1)}, u32[]{:S(2)}, u32[]{:S(2)}) collective-permute-start(bf16[20,7,16,128]{3,2,1,0:T(8,128)(2,1)S(1)} %get-tuple-element.17.refs_1_), channel_id=1, source_target_pairs={{0,3},{1,0},{2,1},{3,2},{4,7},{5,4},{6,5},{7,6},{8,11},{9,8},{10,9... | collective-permute-start | bytes 1720328 | tf_op jit(solution)/shard_map/ppermute | solution.py:53
  39.2 0.4 collective-permute-start.4
  39.5 2.9 %collective-permute-start.5 = (bf16[20,7,16,128]{3,2,1,0:T(8,128)(2,1)S(1)}, bf16[20,7,16,128]{3,2,1,0:T(8,128)(2,1)S(1)}, u32[]{:S(2)}, u32[]{:S(2)}) collective-permute-start(bf16[20,7,16,128]{3,2,1,0:T(8,128)(2,1)S(1)} %get-tuple-element.16.refs_0_), channel_id=1, source_target_pairs={{0,3},{1,0},{2,1},{3,2},{4,7},{5,4},{6,5},{7,6},{8,11},{9,8},{10,9... | collective-permute-start | bytes 1720328 | tf_op jit(solution)/shard_map/ppermute | solution.py:53
  42.4 0.0 collective-permute-start.12
  42.4 4.4 %collective-permute-done.3.refs_2_ = bf16[20,7,16,128]{3,2,1,0:T(8,128)(2,1)S(1)} collective-permute-done((bf16[20,7,16,128]{3,2,1,0:T(8,128)(2,1)S(1)}, bf16[20,7,16,128]{3,2,1,0:T(8,128)(2,1)S(1)}, u32[]{:S(2)}, u32[]{:S(2)}) %collective-permute-start.3) | collective-permute-done | bytes 573472 | tf_op jit(solution)/shard_map/ppermute | solution.py:53
  46.9 0.0 collective-permute-start.13
  46.9 0.4 collective-permute-done.6.refs_5_
  47.2 1.7 %collective-permute-start.7 = (bf16[20,7,16,128]{3,2,1,0:T(8,128)(2,1)S(1)}, bf16[20,7,16,128]{3,2,1,0:T(8,128)(2,1)S(1)}, u32[]{:S(2)}, u32[]{:S(2)}) collective-permute-start(bf16[20,7,16,128]{3,2,1,0:T(8,128)(2,1)S(1)} %collective-permute-done.3.refs_2_), channel_id=1, source_target_pairs={{0,1},{1,2},{2,3},{3,0},{4,5},{5,6},{6,7},{7,4},{8,9},{9,10},{10,1... | collective-permute-start | bytes 1720328 | tf_op jit(solution)/shard_map/ppermute | solution.py:53
  48.9 4.1 %collective-permute-done.4.refs_3_ = bf16[20,7,16,128]{3,2,1,0:T(8,128)(2,1)S(1)} collective-permute-done((bf16[20,7,16,128]{3,2,1,0:T(8,128)(2,1)S(1)}, bf16[20,7,16,128]{3,2,1,0:T(8,128)(2,1)S(1)}, u32[]{:S(2)}, u32[]{:S(2)}) %collective-permute-start.4) | collective-permute-done | bytes 573472 | tf_op jit(solution)/shard_map/ppermute | solution.py:53
  53.0 1.8 %collective-permute-start.8 = (bf16[20,7,16,128]{3,2,1,0:T(8,128)(2,1)S(1)}, bf16[20,7,16,128]{3,2,1,0:T(8,128)(2,1)S(1)}, u32[]{:S(2)}, u32[]{:S(2)}) collective-permute-start(bf16[20,7,16,128]{3,2,1,0:T(8,128)(2,1)S(1)} %collective-permute-done.6.refs_5_), channel_id=1, source_target_pairs={{0,3},{1,0},{2,1},{3,2},{4,7},{5,4},{6,5},{7,6},{8,11},{9,8},{10,9... | collective-permute-start | bytes 1720328 | tf_op jit(solution)/shard_map/ppermute | solution.py:53
  54.8 0.0 collective-permute-done.5.refs_4_
  54.8 0.0 collective-permute-start.14
  54.8 0.0 collective-permute-done.12.refs_8_
  54.8 0.5 collective-permute-start.17
  55.3 0.0 collective-permute-done.13.refs_9_
  55.3 0.1 collective-permute-start.15
  55.4 3.7 %collective-permute-done.7.refs_6_ = bf16[20,7,16,128]{3,2,1,0:T(8,128)(2,1)S(1)} collective-permute-done((bf16[20,7,16,128]{3,2,1,0:T(8,128)(2,1)S(1)}, bf16[20,7,16,128]{3,2,1,0:T(8,128)(2,1)S(1)}, u32[]{:S(2)}, u32[]{:S(2)}) %collective-permute-start.7) | collective-permute-done | bytes 573472 | tf_op jit(solution)/shard_map/ppermute | solution.py:53
  59.1 0.0 collective-permute-start.16
  59.1 3.6 %collective-permute-done.8.refs_7_ = bf16[20,7,16,128]{3,2,1,0:T(8,128)(2,1)S(1)} collective-permute-done((bf16[20,7,16,128]{3,2,1,0:T(8,128)(2,1)S(1)}, bf16[20,7,16,128]{3,2,1,0:T(8,128)(2,1)S(1)}, u32[]{:S(2)}, u32[]{:S(2)}) %collective-permute-start.8) | collective-permute-done | bytes 573472 | tf_op jit(solution)/shard_map/ppermute | solution.py:53
  62.7 0.0 collective-permute-start.18
  62.7 0.0 collective-permute-done.14.refs_10_
  62.7 0.5 collective-permute-start.19
  63.2 0.0 copy-start
  63.3 1.0 temporal_blocks.1.refs_0_
  64.2 0.0 collective-permute-done.17.refs_13_
  64.3 2.2 %collective-permute-start.10 = (bf16[32,7,16,128]{3,2,1,0:T(8,128)(2,1)}, bf16[32,7,16,128]{3,2,1,0:T(8,128)(2,1)S(1)}, u32[]{:S(2)}, u32[]{:S(2)}) collective-permute-start(bf16[32,7,16,128]{3,2,1,0:T(8,128)(2,1)} %temporal_blocks.1.refs_0_), channel_id=1, source_target_pairs={{0,96},{1,97},{2,98},{3,99},{4,100},{5,101},{6,102},{7,103},{8,104... | collective-permute-start | bytes 2752520 | tf_op jit(solution)/shard_map/ppermute | solution.py:47
  66.4 0.0 collective-permute-done.15.refs_11_
  66.4 1.2 collective-permute-start.11
  67.7 0.0 collective-permute-done.16.refs_12_
  67.7 0.1 collective-permute-start.9
  67.7 0.0 collective-permute-done.18.refs_14_
  67.7 0.0 collective-permute-done.19.refs_15_
  67.7 5.6 %spatial.1 = (bf16[128,1280]{1,0:T(8,128)(2,1)S(1)}, bf16[128,5,2,128]{3,2,1,0:T(2,128)(2,1)}) custom-call(bf16[20,7,16,128]{3,2,1,0:T(8,128)(2,1)S(1)} %get-tuple-element.16.refs_0_, bf16[20,7,16,128]{3,2,1,0:T(8,128)(2,1)S(1)} %get-tuple-element.17.refs_1_, bf16[20,7,16,128]{3,2,1,0:T(8,128)(2,1)S(1)} %collective-permute-done.3.refs_2_, ...), custom_call_target="tpu_custom_call" | custom-call | flops 8999999488 | bytes 10168320 | tf_op jit(solution)/shard_map/spatial/pallas_call | solution.py:374
  73.3 9.7 %all-to-all-start.1 = ((bf16[128,5,2,128]{3,2,1,0:T(2,128)(2,1)}), bf16[128,5,2,128]{3,2,1,0:T(2,128)(2,1)S(1)}, u32[]{:S(2)}, u32[]{:S(2)}) async-start(bf16[128,5,2,128]{3,2,1,0:T(2,128)(2,1)} %get-tuple-element.18), calls=%async_computation.1 | async-start | bytes 655360 | tf_op jit(solution)/shard_map/all_to_all | solution.py:431
  83.0 0.1 collective-permute-start.20
  83.1 7.6 %collective-permute-done.10.refs_1_ = bf16[32,7,16,128]{3,2,1,0:T(8,128)(2,1)S(1)} collective-permute-done((bf16[32,7,16,128]{3,2,1,0:T(8,128)(2,1)}, bf16[32,7,16,128]{3,2,1,0:T(8,128)(2,1)S(1)}, u32[]{:S(2)}, u32[]{:S(2)}) %collective-permute-start.10) | collective-permute-done | bytes 917536 | tf_op jit(solution)/shard_map/ppermute | solution.py:47
  90.7 0.0 collective-permute-done.11.refs_2_
  90.7 3.8 %collective-permute-done.9.refs_0_ = bf16[32,7,16,128]{3,2,1,0:T(8,128)(2,1)S(1)} collective-permute-done((bf16[32,7,16,128]{3,2,1,0:T(8,128)(2,1)}, bf16[32,7,16,128]{3,2,1,0:T(8,128)(2,1)S(1)}, u32[]{:S(2)}, u32[]{:S(2)}) %collective-permute-start.9) | collective-permute-done | bytes 917536 | tf_op jit(solution)/shard_map/ppermute | solution.py:47
  94.5 2.8 %all-to-all-done.1.refs_3_.refs_4_.refs_5_ = bf16[128,5,2,128]{3,2,1,0:T(2,128)(2,1)S(1)} async-done(((bf16[128,5,2,128]{3,2,1,0:T(2,128)(2,1)}), bf16[128,5,2,128]{3,2,1,0:T(2,128)(2,1)S(1)}, u32[]{:S(2)}, u32[]{:S(2)}) %all-to-all-start.1) | async-done | bytes 327712 | tf_op jit(solution)/shard_map/all_to_all | solution.py:431
  97.3 0.0 collective-permute-start.21
  97.3 0.5 collective-permute-start.22
  97.8 0.0 collective-permute-start.23
  97.8 2.4 %half.1 = (f32[2048,128]{1,0:T(8,128)S(1)}, bf16[128,2,16,128]{3,2,1,0:T(8,128)(2,1)S(1)}) custom-call(bf16[32,7,16,128]{3,2,1,0:T(8,128)(2,1)} %temporal_blocks.1.refs_0_, bf16[32,7,16,128]{3,2,1,0:T(8,128)(2,1)S(1)} %get-tuple-element.19.refs_1_, bf16[32,7,16,128]{3,2,1,0:T(8,128)(2,1)S(1)} %get-tuple-element.20.refs_2_, ...), custom_call_target="tpu_custom_call" | custom-call | flops 3000000000 | bytes 5570560 | tf_op jit(solution)/shard_map/half/pallas_call | solution.py:374
  100.2 1.0 copy-done.1
  101.2 0.0 collective-permute-done.20.refs_0_
  101.2 0.0 collective-permute-done.22.refs_2_
  101.2 1.2 collective-permute-done.23.refs_3_
  102.4 3.9 %temporal.1 = (bf16[128,3,2,128]{3,2,1,0:T(2,128)(2,1)}, bf16[128,2,16,128]{3,2,1,0:T(8,128)(2,1)S(1)}) custom-call(bf16[32,7,16,128]{3,2,1,0:T(8,128)(2,1)} %collective-permute-done.20.refs_0_, bf16[32,7,16,128]{3,2,1,0:T(8,128)(2,1)S(1)} %collective-permute-done.21.refs_1_, bf16[32,7,16,128]{3,2,1,0:T(8,128)(2,1)S(1)} %collective-permute-done.22.refs_2_, ...), custom_call_target="tpu_custom_call" | custom-call | flops 5000000000 | bytes 6291456 | tf_op jit(solution)/shard_map/temporal/pallas_call | solution.py:374
  106.3 1.0 copy-done.3
  107.3 6.7 %all-to-all-start.2 = ((bf16[128,3,2,128]{3,2,1,0:T(2,128)(2,1)}), bf16[128,3,2,128]{3,2,1,0:T(2,128)(2,1)S(1)}, u32[]{:S(2)}, u32[]{:S(2)}) async-start(bf16[128,3,2,128]{3,2,1,0:T(2,128)(2,1)} %get-tuple-element.25), calls=%async_computation.2 | async-start | bytes 393216 | tf_op jit(solution)/shard_map/all_to_all | solution.py:470
  114.0 1.2 copy-done.4
  115.2 1.0 weights.1
  116.3 11.3 %all-to-all-done.2.attn = bf16[128,3,2,128]{3,2,1,0:T(2,128)(2,1)S(1)} async-done(((bf16[128,3,2,128]{3,2,1,0:T(2,128)(2,1)}), bf16[128,3,2,128]{3,2,1,0:T(2,128)(2,1)S(1)}, u32[]{:S(2)}, u32[]{:S(2)}) %all-to-all-start.2) | async-done | bytes 196640 | tf_op jit(solution)/shard_map/all_to_all | solution.py:470
  127.6 1.4 %mixed.1 = bf16[128,1280]{1,0:T(8,128)(2,1)} custom-call(bf16[1280,640]{1,0:T(8,128)(2,1)S(1)} %weights.1, bf16[128,3,2,128]{3,2,1,0:T(2,128)(2,1)S(1)} %all-to-all-done.2.attn, bf16[128,1280]{1,0:T(8,128)(2,1)S(1)} %get-tuple-element.26.hidden), custom_call_target="tpu_custom_call" | custom-call | flops 1000000000 | bytes 2490368 | tf_op jit(solution)/shard_map/mixed/pallas_call | solution.py:374
  (15 shorter events, 0.0 us)
Async XLA Ops:
  0.0 63.2 %copy-start.5 = (f32[1280]{0:T(1024)S(1)}, f32[1280]{0:T(1024)}, u32[]{:S(2)}) copy-start(f32[1280]{0:T(1024)} %param.10) | copy-start | bytes 15364
  0.0 63.2 %copy-start.6 = (f32[1280]{0:T(1024)S(1)}, f32[1280]{0:T(1024)}, u32[]{:S(2)}) copy-start(f32[1280]{0:T(1024)} %param.13) | copy-start | bytes 15364
  24.9 7.3 %collective-permute-start = (bf16[8,7,16,128]{3,2,1,0:T(8,128)(2,1)S(1)}, bf16[8,7,16,128]{3,2,1,0:T(8,128)(2,1)S(1)}, u32[]{:S(2)}, u32[]{:S(2)}) collective-permute-start(bf16[8,7,16,128]{3,2,1,0:T(8,128)(2,1)S(1)} %slice.4), channel_id=1, source_target_pairs={{0,32},{1,33},{2,34},{3,35},{4,36},{5,37},{6,38},{7,39},{8,40},{9,... | collective-permute-start | bytes 688136 | tf_op jit(solution)/shard_map/ppermute | solution.py:47
  26.5 7.8 %collective-permute-start.1 = (bf16[8,7,16,128]{3,2,1,0:T(8,128)(2,1)S(1)}, bf16[8,7,16,128]{3,2,1,0:T(8,128)(2,1)S(1)}, u32[]{:S(2)}, u32[]{:S(2)}) collective-permute-start(bf16[8,7,16,128]{3,2,1,0:T(8,128)(2,1)S(1)} %slice.4), channel_id=1, source_target_pairs={{0,96},{1,97},{2,98},{3,99},{4,100},{5,101},{6,102},{7,103},{8,104... | collective-permute-start | bytes 688136 | tf_op jit(solution)/shard_map/ppermute | solution.py:47
  28.3 7.5 %collective-permute-start.2 = (bf16[8,7,16,128]{3,2,1,0:T(8,128)(2,1)S(1)}, bf16[8,7,16,128]{3,2,1,0:T(8,128)(2,1)S(1)}, u32[]{:S(2)}, u32[]{:S(2)}) collective-permute-start(bf16[8,7,16,128]{3,2,1,0:T(8,128)(2,1)S(1)} %slice.4), channel_id=1, source_target_pairs={{0,64},{1,65},{2,66},{3,67},{4,68},{5,69},{6,70},{7,71},{8,72},{9,... | collective-permute-start | bytes 688136 | tf_op jit(solution)/shard_map/ppermute | solution.py:47
  35.9 11.0 %collective-permute-start.3 = (bf16[20,7,16,128]{3,2,1,0:T(8,128)(2,1)S(1)}, bf16[20,7,16,128]{3,2,1,0:T(8,128)(2,1)S(1)}, u32[]{:S(2)}, u32[]{:S(2)}) collective-permute-start(bf16[20,7,16,128]{3,2,1,0:T(8,128)(2,1)S(1)} %get-tuple-element.16.refs_0_), channel_id=1, source_target_pairs={{0,1},{1,2},{2,3},{3,0},{4,5},{5,6},{6,7},{7,4},{8,9},{9,10},{10,1... | collective-permute-start | bytes 1720328 | tf_op jit(solution)/shard_map/ppermute | solution.py:53
  37.5 9.7 %collective-permute-start.6 = (bf16[20,7,16,128]{3,2,1,0:T(8,128)(2,1)S(1)}, bf16[20,7,16,128]{3,2,1,0:T(8,128)(2,1)S(1)}, u32[]{:S(2)}, u32[]{:S(2)}) collective-permute-start(bf16[20,7,16,128]{3,2,1,0:T(8,128)(2,1)S(1)} %get-tuple-element.17.refs_1_), channel_id=1, source_target_pairs={{0,3},{1,0},{2,1},{3,2},{4,7},{5,4},{6,5},{7,6},{8,11},{9,8},{10,9... | collective-permute-start | bytes 1720328 | tf_op jit(solution)/shard_map/ppermute | solution.py:53
  39.2 13.8 %collective-permute-start.4 = (bf16[20,7,16,128]{3,2,1,0:T(8,128)(2,1)S(1)}, bf16[20,7,16,128]{3,2,1,0:T(8,128)(2,1)S(1)}, u32[]{:S(2)}, u32[]{:S(2)}) collective-permute-start(bf16[20,7,16,128]{3,2,1,0:T(8,128)(2,1)S(1)} %get-tuple-element.17.refs_1_), channel_id=1, source_target_pairs={{0,1},{1,2},{2,3},{3,0},{4,5},{5,6},{6,7},{7,4},{8,9},{9,10},{10,1... | collective-permute-start | bytes 1720328 | tf_op jit(solution)/shard_map/ppermute | solution.py:53
  39.5 15.3 %collective-permute-start.5 = (bf16[20,7,16,128]{3,2,1,0:T(8,128)(2,1)S(1)}, bf16[20,7,16,128]{3,2,1,0:T(8,128)(2,1)S(1)}, u32[]{:S(2)}, u32[]{:S(2)}) collective-permute-start(bf16[20,7,16,128]{3,2,1,0:T(8,128)(2,1)S(1)} %get-tuple-element.16.refs_0_), channel_id=1, source_target_pairs={{0,3},{1,0},{2,1},{3,2},{4,7},{5,4},{6,5},{7,6},{8,11},{9,8},{10,9... | collective-permute-start | bytes 1720328 | tf_op jit(solution)/shard_map/ppermute | solution.py:53
  42.4 12.4 %collective-permute-start.12 = (bf16[20,7,16,128]{3,2,1,0:T(8,128)(2,1)S(1)}, bf16[20,7,16,128]{3,2,1,0:T(8,128)(2,1)S(1)}, u32[]{:S(2)}, u32[]{:S(2)}) collective-permute-start(bf16[20,7,16,128]{3,2,1,0:T(8,128)(2,1)S(1)} %get-tuple-element.16.refs_0_), channel_id=1, source_target_pairs={{0,128},{1,129},{2,130},{3,131},{4,132},{5,133},{6,134},{7,135},{8... | collective-permute-start | bytes 1720328 | tf_op jit(solution)/shard_map/ppermute | solution.py:63
  46.9 8.5 %collective-permute-start.13 = (bf16[20,7,16,128]{3,2,1,0:T(8,128)(2,1)S(1)}, bf16[20,7,16,128]{3,2,1,0:T(8,128)(2,1)S(1)}, u32[]{:S(2)}, u32[]{:S(2)}) collective-permute-start(bf16[20,7,16,128]{3,2,1,0:T(8,128)(2,1)S(1)} %get-tuple-element.17.refs_1_), channel_id=1, source_target_pairs={{0,128},{1,129},{2,130},{3,131},{4,132},{5,133},{6,134},{7,135},{8... | collective-permute-start | bytes 1720328 | tf_op jit(solution)/shard_map/ppermute | solution.py:63
  47.2 11.9 %collective-permute-start.7 = (bf16[20,7,16,128]{3,2,1,0:T(8,128)(2,1)S(1)}, bf16[20,7,16,128]{3,2,1,0:T(8,128)(2,1)S(1)}, u32[]{:S(2)}, u32[]{:S(2)}) collective-permute-start(bf16[20,7,16,128]{3,2,1,0:T(8,128)(2,1)S(1)} %collective-permute-done.3.refs_2_), channel_id=1, source_target_pairs={{0,1},{1,2},{2,3},{3,0},{4,5},{5,6},{6,7},{7,4},{8,9},{9,10},{10,1... | collective-permute-start | bytes 1720328 | tf_op jit(solution)/shard_map/ppermute | solution.py:53
  53.0 9.7 %collective-permute-start.8 = (bf16[20,7,16,128]{3,2,1,0:T(8,128)(2,1)S(1)}, bf16[20,7,16,128]{3,2,1,0:T(8,128)(2,1)S(1)}, u32[]{:S(2)}, u32[]{:S(2)}) collective-permute-start(bf16[20,7,16,128]{3,2,1,0:T(8,128)(2,1)S(1)} %collective-permute-done.6.refs_5_), channel_id=1, source_target_pairs={{0,3},{1,0},{2,1},{3,2},{4,7},{5,4},{6,5},{7,6},{8,11},{9,8},{10,9... | collective-permute-start | bytes 1720328 | tf_op jit(solution)/shard_map/ppermute | solution.py:53
  54.8 7.9 %collective-permute-start.14 = (bf16[20,7,16,128]{3,2,1,0:T(8,128)(2,1)S(1)}, bf16[20,7,16,128]{3,2,1,0:T(8,128)(2,1)S(1)}, u32[]{:S(2)}, u32[]{:S(2)}) collective-permute-start(bf16[20,7,16,128]{3,2,1,0:T(8,128)(2,1)S(1)} %collective-permute-done.3.refs_2_), channel_id=1, source_target_pairs={{0,128},{1,129},{2,130},{3,131},{4,132},{5,133},{6,134},{7,135},{8... | collective-permute-start | bytes 1720328 | tf_op jit(solution)/shard_map/ppermute | solution.py:63
  54.8 9.4 %collective-permute-start.17 = (bf16[20,7,16,128]{3,2,1,0:T(8,128)(2,1)S(1)}, bf16[20,7,16,128]{3,2,1,0:T(8,128)(2,1)S(1)}, u32[]{:S(2)}, u32[]{:S(2)}) collective-permute-start(bf16[20,7,16,128]{3,2,1,0:T(8,128)(2,1)S(1)} %collective-permute-done.6.refs_5_), channel_id=1, source_target_pairs={{0,128},{1,129},{2,130},{3,131},{4,132},{5,133},{6,134},{7,135},{8... | collective-permute-start | bytes 1720328 | tf_op jit(solution)/shard_map/ppermute | solution.py:63
  55.3 11.1 %collective-permute-start.15 = (bf16[20,7,16,128]{3,2,1,0:T(8,128)(2,1)S(1)}, bf16[20,7,16,128]{3,2,1,0:T(8,128)(2,1)S(1)}, u32[]{:S(2)}, u32[]{:S(2)}) collective-permute-start(bf16[20,7,16,128]{3,2,1,0:T(8,128)(2,1)S(1)} %collective-permute-done.4.refs_3_), channel_id=1, source_target_pairs={{0,128},{1,129},{2,130},{3,131},{4,132},{5,133},{6,134},{7,135},{8... | collective-permute-start | bytes 1720328 | tf_op jit(solution)/shard_map/ppermute | solution.py:63
  59.1 8.5 %collective-permute-start.16 = (bf16[20,7,16,128]{3,2,1,0:T(8,128)(2,1)S(1)}, bf16[20,7,16,128]{3,2,1,0:T(8,128)(2,1)S(1)}, u32[]{:S(2)}, u32[]{:S(2)}) collective-permute-start(bf16[20,7,16,128]{3,2,1,0:T(8,128)(2,1)S(1)} %collective-permute-done.5.refs_4_), channel_id=1, source_target_pairs={{0,128},{1,129},{2,130},{3,131},{4,132},{5,133},{6,134},{7,135},{8... | collective-permute-start | bytes 1720328 | tf_op jit(solution)/shard_map/ppermute | solution.py:63
  62.7 5.0 %collective-permute-start.18 = (bf16[20,7,16,128]{3,2,1,0:T(8,128)(2,1)S(1)}, bf16[20,7,16,128]{3,2,1,0:T(8,128)(2,1)S(1)}, u32[]{:S(2)}, u32[]{:S(2)}) collective-permute-start(bf16[20,7,16,128]{3,2,1,0:T(8,128)(2,1)S(1)} %collective-permute-done.7.refs_6_), channel_id=1, source_target_pairs={{0,128},{1,129},{2,130},{3,131},{4,132},{5,133},{6,134},{7,135},{8... | collective-permute-start | bytes 1720328 | tf_op jit(solution)/shard_map/ppermute | solution.py:63
  62.7 5.0 %collective-permute-start.19 = (bf16[20,7,16,128]{3,2,1,0:T(8,128)(2,1)S(1)}, bf16[20,7,16,128]{3,2,1,0:T(8,128)(2,1)S(1)}, u32[]{:S(2)}, u32[]{:S(2)}) collective-permute-start(bf16[20,7,16,128]{3,2,1,0:T(8,128)(2,1)S(1)} %collective-permute-done.8.refs_7_), channel_id=1, source_target_pairs={{0,128},{1,129},{2,130},{3,131},{4,132},{5,133},{6,134},{7,135},{8... | collective-permute-start | bytes 1720328 | tf_op jit(solution)/shard_map/ppermute | solution.py:63
  63.2 4.5 %copy-start = (bf16[1,128,1280]{2,1,0:T(8,128)(2,1)S(1)}, bf16[1,128,1280]{2,1,0:T(8,128)(2,1)}, u32[]{:S(2)}) copy-start(bf16[1,128,1280]{2,1,0:T(8,128)(2,1)} %param.8) | copy-start | bytes 983044
  64.3 26.4 %collective-permute-start.10 = (bf16[32,7,16,128]{3,2,1,0:T(8,128)(2,1)}, bf16[32,7,16,128]{3,2,1,0:T(8,128)(2,1)S(1)}, u32[]{:S(2)}, u32[]{:S(2)}) collective-permute-start(bf16[32,7,16,128]{3,2,1,0:T(8,128)(2,1)} %temporal_blocks.1.refs_0_), channel_id=1, source_target_pairs={{0,96},{1,97},{2,98},{3,99},{4,100},{5,101},{6,102},{7,103},{8,104... | collective-permute-start | bytes 2752520 | tf_op jit(solution)/shard_map/ppermute | solution.py:47
  66.4 24.3 %collective-permute-start.11 = (bf16[32,7,16,128]{3,2,1,0:T(8,128)(2,1)}, bf16[32,7,16,128]{3,2,1,0:T(8,128)(2,1)S(1)}, u32[]{:S(2)}, u32[]{:S(2)}) collective-permute-start(bf16[32,7,16,128]{3,2,1,0:T(8,128)(2,1)} %temporal_blocks.1.refs_0_), channel_id=1, source_target_pairs={{0,64},{1,65},{2,66},{3,67},{4,68},{5,69},{6,70},{7,71},{8,72},{9,... | collective-permute-start | bytes 2752520 | tf_op jit(solution)/shard_map/ppermute | solution.py:47
  67.7 26.9 %collective-permute-start.9 = (bf16[32,7,16,128]{3,2,1,0:T(8,128)(2,1)}, bf16[32,7,16,128]{3,2,1,0:T(8,128)(2,1)S(1)}, u32[]{:S(2)}, u32[]{:S(2)}) collective-permute-start(bf16[32,7,16,128]{3,2,1,0:T(8,128)(2,1)} %temporal_blocks.1.refs_0_), channel_id=1, source_target_pairs={{0,32},{1,33},{2,34},{3,35},{4,36},{5,37},{6,38},{7,39},{8,40},{9,... | collective-permute-start | bytes 2752520 | tf_op jit(solution)/shard_map/ppermute | solution.py:47
  73.3 24.0 %all-to-all-start.1 = ((bf16[128,5,2,128]{3,2,1,0:T(2,128)(2,1)}), bf16[128,5,2,128]{3,2,1,0:T(2,128)(2,1)S(1)}, u32[]{:S(2)}, u32[]{:S(2)}) async-start(bf16[128,5,2,128]{3,2,1,0:T(2,128)(2,1)} %get-tuple-element.18), calls=%async_computation.1 | async-start | bytes 655360 | tf_op jit(solution)/shard_map/all_to_all | solution.py:431
  83.0 18.2 %collective-permute-start.20 = (bf16[32,7,16,128]{3,2,1,0:T(8,128)(2,1)}, bf16[32,7,16,128]{3,2,1,0:T(8,128)(2,1)}, u32[]{:S(2)}, u32[]{:S(2)}) collective-permute-start(bf16[32,7,16,128]{3,2,1,0:T(8,128)(2,1)} %temporal_blocks.1.refs_0_), channel_id=1, source_target_pairs={{0,128},{1,129},{2,130},{3,131},{4,132},{5,133},{6,134},{7,135},{8... | collective-permute-start | bytes 2752520 | tf_op jit(solution)/shard_map/ppermute | solution.py:63
  97.3 3.9 %collective-permute-start.21 = (bf16[32,7,16,128]{3,2,1,0:T(8,128)(2,1)S(1)}, bf16[32,7,16,128]{3,2,1,0:T(8,128)(2,1)S(1)}, u32[]{:S(2)}, u32[]{:S(2)}) collective-permute-start(bf16[32,7,16,128]{3,2,1,0:T(8,128)(2,1)S(1)} %get-tuple-element.19.refs_1_), channel_id=1, source_target_pairs={{0,128},{1,129},{2,130},{3,131},{4,132},{5,133},{6,134},{7,135},{8... | collective-permute-start | bytes 2752520 | tf_op jit(solution)/shard_map/ppermute | solution.py:63
  97.3 3.9 %collective-permute-start.22 = (bf16[32,7,16,128]{3,2,1,0:T(8,128)(2,1)S(1)}, bf16[32,7,16,128]{3,2,1,0:T(8,128)(2,1)S(1)}, u32[]{:S(2)}, u32[]{:S(2)}) collective-permute-start(bf16[32,7,16,128]{3,2,1,0:T(8,128)(2,1)S(1)} %get-tuple-element.20.refs_2_), channel_id=1, source_target_pairs={{0,128},{1,129},{2,130},{3,131},{4,132},{5,133},{6,134},{7,135},{8... | collective-permute-start | bytes 2752520 | tf_op jit(solution)/shard_map/ppermute | solution.py:63
  97.8 4.6 %collective-permute-start.23 = (bf16[32,7,16,128]{3,2,1,0:T(8,128)(2,1)S(1)}, bf16[32,7,16,128]{3,2,1,0:T(8,128)(2,1)S(1)}, u32[]{:S(2)}, u32[]{:S(2)}) collective-permute-start(bf16[32,7,16,128]{3,2,1,0:T(8,128)(2,1)S(1)} %get-tuple-element.21.refs_3_), channel_id=1, source_target_pairs={{0,128},{1,129},{2,130},{3,131},{4,132},{5,133},{6,134},{7,135},{8... | collective-permute-start | bytes 2752520 | tf_op jit(solution)/shard_map/ppermute | solution.py:63
  100.2 1.0 copy-start.1
  102.4 11.6 %copy-start.2 = (bf16[128,2,16,128]{3,2,1,0:T(8,128)(2,1)S(1)}, bf16[128,2,16,128]{3,2,1,0:T(8,128)(2,1)}, u32[]{:S(2)}) copy-start(bf16[128,2,16,128]{3,2,1,0:T(8,128)(2,1)} %copy-done.1) | copy-start | bytes 3145732
  106.3 1.0 copy-start.3
  107.3 20.2 %all-to-all-start.2 = ((bf16[128,3,2,128]{3,2,1,0:T(2,128)(2,1)}), bf16[128,3,2,128]{3,2,1,0:T(2,128)(2,1)S(1)}, u32[]{:S(2)}, u32[]{:S(2)}) async-start(bf16[128,3,2,128]{3,2,1,0:T(2,128)(2,1)} %get-tuple-element.25), calls=%async_computation.2 | async-start | bytes 393216 | tf_op jit(solution)/shard_map/all_to_all | solution.py:470
  114.0 1.2 copy-start.4

commit v5 on v4

--- a/solution.py
+++ b/solution.py
@@ -68,7 +68,6 @@
 
 
 ANY = pl.BlockSpec(memory_space=pl.ANY)
-HBM = pl.BlockSpec(memory_space=pltpu.HBM)
 
 
 def small(mib):
@@ -230,25 +229,26 @@
 
 def qkv_project(own, oth, acc, rows, tokens, x_core):
     c, _, _ = place()
-    xa, xb = halves(tokens, c)
+    both = jnp.concatenate(halves(tokens, c), axis=1)
     for j in range(4):
-        wa, wb = pieces_of(own, oth, j, 0, 5)
-        spread(acc, dot(wa, xa, NT) + dot(wb, xb, NT), j, 0, x_core)
+        w = jnp.concatenate(pieces_of(own, oth, j, 0, 5), axis=1)
+        spread(acc, dot(w, both, NT), j, 0, x_core)
     compact(acc, rows)
 
 
-def out_project(own, oth, acc, rows, part, dims, x_core):
+def out_project(own, oth, acc, rows, attn, x_core):
     c, _, _ = place()
-    lo, mid, hi = part(0, 256), part(256, 384), part(384, 640)
+    lo, mid, hi = attn[0:256, :], attn[256:384, :], attn[384:640, :]
+    mid = jnp.concatenate([mid, jnp.zeros_like(mid)], axis=0)
+    xa = jnp.concatenate([jnp.where(c == 0, lo, hi), mid], axis=1)
+    xb = jnp.concatenate([jnp.where(c == 0, hi, lo), mid], axis=1)
     upper = lax.rem(lax.broadcasted_iota(jnp.int32, (512, 128), 0), 16) < 10
-    xa = jnp.where(c == 0, lo, hi)
-    xb = jnp.where(c == 0, hi, lo)
     for j in range(4):
-        wa, wb = pieces_of(own, oth, j, 5, 2)
-        both = dot(wa, xa, dims) + dot(wb, xb, dims)
-        ma, mb = dot(wa[:, :128], mid, dims), dot(wb[:, :128], mid, dims)
+        wa, wb = pieces_of(own, oth, j, 0, 2)
+        ra, rb = dot(wa, xa, NN), dot(wb, xb, NN)
+        ma, mb = ra[:, 128:], rb[:, 128:]
         m0, m1 = jnp.where(c == 0, ma, mb), jnp.where(c == 0, mb, ma)
-        spread(acc, jnp.where(upper, both, m0), j, 0, x_core)
+        spread(acc, jnp.where(upper, ra[:, :128] + rb[:, :128], m0), j, 0, x_core)
         spread(acc, m1, j, 16, x_core)
     for s in range(SEQ):
         x, z, y = s // 32, (s // 4) % 8, s % 4
@@ -298,73 +298,52 @@
     tokens = jnp.concatenate([normed, reference_tokens(own, last)], axis=0)
     qkv_project(own, oth, acc, rows, tokens, 0)
     heads(rows, scores, attn)
-    part = lambda a, b: attn[a:b, :].astype(BF)
-    out_project(own, oth, acc_out, rows_out, part, NN, 0)
+    views = [[p.at[:, pl.ds(5, 2)] for p in pieces] for pieces in (own, oth)]
+    out_project(*views, acc_out, rows_out, attn[...].astype(BF), 0)
     h = (latents[...].astype(F32) + rows_out[...].T).astype(BF)
     hidden[...] = h
     to_rows(layer_norm(h.astype(F32), gain_t[...]).astype(F32), tnormed, rows_out, 10)
 
 
-def output_tiles(pieces, out, sems):
+def half_kernel(*refs):
+    own, (tokens, out, rest, wide) = refs[0:4], refs[4:]
+    c, _, _ = place()
+    xa, xb = halves(from_rows(tokens, wide, 10), c)
+    rest[...] = xb
+    for j in range(4):
+        wa = jnp.concatenate([lanes(own, j, i, 0, 5) for i in range(4)], axis=0)
+        out[512 * j : 512 * (j + 1), :] = dot(wa, xa, NT)
+
+
+def temporal_kernel(*refs):
+    oth = refs[0:4]
+    half, rest, out, acc, rows, attn, scores, wide_out = refs[4:]
+    for j in range(4):
+        wb = jnp.concatenate([lanes(oth, i, j, 0, 5) for i in range(4)], axis=0)
+        spread(acc, half[512 * j : 512 * (j + 1), :] + dot(wb, rest[...], NT), j, 0, 1)
+    compact(acc, rows)
+    heads(rows, scores, attn)
+    to_rows(attn[...].T, out, wide_out, 5)
+
+
+def mixed_kernel(*refs):
+    own, oth = refs[0:4], refs[4:8]
+    attn, hidden, mixed, acc, rows, wide, own_tiles, oth_tiles, sems = refs[8:]
     copies = [
-        pltpu.make_async_copy(p.at[:, pl.ds(5, 2)], out.at[pl.ds(32 * j, 32)], sems.at[j])
-        for j, p in enumerate(pieces)
+        pltpu.make_async_copy(src.at[:, pl.ds(5, 2)], dst, sems.at[i])
+        for i, (src, dst) in enumerate(((own[0], own_tiles), (oth[0], oth_tiles)))
     ]
     for copy in copies:
         copy.start()
-    return copies
-
-
-def half_kernel(*refs):
-    own, (tokens, out, for_out, wide, sems) = refs[0:4], refs[4:]
-    c, _, _ = place()
-    copies = output_tiles(own, for_out, sems)
-    xa, _ = halves(from_rows(tokens, wide, 10), c)
-    for j in range(4):
-        wa = jnp.concatenate([lanes(own, j, i, 0, 5) for i in range(4)], axis=0)
-        out[512 * j : 512 * (j + 1), :] = dot(wa, xa, NT)
+    a = from_rows(attn, wide, 5).astype(F32).T.astype(BF)
     for copy in copies:
         copy.wait()
-
-
-def temporal_kernel(*refs):
-    oth = refs[0:4]
-    half, tokens, out, for_out, acc, rows, attn, scores, wide, wide_out, sems = refs[4:]
-    c, _, _ = place()
-    copies = output_tiles(oth, for_out, sems)
-    _, xb = halves(from_rows(tokens, wide, 10), c)
-    for j in range(4):
-        wb = jnp.concatenate([lanes(oth, i, j, 0, 5) for i in range(4)], axis=0)
-        spread(acc, half[512 * j : 512 * (j + 1), :] + dot(wb, xb, NT), j, 0, 1)
-    compact(acc, rows)
-    heads(rows, scores, attn)
-    to_rows(attn[...].T, out, wide_out, 5)
-    for copy in copies:
-        copy.wait()
-
-
-def weights_kernel(*refs):
-    own, oth, out, acc, rows = refs
-    c, _, _ = place()
-    for j in range(4):
-        wa, wb = pieces_of([own], [oth], j, 0, 2)
-        lo = jnp.where(c == 0, wa, wb).astype(F32)
-        hi = jnp.where(c == 0, wb, wa).astype(F32)
-        spread(acc, jnp.concatenate([lo, hi], axis=1), j, 0, 1)
-    for s in range(SEQ):
-        x, z, y = s // 32, (s // 4) % 8, s % 4
-        at = slice(10 * s, 10 * s + 10)
-        rows[at, 0:256] = acc[x, z, y, 0:10, 0:256]
-        rows[at, 384:640] = acc[x, z, y, 0:10, 256:512]
-        rows[at, 256:384] = jnp.concatenate(
-            [acc[x, z, y, 10:15, 0:128], acc[x, z, y, 10:15, 256:384]], axis=0
-        )
-    out[...] = rows[...].astype(BF)
-
-
-def mixed_kernel(weights, attn, hidden, mixed, wide):
-    a = from_rows(attn, wide, 5)
-    mixed[...] = (hidden[...].astype(F32) + dot(a, weights[...], NT)).astype(BF)
+    views = [
+        [first] + [p.at[:, pl.ds(5, 2)] for p in rest]
+        for first, rest in ((own_tiles, own[1:]), (oth_tiles, oth[1:]))
+    ]
+    out_project(*views, acc, rows, a, 1)
+    mixed[...] = (hidden[...].astype(F32) + rows[...].T).astype(BF)
 
 
 def call(kernel, args, outs, scratch, name, flops, mib, dtypes=(BF, BF)):
@@ -375,8 +354,8 @@
         kernel,
         out_shape=shapes[0] if single else shapes,
         in_specs=vmem(len(args)),
-        out_specs=vmem(1)[0] if single else [HBM if s == (SEQ, 2, 16, 128) else vmem(1)[0] for s in outs],
-        scratch_shapes=[pltpu.VMEM(s, F32) if isinstance(s, tuple) else s for s in scratch],
+        out_specs=vmem(1)[0] if single else vmem(len(shapes)),
+        scratch_shapes=[pltpu.VMEM(s, F32) for s in scratch],
         compiler_params=small(mib),
         cost_estimate=pl.CostEstimate(flops=flops, bytes_accessed=size, transcendentals=0),
         name=name,
@@ -431,52 +410,49 @@
     tokens = lax.all_to_all(tnormed, "seq", 0, 0, tiled=True)
     own_t = ring_t[:1] + gate(ring_t[1:], tokens)
     oth_t = [swap(ring_t[0])] + [swap(b) for b in own_t[1:]]
-    half_t, own_u = call(
+    half_t, rest = call(
         half_kernel,
         own_t + [tokens],
-        [(2048, 128), (SEQ, 2, 16, 128)],
-        [(D, 128), pltpu.SemaphoreType.DMA((4,))],
+        [(2048, 128), (PIX, INNER)],
+        [(D, 128)],
         "half",
         3 * 10**9,
         16,
         [F32, BF],
     )
-    tattn, oth_u = call(
+    tattn = call(
         temporal_kernel,
-        oth_t + [half_t, tokens],
-        [(PIX, 3, 2, 128), (SEQ, 2, 16, 128)],
+        oth_t + [half_t, rest],
+        [(PIX, 3, 2, 128)],
         [
             (NX, NZ, NY, 16, 128),
             (1920, 128),
             (INNER, 128),
             (HEADS, 128, 128),
-            (D, 128),
             (768, 128),
-            pltpu.SemaphoreType.DMA((4,)),
         ],
         "temporal",
         5 * 10**9,
         16,
     )
-    weights_u = call(
-        weights_kernel,
-        [own_u, oth_u],
-        [(D, INNER)],
-        [(NX, NZ, NY, 16, 512), (D, INNER)],
-        "weights",
-        3 * 10**9,
-        16,
-    )
     back = lax.all_to_all(tattn, "seq", 0, 0, tiled=True)
-    mixed = call(
+    mixed = pl.pallas_call(
         mixed_kernel,
-        [weights_u, back, hidden],
-        [(PIX, D)],
-        [(768, 128)],
-        "mixed",
-        10**9,
-        8,
-    )
+        out_shape=jax.ShapeDtypeStruct((PIX, D), BF),
+        in_specs=([ANY] + vmem(3)) * 2 + vmem(2),
+        out_specs=vmem(1)[0],
+        scratch_shapes=[
+            pltpu.VMEM((NX, NZ, NY, 32, 128), F32),
+            pltpu.VMEM((D, 128), F32),
+            pltpu.VMEM((768, 128), F32),
+            pltpu.VMEM((32, 2, 16, 128), BF),
+            pltpu.VMEM((32, 2, 16, 128), BF),
+            pltpu.SemaphoreType.DMA((2,)),
+        ],
+        compiler_params=small(16),
+        cost_estimate=pl.CostEstimate(flops=3 * 10**9, bytes_accessed=10**7, transcendentals=0),
+        name="mixed",
+    )(*own_t, *oth_t, back, hidden)
     return mixed.reshape(1, PIX, D)
 
 

time: 130 us -> 129 us (level)
  blocking collectives: 23.2 us -> 42.9 us
  waiting for transfers between devices: 48.5 us -> 40 us
  starting transfers between devices: 36.8 us -> 29.7 us
  local copies, waits for them, and re-layouts: 3.2 us -> 0.04 us
  Pallas kernels: 17.1 us -> 15.8 us
    all_to_all x0 -> x1, blocking collectives: none -> 19.7 us  [body(): back = lax.all_to_all(tattn, 'seq', 0, 0, tiled=True)]
    all_to_all x1 -> x0, waiting for transfers between devices: 11.3 us -> none  [body(): back = lax.all_to_all(tattn, 'seq', 0, 0, tiled=True)]
    all_to_all x1 -> x0, starting transfers between devices: 6.68 us -> none  [body(): back = lax.all_to_all(tattn, 'seq', 0, 0, tiled=True)]
    pallas_call x5 -> x3, Pallas kernels: 14.3 us -> 10.1 us  [call(): pl.pallas_call(kernel, out_shape=shapes[0] if single else shapes, in_spec...]
    unnamed x14 -> x6, local copies, waits for them, and re-layouts: 3.18 us -> 0.02 us
    pallas_call x0 -> x1, Pallas kernels: none -> 2.94 us  [body(): pl.pallas_call(mixed_kernel, out_shape=jax.ShapeDtypeStruct((PIX, D), BF)...]
    all_to_all x1, waiting for transfers between devices: 2.77 us -> 5.45 us  [body(): tokens = lax.all_to_all(tnormed, 'seq', 0, 0, tiled=True)]
    ppermute x6, waiting for transfers between devices: 17.1 us -> 15.5 us  [ring(): lax.ppermute(block, ('clip', 'seq'), ring_perm(k, stage))]
  transfers between devices with their start and end apart: 26 -> 25, of which waited for: 13 -> 13; matrix products, arithmetic and copies ran while one was open for 0% -> 0% of each run, Pallas kernels for 8% -> 6%
where the time goes in v5:
time: 129 us
  blocking collectives  42.9 us (33%)
  waiting for transfers between devices  40 us (31%)
  starting transfers between devices  29.7 us (23%)
  Pallas kernels  15.8 us (12%)
    all_to_all x1, blocking collectives, body(): lax.all_to_all(packed, 'seq', 0, 0, axis_index_groups=Z_GROUPS, tiled=True)  23.2 us
    all_to_all x1, blocking collectives, body(): back = lax.all_to_all(tattn, 'seq', 0, 0, tiled=True)  19.7 us
    ppermute x6, waiting for transfers between devices, shift(): return lax.ppermute(part, ('clip', 'seq'), ring_perm(k, stage))  16.7 us
    ppermute x6, waiting for transfers between devices, ring(): lax.ppermute(block, ('clip', 'seq'), ring_perm(k, stage))  15.5 us
    pallas_call x3, Pallas kernels, call(): pl.pallas_call(kernel, out_shape=shapes[0] if single else shapes, in_spec...  10.1 us
    ppermute x6, starting transfers between devices, shift(): return lax.ppermute(part, ('clip', 'seq'), ring_perm(k, stage))  10 us
    all_to_all x1, starting transfers between devices, body(): tokens = lax.all_to_all(tnormed, 'seq', 0, 0, tiled=True)  9.6 us
    ppermute x6, starting transfers between devices, ring(): lax.ppermute(block, ('clip', 'seq'), ring_perm(k, stage))  8.77 us
  transfers between devices with their start and end apart: 25, of which 13 were waited for; matrix products, arithmetic and copies ran while one was open for 0% of the time, Pallas kernels for 6%

profile of v5, /device:TPU:32, one launch (start us, length us, event | category | flops | bytes accessed | tf_op | source)
XLA Modules:
  0.0 128.8 jit_solution(11650079791973254156)
XLA Ops:
  0.0 1.7 %pack.1 = bf16[8,14,16,128]{3,2,1,0:T(8,128)(2,1)} custom-call(bf16[15,1280]{1,0:T(8,128)(2,1)} %bitcast.7, bf16[1,1280]{1,0:T(2,128)(2,1)} %ref_in.1, bf16[10,640]{1,0:T(8,128)(2,1)} %bitcast.9, bf16[15,1280]{1,0:T(8,128)(2,1)} %bitcast.8, bf16[10,640]{1,0:T(8,128)(2,1)} %bitcast.10), custom_call_target="tpu_custom_call" | custom-call | tf_op jit(solution)/shard_map/pack/pallas_call | solution.py:370
  1.7 23.2 %all_to_all.15.along_z = bf16[8,14,16,128]{3,2,1,0:T(8,128)(2,1)S(1)} all-to-all(bf16[8,14,16,128]{3,2,1,0:T(8,128)(2,1)} %pack.1), channel_id=1, replica_groups={{0,4,8,12,16,20,24,28},{1,5,9,13,17,21,25,29},{2,6,10,14,18,22,26,30},{..., dimensions={0} | all-to-all | bytes 917504 | tf_op jit(solution)/shard_map/all_to_all | solution.py:379
  24.9 3.1 %collective-permute-start.2 = (bf16[8,7,16,128]{3,2,1,0:T(8,128)(2,1)S(1)}, bf16[8,7,16,128]{3,2,1,0:T(8,128)(2,1)S(1)}, u32[]{:S(2)}, u32[]{:S(2)}) collective-permute-start(bf16[8,7,16,128]{3,2,1,0:T(8,128)(2,1)S(1)} %slice.4), channel_id=1, source_target_pairs={{0,64},{1,65},{2,66},{3,67},{4,68},{5,69},{6,70},{7,71},{8,72},{9,... | collective-permute-start | bytes 688136 | tf_op jit(solution)/shard_map/ppermute | solution.py:47
  28.0 1.1 collective-permute-start.1
  29.2 0.9 collective-permute-start
  30.1 2.5 %collective-permute-done.2.p3 = bf16[8,7,16,128]{3,2,1,0:T(8,128)(2,1)S(1)} collective-permute-done((bf16[8,7,16,128]{3,2,1,0:T(8,128)(2,1)S(1)}, bf16[8,7,16,128]{3,2,1,0:T(8,128)(2,1)S(1)}, u32[]{:S(2)}, u32[]{:S(2)}) %collective-permute-start.2) | collective-permute-done | bytes 229408 | tf_op jit(solution)/shard_map/ppermute | solution.py:47
  32.5 2.5 %collective-permute-done.1.p2 = bf16[8,7,16,128]{3,2,1,0:T(8,128)(2,1)S(1)} collective-permute-done((bf16[8,7,16,128]{3,2,1,0:T(8,128)(2,1)S(1)}, bf16[8,7,16,128]{3,2,1,0:T(8,128)(2,1)S(1)}, u32[]{:S(2)}, u32[]{:S(2)}) %collective-permute-start.1) | collective-permute-done | bytes 229408 | tf_op jit(solution)/shard_map/ppermute | solution.py:47
  35.1 1.3 %collective-permute-done.p1 = bf16[8,7,16,128]{3,2,1,0:T(8,128)(2,1)S(1)} collective-permute-done((bf16[8,7,16,128]{3,2,1,0:T(8,128)(2,1)S(1)}, bf16[8,7,16,128]{3,2,1,0:T(8,128)(2,1)S(1)}, u32[]{:S(2)}, u32[]{:S(2)}) %collective-permute-start) | collective-permute-done | bytes 229408 | tf_op jit(solution)/shard_map/ppermute | solution.py:47
  36.4 0.1 halves.1
  36.5 0.0 copy-start.2
  36.5 0.1 collective-permute-start.12
  36.6 3.1 %collective-permute-start.5 = (bf16[20,7,16,128]{3,2,1,0:T(8,128)(2,1)S(1)}, bf16[20,7,16,128]{3,2,1,0:T(8,128)(2,1)S(1)}, u32[]{:S(2)}, u32[]{:S(2)}) collective-permute-start(bf16[20,7,16,128]{3,2,1,0:T(8,128)(2,1)S(1)} %get-tuple-element.14.refs_0_), channel_id=1, source_target_pairs={{0,3},{1,0},{2,1},{3,2},{4,7},{5,4},{6,5},{7,6},{8,11},{9,8},{10,9... | collective-permute-start | bytes 1720328 | tf_op jit(solution)/shard_map/ppermute | solution.py:53
  39.7 0.0 collective-permute-start.3
  39.7 3.2 %collective-permute-start.6 = (bf16[20,7,16,128]{3,2,1,0:T(8,128)(2,1)S(1)}, bf16[20,7,16,128]{3,2,1,0:T(8,128)(2,1)S(1)}, u32[]{:S(2)}, u32[]{:S(2)}) collective-permute-start(bf16[20,7,16,128]{3,2,1,0:T(8,128)(2,1)S(1)} %get-tuple-element.15.refs_1_), channel_id=1, source_target_pairs={{0,3},{1,0},{2,1},{3,2},{4,7},{5,4},{6,5},{7,6},{8,11},{9,8},{10,9... | collective-permute-start | bytes 1720328 | tf_op jit(solution)/shard_map/ppermute | solution.py:53
  42.9 0.0 collective-permute-start.13
  42.9 0.0 collective-permute-done.12.refs_8_
  42.9 0.0 collective-permute-start.4
  42.9 4.0 %collective-permute-done.5.refs_4_ = bf16[20,7,16,128]{3,2,1,0:T(8,128)(2,1)S(1)} collective-permute-done((bf16[20,7,16,128]{3,2,1,0:T(8,128)(2,1)S(1)}, bf16[20,7,16,128]{3,2,1,0:T(8,128)(2,1)S(1)}, u32[]{:S(2)}, u32[]{:S(2)}) %collective-permute-start.5) | collective-permute-done | bytes 573472 | tf_op jit(solution)/shard_map/ppermute | solution.py:53
  46.9 0.0 collective-permute-start.16
  46.9 3.7 %collective-permute-done.3.refs_2_ = bf16[20,7,16,128]{3,2,1,0:T(8,128)(2,1)S(1)} collective-permute-done((bf16[20,7,16,128]{3,2,1,0:T(8,128)(2,1)S(1)}, bf16[20,7,16,128]{3,2,1,0:T(8,128)(2,1)S(1)}, u32[]{:S(2)}, u32[]{:S(2)}) %collective-permute-start.3) | collective-permute-done | bytes 573472 | tf_op jit(solution)/shard_map/ppermute | solution.py:53
  50.6 0.0 collective-permute-start.7
  50.6 2.4 %collective-permute-done.6.refs_5_ = bf16[20,7,16,128]{3,2,1,0:T(8,128)(2,1)S(1)} collective-permute-done((bf16[20,7,16,128]{3,2,1,0:T(8,128)(2,1)S(1)}, bf16[20,7,16,128]{3,2,1,0:T(8,128)(2,1)S(1)}, u32[]{:S(2)}, u32[]{:S(2)}) %collective-permute-start.6) | collective-permute-done | bytes 573472 | tf_op jit(solution)/shard_map/ppermute | solution.py:53
  53.1 3.7 %collective-permute-start.8 = (bf16[20,7,16,128]{3,2,1,0:T(8,128)(2,1)S(1)}, bf16[20,7,16,128]{3,2,1,0:T(8,128)(2,1)S(1)}, u32[]{:S(2)}, u32[]{:S(2)}) collective-permute-start(bf16[20,7,16,128]{3,2,1,0:T(8,128)(2,1)S(1)} %collective-permute-done.6.refs_5_), channel_id=1, source_target_pairs={{0,3},{1,0},{2,1},{3,2},{4,7},{5,4},{6,5},{7,6},{8,11},{9,8},{10,9... | collective-permute-start | bytes 1720328 | tf_op jit(solution)/shard_map/ppermute | solution.py:53
  56.8 0.0 collective-permute-done.13.refs_9_
  56.8 0.0 collective-permute-start.14
  56.8 0.0 collective-permute-done.4.refs_3_
  56.8 0.5 collective-permute-start.17
  57.3 0.0 collective-permute-done.16.refs_12_
  57.3 0.1 collective-permute-start.15
  57.4 5.5 %collective-permute-done.7.refs_6_ = bf16[20,7,16,128]{3,2,1,0:T(8,128)(2,1)S(1)} collective-permute-done((bf16[20,7,16,128]{3,2,1,0:T(8,128)(2,1)S(1)}, bf16[20,7,16,128]{3,2,1,0:T(8,128)(2,1)S(1)}, u32[]{:S(2)}, u32[]{:S(2)}) %collective-permute-start.7) | collective-permute-done | bytes 573472 | tf_op jit(solution)/shard_map/ppermute | solution.py:53
  62.9 0.0 collective-permute-start.18
  62.9 1.1 collective-permute-done.8.refs_7_
  64.0 0.0 collective-permute-start.19
  64.0 0.0 copy-done.1
  64.0 0.0 copy-done.2
  64.0 0.0 copy-start
  64.0 1.0 temporal_blocks.1.refs_0_
  65.0 0.0 collective-permute-done.14.refs_10_
  65.0 1.6 %collective-permute-start.11 = (bf16[32,7,16,128]{3,2,1,0:T(8,128)(2,1)}, bf16[32,7,16,128]{3,2,1,0:T(8,128)(2,1)S(1)}, u32[]{:S(2)}, u32[]{:S(2)}) collective-permute-start(bf16[32,7,16,128]{3,2,1,0:T(8,128)(2,1)} %temporal_blocks.1.refs_0_), channel_id=1, source_target_pairs={{0,64},{1,65},{2,66},{3,67},{4,68},{5,69},{6,70},{7,71},{8,72},{9,... | collective-permute-start | bytes 2752520 | tf_op jit(solution)/shard_map/ppermute | solution.py:47
  66.6 0.0 collective-permute-done.17.refs_13_
  66.6 1.2 collective-permute-start.10
  67.8 0.0 collective-permute-done.15.refs_11_
  67.8 0.9 collective-permute-start.9
  68.7 0.0 collective-permute-done.18.refs_14_
  68.7 0.0 collective-permute-done.19.refs_15_
  68.7 0.0 copy-done
  68.7 5.0 %spatial.1 = (bf16[128,1280]{1,0:T(8,128)(2,1)S(1)}, bf16[128,5,2,128]{3,2,1,0:T(2,128)(2,1)}) custom-call(bf16[20,7,16,128]{3,2,1,0:T(8,128)(2,1)S(1)} %get-tuple-element.14.refs_0_, bf16[20,7,16,128]{3,2,1,0:T(8,128)(2,1)S(1)} %get-tuple-element.15.refs_1_, bf16[20,7,16,128]{3,2,1,0:T(8,128)(2,1)S(1)} %collective-permute-done.3.refs_2_, ...), custom_call_target="tpu_custom_call" | custom-call | flops 8999999488 | bytes 10168320 | tf_op jit(solution)/shard_map/spatial/pallas_call | solution.py:353
  73.7 9.6 %all-to-all-start.1 = ((bf16[128,5,2,128]{3,2,1,0:T(2,128)(2,1)}), bf16[128,5,2,128]{3,2,1,0:T(2,128)(2,1)S(1)}, u32[]{:S(2)}, u32[]{:S(2)}) async-start(bf16[128,5,2,128]{3,2,1,0:T(2,128)(2,1)} %get-tuple-element.16), calls=%async_computation.1 | async-start | bytes 655360 | tf_op jit(solution)/shard_map/all_to_all | solution.py:410
  83.3 0.1 collective-permute-start.20
  83.4 0.0 collective-permute-done.11.refs_2_
  83.4 8.0 %collective-permute-done.10.refs_1_ = bf16[32,7,16,128]{3,2,1,0:T(8,128)(2,1)S(1)} collective-permute-done((bf16[32,7,16,128]{3,2,1,0:T(8,128)(2,1)}, bf16[32,7,16,128]{3,2,1,0:T(8,128)(2,1)S(1)}, u32[]{:S(2)}, u32[]{:S(2)}) %collective-permute-start.10) | collective-permute-done | bytes 917536 | tf_op jit(solution)/shard_map/ppermute | solution.py:47
  91.4 1.2 collective-permute-done.9.refs_0_
  92.6 5.5 %all-to-all-done.1.refs_3_.refs_4_ = bf16[128,5,2,128]{3,2,1,0:T(2,128)(2,1)S(1)} async-done(((bf16[128,5,2,128]{3,2,1,0:T(2,128)(2,1)}), bf16[128,5,2,128]{3,2,1,0:T(2,128)(2,1)S(1)}, u32[]{:S(2)}, u32[]{:S(2)}) %all-to-all-start.1) | async-done | bytes 327712 | tf_op jit(solution)/shard_map/all_to_all | solution.py:410
  98.0 0.0 collective-permute-start.21
  98.0 0.5 collective-permute-start.22
  98.5 0.0 collective-permute-start.23
  98.5 2.3 %half.1 = (f32[2048,128]{1,0:T(8,128)S(1)}, bf16[128,640]{1,0:T(8,128)(2,1)S(1)}) custom-call(bf16[32,7,16,128]{3,2,1,0:T(8,128)(2,1)} %temporal_blocks.1.refs_0_, bf16[32,7,16,128]{3,2,1,0:T(8,128)(2,1)S(1)} %get-tuple-element.17.refs_1_, bf16[32,7,16,128]{3,2,1,0:T(8,128)(2,1)S(1)} %get-tuple-element.18.refs_2_, ...), custom_call_target="tpu_custom_call" | custom-call | flops 3000000000 | bytes 4685824 | tf_op jit(solution)/shard_map/half/pallas_call | solution.py:353
  100.8 0.0 collective-permute-done.20.refs_0_.refs_4_
  100.8 0.0 collective-permute-done.21.refs_1_.refs_5_
  100.8 1.0 collective-permute-done.22.refs_2_.refs_6_
  101.8 1.3 %collective-permute-done.23.refs_3_.refs_7_ = bf16[32,7,16,128]{3,2,1,0:T(8,128)(2,1)S(1)} collective-permute-done((bf16[32,7,16,128]{3,2,1,0:T(8,128)(2,1)S(1)}, bf16[32,7,16,128]{3,2,1,0:T(8,128)(2,1)S(1)}, u32[]{:S(2)}, u32[]{:S(2)}) %collective-permute-start.23) | collective-permute-done | bytes 917536 | tf_op jit(solution)/shard_map/ppermute | solution.py:63
  103.1 2.8 %temporal.1 = bf16[128,3,2,128]{3,2,1,0:T(2,128)(2,1)S(1)} custom-call(bf16[32,7,16,128]{3,2,1,0:T(8,128)(2,1)} %collective-permute-done.20.refs_0_.refs_4_, bf16[32,7,16,128]{3,2,1,0:T(8,128)(2,1)S(1)} %collective-permute-done.21.refs_1_.refs_5_, bf16[32,7,16,128]{3,2,1,0:T(8,128)(2,1)S(1)} %collective-permute-done.22.refs_2_.refs_6_, ...), custom_call_target="tpu_custom_call" | custom-call | flops 5000000000 | bytes 5079040 | tf_op jit(solution)/shard_map/temporal/pallas_call | solution.py:353
  105.9 19.7 %all_to_all.16.refs_8_ = bf16[128,3,2,128]{3,2,1,0:T(2,128)(2,1)S(1)} all-to-all(bf16[128,3,2,128]{3,2,1,0:T(2,128)(2,1)S(1)} %temporal.1), channel_id=1, replica_groups=mesh['clip'=2,'seq'=128] {'seq'}, dimensions={0} | all-to-all | bytes 393216 | tf_op jit(solution)/shard_map/all_to_all | solution.py:438
  125.7 2.9 %mixed.1 = bf16[128,1280]{1,0:T(8,128)(2,1)} custom-call(bf16[32,7,16,128]{3,2,1,0:T(8,128)(2,1)} %temporal_blocks.1.refs_0_, bf16[32,7,16,128]{3,2,1,0:T(8,128)(2,1)S(1)} %get-tuple-element.17.refs_1_, bf16[32,7,16,128]{3,2,1,0:T(8,128)(2,1)S(1)} %get-tuple-element.18.refs_2_, bf16[32,7,16,128]{3,2,1,0:T(8,128)(2,1)S(1)} %get-tuple-element.19.refs_3_, ...), custom_call_target="tpu_custom_call" | custom-call | flops 3000000000 | bytes 10000000 | tf_op jit(solution)/shard_map/mixed/pallas_call | solution.py:439
  (5 shorter events, 0.0 us)
Async XLA Ops:
  24.9 7.6 %collective-permute-start.2 = (bf16[8,7,16,128]{3,2,1,0:T(8,128)(2,1)S(1)}, bf16[8,7,16,128]{3,2,1,0:T(8,128)(2,1)S(1)}, u32[]{:S(2)}, u32[]{:S(2)}) collective-permute-start(bf16[8,7,16,128]{3,2,1,0:T(8,128)(2,1)S(1)} %slice.4), channel_id=1, source_target_pairs={{0,64},{1,65},{2,66},{3,67},{4,68},{5,69},{6,70},{7,71},{8,72},{9,... | collective-permute-start | bytes 688136 | tf_op jit(solution)/shard_map/ppermute | solution.py:47
  28.0 7.0 %collective-permute-start.1 = (bf16[8,7,16,128]{3,2,1,0:T(8,128)(2,1)S(1)}, bf16[8,7,16,128]{3,2,1,0:T(8,128)(2,1)S(1)}, u32[]{:S(2)}, u32[]{:S(2)}) collective-permute-start(bf16[8,7,16,128]{3,2,1,0:T(8,128)(2,1)S(1)} %slice.4), channel_id=1, source_target_pairs={{0,96},{1,97},{2,98},{3,99},{4,100},{5,101},{6,102},{7,103},{8,104... | collective-permute-start | bytes 688136 | tf_op jit(solution)/shard_map/ppermute | solution.py:47
  29.2 7.2 %collective-permute-start = (bf16[8,7,16,128]{3,2,1,0:T(8,128)(2,1)S(1)}, bf16[8,7,16,128]{3,2,1,0:T(8,128)(2,1)S(1)}, u32[]{:S(2)}, u32[]{:S(2)}) collective-permute-start(bf16[8,7,16,128]{3,2,1,0:T(8,128)(2,1)S(1)} %slice.4), channel_id=1, source_target_pairs={{0,32},{1,33},{2,34},{3,35},{4,36},{5,37},{6,38},{7,39},{8,40},{9,... | collective-permute-start | bytes 688136 | tf_op jit(solution)/shard_map/ppermute | solution.py:47
  36.4 27.6 %copy-start.1 = (f32[1280]{0:T(1024)S(1)}, f32[1280]{0:T(1024)}, u32[]{:S(2)}) copy-start(f32[1280]{0:T(1024)} %param.10) | copy-start | bytes 15364
  36.5 27.5 %copy-start.2 = (f32[1280]{0:T(1024)S(1)}, f32[1280]{0:T(1024)}, u32[]{:S(2)}) copy-start(f32[1280]{0:T(1024)} %param.13) | copy-start | bytes 15364
  36.5 6.4 %collective-permute-start.12 = (bf16[20,7,16,128]{3,2,1,0:T(8,128)(2,1)S(1)}, bf16[20,7,16,128]{3,2,1,0:T(8,128)(2,1)S(1)}, u32[]{:S(2)}, u32[]{:S(2)}) collective-permute-start(bf16[20,7,16,128]{3,2,1,0:T(8,128)(2,1)S(1)} %get-tuple-element.14.refs_0_), channel_id=1, source_target_pairs={{0,128},{1,129},{2,130},{3,131},{4,132},{5,133},{6,134},{7,135},{8... | collective-permute-start | bytes 1720328 | tf_op jit(solution)/shard_map/ppermute | solution.py:63
  36.6 10.3 %collective-permute-start.5 = (bf16[20,7,16,128]{3,2,1,0:T(8,128)(2,1)S(1)}, bf16[20,7,16,128]{3,2,1,0:T(8,128)(2,1)S(1)}, u32[]{:S(2)}, u32[]{:S(2)}) collective-permute-start(bf16[20,7,16,128]{3,2,1,0:T(8,128)(2,1)S(1)} %get-tuple-element.14.refs_0_), channel_id=1, source_target_pairs={{0,3},{1,0},{2,1},{3,2},{4,7},{5,4},{6,5},{7,6},{8,11},{9,8},{10,9... | collective-permute-start | bytes 1720328 | tf_op jit(solution)/shard_map/ppermute | solution.py:53
  39.7 10.9 %collective-permute-start.3 = (bf16[20,7,16,128]{3,2,1,0:T(8,128)(2,1)S(1)}, bf16[20,7,16,128]{3,2,1,0:T(8,128)(2,1)S(1)}, u32[]{:S(2)}, u32[]{:S(2)}) collective-permute-start(bf16[20,7,16,128]{3,2,1,0:T(8,128)(2,1)S(1)} %get-tuple-element.14.refs_0_), channel_id=1, source_target_pairs={{0,1},{1,2},{2,3},{3,0},{4,5},{5,6},{6,7},{7,4},{8,9},{9,10},{10,1... | collective-permute-start | bytes 1720328 | tf_op jit(solution)/shard_map/ppermute | solution.py:53
  39.7 13.4 %collective-permute-start.6 = (bf16[20,7,16,128]{3,2,1,0:T(8,128)(2,1)S(1)}, bf16[20,7,16,128]{3,2,1,0:T(8,128)(2,1)S(1)}, u32[]{:S(2)}, u32[]{:S(2)}) collective-permute-start(bf16[20,7,16,128]{3,2,1,0:T(8,128)(2,1)S(1)} %get-tuple-element.15.refs_1_), channel_id=1, source_target_pairs={{0,3},{1,0},{2,1},{3,2},{4,7},{5,4},{6,5},{7,6},{8,11},{9,8},{10,9... | collective-permute-start | bytes 1720328 | tf_op jit(solution)/shard_map/ppermute | solution.py:53
  42.9 13.8 %collective-permute-start.13 = (bf16[20,7,16,128]{3,2,1,0:T(8,128)(2,1)S(1)}, bf16[20,7,16,128]{3,2,1,0:T(8,128)(2,1)S(1)}, u32[]{:S(2)}, u32[]{:S(2)}) collective-permute-start(bf16[20,7,16,128]{3,2,1,0:T(8,128)(2,1)S(1)} %get-tuple-element.15.refs_1_), channel_id=1, source_target_pairs={{0,128},{1,129},{2,130},{3,131},{4,132},{5,133},{6,134},{7,135},{8... | collective-permute-start | bytes 1720328 | tf_op jit(solution)/shard_map/ppermute | solution.py:63
  42.9 13.8 %collective-permute-start.4 = (bf16[20,7,16,128]{3,2,1,0:T(8,128)(2,1)S(1)}, bf16[20,7,16,128]{3,2,1,0:T(8,128)(2,1)S(1)}, u32[]{:S(2)}, u32[]{:S(2)}) collective-permute-start(bf16[20,7,16,128]{3,2,1,0:T(8,128)(2,1)S(1)} %get-tuple-element.15.refs_1_), channel_id=1, source_target_pairs={{0,1},{1,2},{2,3},{3,0},{4,5},{5,6},{6,7},{7,4},{8,9},{9,10},{10,1... | collective-permute-start | bytes 1720328 | tf_op jit(solution)/shard_map/ppermute | solution.py:53
  46.9 10.4 %collective-permute-start.16 = (bf16[20,7,16,128]{3,2,1,0:T(8,128)(2,1)S(1)}, bf16[20,7,16,128]{3,2,1,0:T(8,128)(2,1)S(1)}, u32[]{:S(2)}, u32[]{:S(2)}) collective-permute-start(bf16[20,7,16,128]{3,2,1,0:T(8,128)(2,1)S(1)} %collective-permute-done.5.refs_4_), channel_id=1, source_target_pairs={{0,128},{1,129},{2,130},{3,131},{4,132},{5,133},{6,134},{7,135},{8... | collective-permute-start | bytes 1720328 | tf_op jit(solution)/shard_map/ppermute | solution.py:63
  50.6 12.3 %collective-permute-start.7 = (bf16[20,7,16,128]{3,2,1,0:T(8,128)(2,1)S(1)}, bf16[20,7,16,128]{3,2,1,0:T(8,128)(2,1)S(1)}, u32[]{:S(2)}, u32[]{:S(2)}) collective-permute-start(bf16[20,7,16,128]{3,2,1,0:T(8,128)(2,1)S(1)} %collective-permute-done.3.refs_2_), channel_id=1, source_target_pairs={{0,1},{1,2},{2,3},{3,0},{4,5},{5,6},{6,7},{7,4},{8,9},{9,10},{10,1... | collective-permute-start | bytes 1720328 | tf_op jit(solution)/shard_map/ppermute | solution.py:53
  53.1 10.9 %collective-permute-start.8 = (bf16[20,7,16,128]{3,2,1,0:T(8,128)(2,1)S(1)}, bf16[20,7,16,128]{3,2,1,0:T(8,128)(2,1)S(1)}, u32[]{:S(2)}, u32[]{:S(2)}) collective-permute-start(bf16[20,7,16,128]{3,2,1,0:T(8,128)(2,1)S(1)} %collective-permute-done.6.refs_5_), channel_id=1, source_target_pairs={{0,3},{1,0},{2,1},{3,2},{4,7},{5,4},{6,5},{7,6},{8,11},{9,8},{10,9... | collective-permute-start | bytes 1720328 | tf_op jit(solution)/shard_map/ppermute | solution.py:53
  56.8 8.3 %collective-permute-start.14 = (bf16[20,7,16,128]{3,2,1,0:T(8,128)(2,1)S(1)}, bf16[20,7,16,128]{3,2,1,0:T(8,128)(2,1)S(1)}, u32[]{:S(2)}, u32[]{:S(2)}) collective-permute-start(bf16[20,7,16,128]{3,2,1,0:T(8,128)(2,1)S(1)} %collective-permute-done.3.refs_2_), channel_id=1, source_target_pairs={{0,128},{1,129},{2,130},{3,131},{4,132},{5,133},{6,134},{7,135},{8... | collective-permute-start | bytes 1720328 | tf_op jit(solution)/shard_map/ppermute | solution.py:63
  56.8 9.9 %collective-permute-start.17 = (bf16[20,7,16,128]{3,2,1,0:T(8,128)(2,1)S(1)}, bf16[20,7,16,128]{3,2,1,0:T(8,128)(2,1)S(1)}, u32[]{:S(2)}, u32[]{:S(2)}) collective-permute-start(bf16[20,7,16,128]{3,2,1,0:T(8,128)(2,1)S(1)} %collective-permute-done.6.refs_5_), channel_id=1, source_target_pairs={{0,128},{1,129},{2,130},{3,131},{4,132},{5,133},{6,134},{7,135},{8... | collective-permute-start | bytes 1720328 | tf_op jit(solution)/shard_map/ppermute | solution.py:63
  57.3 10.5 %collective-permute-start.15 = (bf16[20,7,16,128]{3,2,1,0:T(8,128)(2,1)S(1)}, bf16[20,7,16,128]{3,2,1,0:T(8,128)(2,1)S(1)}, u32[]{:S(2)}, u32[]{:S(2)}) collective-permute-start(bf16[20,7,16,128]{3,2,1,0:T(8,128)(2,1)S(1)} %collective-permute-done.4.refs_3_), channel_id=1, source_target_pairs={{0,128},{1,129},{2,130},{3,131},{4,132},{5,133},{6,134},{7,135},{8... | collective-permute-start | bytes 1720328 | tf_op jit(solution)/shard_map/ppermute | solution.py:63
  62.9 5.8 %collective-permute-start.18 = (bf16[20,7,16,128]{3,2,1,0:T(8,128)(2,1)S(1)}, bf16[20,7,16,128]{3,2,1,0:T(8,128)(2,1)S(1)}, u32[]{:S(2)}, u32[]{:S(2)}) collective-permute-start(bf16[20,7,16,128]{3,2,1,0:T(8,128)(2,1)S(1)} %collective-permute-done.7.refs_6_), channel_id=1, source_target_pairs={{0,128},{1,129},{2,130},{3,131},{4,132},{5,133},{6,134},{7,135},{8... | collective-permute-start | bytes 1720328 | tf_op jit(solution)/shard_map/ppermute | solution.py:63
  64.0 4.7 %collective-permute-start.19 = (bf16[20,7,16,128]{3,2,1,0:T(8,128)(2,1)S(1)}, bf16[20,7,16,128]{3,2,1,0:T(8,128)(2,1)S(1)}, u32[]{:S(2)}, u32[]{:S(2)}) collective-permute-start(bf16[20,7,16,128]{3,2,1,0:T(8,128)(2,1)S(1)} %collective-permute-done.8.refs_7_), channel_id=1, source_target_pairs={{0,128},{1,129},{2,130},{3,131},{4,132},{5,133},{6,134},{7,135},{8... | collective-permute-start | bytes 1720328 | tf_op jit(solution)/shard_map/ppermute | solution.py:63
  64.0 4.7 %copy-start = (bf16[1,128,1280]{2,1,0:T(8,128)(2,1)S(1)}, bf16[1,128,1280]{2,1,0:T(8,128)(2,1)}, u32[]{:S(2)}) copy-start(bf16[1,128,1280]{2,1,0:T(8,128)(2,1)} %param.8) | copy-start | bytes 983044
  65.0 18.4 %collective-permute-start.11 = (bf16[32,7,16,128]{3,2,1,0:T(8,128)(2,1)}, bf16[32,7,16,128]{3,2,1,0:T(8,128)(2,1)S(1)}, u32[]{:S(2)}, u32[]{:S(2)}) collective-permute-start(bf16[32,7,16,128]{3,2,1,0:T(8,128)(2,1)} %temporal_blocks.1.refs_0_), channel_id=1, source_target_pairs={{0,64},{1,65},{2,66},{3,67},{4,68},{5,69},{6,70},{7,71},{8,72},{9,... | collective-permute-start | bytes 2752520 | tf_op jit(solution)/shard_map/ppermute | solution.py:47
  66.6 24.8 %collective-permute-start.10 = (bf16[32,7,16,128]{3,2,1,0:T(8,128)(2,1)}, bf16[32,7,16,128]{3,2,1,0:T(8,128)(2,1)S(1)}, u32[]{:S(2)}, u32[]{:S(2)}) collective-permute-start(bf16[32,7,16,128]{3,2,1,0:T(8,128)(2,1)} %temporal_blocks.1.refs_0_), channel_id=1, source_target_pairs={{0,96},{1,97},{2,98},{3,99},{4,100},{5,101},{6,102},{7,103},{8,104... | collective-permute-start | bytes 2752520 | tf_op jit(solution)/shard_map/ppermute | solution.py:47
  67.8 24.8 %collective-permute-start.9 = (bf16[32,7,16,128]{3,2,1,0:T(8,128)(2,1)}, bf16[32,7,16,128]{3,2,1,0:T(8,128)(2,1)S(1)}, u32[]{:S(2)}, u32[]{:S(2)}) collective-permute-start(bf16[32,7,16,128]{3,2,1,0:T(8,128)(2,1)} %temporal_blocks.1.refs_0_), channel_id=1, source_target_pairs={{0,32},{1,33},{2,34},{3,35},{4,36},{5,37},{6,38},{7,39},{8,40},{9,... | collective-permute-start | bytes 2752520 | tf_op jit(solution)/shard_map/ppermute | solution.py:47
  73.7 24.3 %all-to-all-start.1 = ((bf16[128,5,2,128]{3,2,1,0:T(2,128)(2,1)}), bf16[128,5,2,128]{3,2,1,0:T(2,128)(2,1)S(1)}, u32[]{:S(2)}, u32[]{:S(2)}) async-start(bf16[128,5,2,128]{3,2,1,0:T(2,128)(2,1)} %get-tuple-element.16), calls=%async_computation.1 | async-start | bytes 655360 | tf_op jit(solution)/shard_map/all_to_all | solution.py:410
  83.3 17.5 %collective-permute-start.20 = (bf16[32,7,16,128]{3,2,1,0:T(8,128)(2,1)}, bf16[32,7,16,128]{3,2,1,0:T(8,128)(2,1)}, u32[]{:S(2)}, u32[]{:S(2)}) collective-permute-start(bf16[32,7,16,128]{3,2,1,0:T(8,128)(2,1)} %temporal_blocks.1.refs_0_), channel_id=1, source_target_pairs={{0,128},{1,129},{2,130},{3,131},{4,132},{5,133},{6,134},{7,135},{8... | collective-permute-start | bytes 2752520 | tf_op jit(solution)/shard_map/ppermute | solution.py:63
  98.0 2.8 %collective-permute-start.21 = (bf16[32,7,16,128]{3,2,1,0:T(8,128)(2,1)S(1)}, bf16[32,7,16,128]{3,2,1,0:T(8,128)(2,1)S(1)}, u32[]{:S(2)}, u32[]{:S(2)}) collective-permute-start(bf16[32,7,16,128]{3,2,1,0:T(8,128)(2,1)S(1)} %get-tuple-element.17.refs_1_), channel_id=1, source_target_pairs={{0,128},{1,129},{2,130},{3,131},{4,132},{5,133},{6,134},{7,135},{8... | collective-permute-start | bytes 2752520 | tf_op jit(solution)/shard_map/ppermute | solution.py:63
  98.0 3.8 %collective-permute-start.22 = (bf16[32,7,16,128]{3,2,1,0:T(8,128)(2,1)S(1)}, bf16[32,7,16,128]{3,2,1,0:T(8,128)(2,1)S(1)}, u32[]{:S(2)}, u32[]{:S(2)}) collective-permute-start(bf16[32,7,16,128]{3,2,1,0:T(8,128)(2,1)S(1)} %get-tuple-element.18.refs_2_), channel_id=1, source_target_pairs={{0,128},{1,129},{2,130},{3,131},{4,132},{5,133},{6,134},{7,135},{8... | collective-permute-start | bytes 2752520 | tf_op jit(solution)/shard_map/ppermute | solution.py:63
  98.5 4.6 %collective-permute-start.23 = (bf16[32,7,16,128]{3,2,1,0:T(8,128)(2,1)S(1)}, bf16[32,7,16,128]{3,2,1,0:T(8,128)(2,1)S(1)}, u32[]{:S(2)}, u32[]{:S(2)}) collective-permute-start(bf16[32,7,16,128]{3,2,1,0:T(8,128)(2,1)S(1)} %get-tuple-element.19.refs_3_), channel_id=1, source_target_pairs={{0,128},{1,129},{2,130},{3,131},{4,132},{5,133},{6,134},{7,135},{8... | collective-permute-start | bytes 2752520 | tf_op jit(solution)/shard_map/ppermute | solution.py:63

commit v6 on v5

--- a/solution.py
+++ b/solution.py
@@ -118,7 +118,7 @@
         pl.when(c == half)(functools.partial(fill, half))
 
 
-def halves_kernel(along_z, p1, p2, p3, one, two):
+def halves_kernel(along_z, p1, p2, p3, after, one, two):
     spatial = (along_z, p1, p2, p3)
     for half, out in enumerate((one, two)):
         for i in range(2):
@@ -291,11 +291,14 @@
     return jnp.concatenate(parts, axis=1).astype(BF)
 
 
+def norm_kernel(latents, gain, out):
+    out[...] = layer_norm(latents[...].astype(F32), gain[...])
+
+
 def spatial_kernel(*refs):
     own, oth = refs[0:8], refs[8:16]
-    latents, gain_s, gain_t, hidden, tnormed, acc, rows, last, attn, scores, acc_out, rows_out = refs[16:]
-    normed = layer_norm(latents[...].astype(F32), gain_s[...])
-    tokens = jnp.concatenate([normed, reference_tokens(own, last)], axis=0)
+    latents, normed, gain_t, hidden, tnormed, acc, rows, last, attn, scores, acc_out, rows_out = refs[16:]
+    tokens = jnp.concatenate([normed[...], reference_tokens(own, last)], axis=0)
     qkv_project(own, oth, acc, rows, tokens, 0)
     heads(rows, scores, attn)
     views = [[p.at[:, pl.ds(5, 2)] for p in pieces] for pieces in (own, oth)]
@@ -385,14 +388,16 @@
         tiled=True,
     )
     first = ring(along_z[:, :GROUP], 0)
-    own_s = ring_by_halves(reorder(halves_kernel, [along_z] + first[1:], [(20, GROUP)] * 2, "halves"), 1)
+    normed = call(norm_kernel, [latents, gain_s], [(PIX, D)], [], "norm", 10**9, 4)
+    args = [along_z] + first[1:] + [normed]
+    own_s = ring_by_halves(reorder(halves_kernel, args, [(20, GROUP)] * 2, "halves"), 1)
     oth_s = [swap(b) for b in own_s]
     (part_t,) = reorder(temporal_blocks_kernel, own_s, [(32, GROUP)], "temporal_blocks")
     ring_t = ring(part_t, 0)
 
     hidden, tnormed = call(
         spatial_kernel,
-        own_s + oth_s + [latents, gain_s, gain_t],
+        own_s + oth_s + [latents, normed, gain_t],
         [(PIX, D), (PIX, 5, 2, 128)],
         [
             (NX, NZ, NY, 16, 256),

time: 129 us -> 129 us (level)
    pallas_call x3 -> x4, Pallas kernels: 10.1 us -> 10.3 us  [call(): pl.pallas_call(kernel, out_shape=shapes[0] if single else shapes, in_spec...]
  transfers between devices with their start and end apart: 25 -> 25, of which waited for: 13 -> 13; matrix products, arithmetic and copies ran while one was open for 0% -> 0% of each run, Pallas kernels for 6% -> 7%
where the time goes in v6:
time: 129 us
  blocking collectives  43.1 us (33%)
  waiting for transfers between devices  39.5 us (31%)
  starting transfers between devices  29.7 us (23%)
  Pallas kernels  15.9 us (12%)
    all_to_all x1, blocking collectives, body(): lax.all_to_all(packed, 'seq', 0, 0, axis_index_groups=Z_GROUPS, tiled=True)  23.2 us
    all_to_all x1, blocking collectives, body(): back = lax.all_to_all(tattn, 'seq', 0, 0, tiled=True)  19.9 us
    ppermute x6, waiting for transfers between devices, shift(): return lax.ppermute(part, ('clip', 'seq'), ring_perm(k, stage))  16.7 us
    ppermute x6, waiting for transfers between devices, ring(): lax.ppermute(block, ('clip', 'seq'), ring_perm(k, stage))  15.5 us
    pallas_call x4, Pallas kernels, call(): pl.pallas_call(kernel, out_shape=shapes[0] if single else shapes, in_spec...  10.3 us
    ppermute x6, starting transfers between devices, shift(): return lax.ppermute(part, ('clip', 'seq'), ring_perm(k, stage))  10 us
    all_to_all x1, starting transfers between devices, body(): tokens = lax.all_to_all(tnormed, 'seq', 0, 0, tiled=True)  9.57 us
    ppermute x6, starting transfers between devices, ring(): lax.ppermute(block, ('clip', 'seq'), ring_perm(k, stage))  8.77 us
  transfers between devices with their start and end apart: 25, of which 13 were waited for; matrix products, arithmetic and copies ran while one was open for 0% of the time, Pallas kernels for 7%

profile of v6, /device:TPU:32, one launch (start us, length us, event | category | flops | bytes accessed | tf_op | source)
XLA Modules:
  0.0 128.6 jit_solution(16289598900771698767)
XLA Ops:
  0.0 1.7 %pack.1 = bf16[8,14,16,128]{3,2,1,0:T(8,128)(2,1)} custom-call(bf16[15,1280]{1,0:T(8,128)(2,1)} %bitcast.8, bf16[1,1280]{1,0:T(2,128)(2,1)} %ref_in.1, bf16[10,640]{1,0:T(8,128)(2,1)} %bitcast.10, bf16[15,1280]{1,0:T(8,128)(2,1)} %bitcast.9, bf16[10,640]{1,0:T(8,128)(2,1)} %bitcast.11), custom_call_target="tpu_custom_call" | custom-call | tf_op jit(solution)/shard_map/pack/pallas_call | solution.py:373
  1.7 23.2 %all_to_all.15.along_z = bf16[8,14,16,128]{3,2,1,0:T(8,128)(2,1)S(1)} all-to-all(bf16[8,14,16,128]{3,2,1,0:T(8,128)(2,1)} %pack.1), channel_id=1, replica_groups={{0,4,8,12,16,20,24,28},{1,5,9,13,17,21,25,29},{2,6,10,14,18,22,26,30},{..., dimensions={0} | all-to-all | bytes 917504 | tf_op jit(solution)/shard_map/all_to_all | solution.py:382
  24.9 0.0 copy-start.1
  24.9 3.1 %collective-permute-start.2 = (bf16[8,7,16,128]{3,2,1,0:T(8,128)(2,1)S(1)}, bf16[8,7,16,128]{3,2,1,0:T(8,128)(2,1)S(1)}, u32[]{:S(2)}, u32[]{:S(2)}) collective-permute-start(bf16[8,7,16,128]{3,2,1,0:T(8,128)(2,1)S(1)} %slice.4), channel_id=1, source_target_pairs={{0,64},{1,65},{2,66},{3,67},{4,68},{5,69},{6,70},{7,71},{8,72},{9,... | collective-permute-start | bytes 688136 | tf_op jit(solution)/shard_map/ppermute | solution.py:47
  28.0 1.1 collective-permute-start.1
  29.2 0.9 collective-permute-start
  30.1 0.0 copy-done.1
  30.1 0.0 copy-done
  30.1 0.3 norm.1.after.refs_17_
  30.4 2.2 %collective-permute-done.2.p3 = bf16[8,7,16,128]{3,2,1,0:T(8,128)(2,1)S(1)} collective-permute-done((bf16[8,7,16,128]{3,2,1,0:T(8,128)(2,1)S(1)}, bf16[8,7,16,128]{3,2,1,0:T(8,128)(2,1)S(1)}, u32[]{:S(2)}, u32[]{:S(2)}) %collective-permute-start.2) | collective-permute-done | bytes 229408 | tf_op jit(solution)/shard_map/ppermute | solution.py:47
  32.5 2.5 %collective-permute-done.1.p2 = bf16[8,7,16,128]{3,2,1,0:T(8,128)(2,1)S(1)} collective-permute-done((bf16[8,7,16,128]{3,2,1,0:T(8,128)(2,1)S(1)}, bf16[8,7,16,128]{3,2,1,0:T(8,128)(2,1)S(1)}, u32[]{:S(2)}, u32[]{:S(2)}) %collective-permute-start.1) | collective-permute-done | bytes 229408 | tf_op jit(solution)/shard_map/ppermute | solution.py:47
  35.1 1.3 %collective-permute-done.p1 = bf16[8,7,16,128]{3,2,1,0:T(8,128)(2,1)S(1)} collective-permute-done((bf16[8,7,16,128]{3,2,1,0:T(8,128)(2,1)S(1)}, bf16[8,7,16,128]{3,2,1,0:T(8,128)(2,1)S(1)}, u32[]{:S(2)}, u32[]{:S(2)}) %collective-permute-start) | collective-permute-done | bytes 229408 | tf_op jit(solution)/shard_map/ppermute | solution.py:47
  36.4 0.1 halves.1
  36.5 0.1 collective-permute-start.12
  36.6 3.1 %collective-permute-start.5 = (bf16[20,7,16,128]{3,2,1,0:T(8,128)(2,1)S(1)}, bf16[20,7,16,128]{3,2,1,0:T(8,128)(2,1)S(1)}, u32[]{:S(2)}, u32[]{:S(2)}) collective-permute-start(bf16[20,7,16,128]{3,2,1,0:T(8,128)(2,1)S(1)} %get-tuple-element.14.refs_0_), channel_id=1, source_target_pairs={{0,3},{1,0},{2,1},{3,2},{4,7},{5,4},{6,5},{7,6},{8,11},{9,8},{10,9... | collective-permute-start | bytes 1720328 | tf_op jit(solution)/shard_map/ppermute | solution.py:53
  39.7 0.0 collective-permute-start.3
  39.7 3.2 %collective-permute-start.6 = (bf16[20,7,16,128]{3,2,1,0:T(8,128)(2,1)S(1)}, bf16[20,7,16,128]{3,2,1,0:T(8,128)(2,1)S(1)}, u32[]{:S(2)}, u32[]{:S(2)}) collective-permute-start(bf16[20,7,16,128]{3,2,1,0:T(8,128)(2,1)S(1)} %get-tuple-element.15.refs_1_), channel_id=1, source_target_pairs={{0,3},{1,0},{2,1},{3,2},{4,7},{5,4},{6,5},{7,6},{8,11},{9,8},{10,9... | collective-permute-start | bytes 1720328 | tf_op jit(solution)/shard_map/ppermute | solution.py:53
  42.9 0.0 collective-permute-start.13
  42.9 0.0 collective-permute-done.12.refs_8_
  42.9 0.0 collective-permute-start.4
  42.9 4.0 %collective-permute-done.5.refs_4_ = bf16[20,7,16,128]{3,2,1,0:T(8,128)(2,1)S(1)} collective-permute-done((bf16[20,7,16,128]{3,2,1,0:T(8,128)(2,1)S(1)}, bf16[20,7,16,128]{3,2,1,0:T(8,128)(2,1)S(1)}, u32[]{:S(2)}, u32[]{:S(2)}) %collective-permute-start.5) | collective-permute-done | bytes 573472 | tf_op jit(solution)/shard_map/ppermute | solution.py:53
  46.9 0.0 collective-permute-start.16
  46.9 3.7 %collective-permute-done.3.refs_2_ = bf16[20,7,16,128]{3,2,1,0:T(8,128)(2,1)S(1)} collective-permute-done((bf16[20,7,16,128]{3,2,1,0:T(8,128)(2,1)S(1)}, bf16[20,7,16,128]{3,2,1,0:T(8,128)(2,1)S(1)}, u32[]{:S(2)}, u32[]{:S(2)}) %collective-permute-start.3) | collective-permute-done | bytes 573472 | tf_op jit(solution)/shard_map/ppermute | solution.py:53
  50.6 0.0 collective-permute-start.7
  50.6 2.4 %collective-permute-done.6.refs_5_ = bf16[20,7,16,128]{3,2,1,0:T(8,128)(2,1)S(1)} collective-permute-done((bf16[20,7,16,128]{3,2,1,0:T(8,128)(2,1)S(1)}, bf16[20,7,16,128]{3,2,1,0:T(8,128)(2,1)S(1)}, u32[]{:S(2)}, u32[]{:S(2)}) %collective-permute-start.6) | collective-permute-done | bytes 573472 | tf_op jit(solution)/shard_map/ppermute | solution.py:53
  53.1 3.7 %collective-permute-start.8 = (bf16[20,7,16,128]{3,2,1,0:T(8,128)(2,1)S(1)}, bf16[20,7,16,128]{3,2,1,0:T(8,128)(2,1)S(1)}, u32[]{:S(2)}, u32[]{:S(2)}) collective-permute-start(bf16[20,7,16,128]{3,2,1,0:T(8,128)(2,1)S(1)} %collective-permute-done.6.refs_5_), channel_id=1, source_target_pairs={{0,3},{1,0},{2,1},{3,2},{4,7},{5,4},{6,5},{7,6},{8,11},{9,8},{10,9... | collective-permute-start | bytes 1720328 | tf_op jit(solution)/shard_map/ppermute | solution.py:53
  56.7 0.0 collective-permute-done.13.refs_9_
  56.7 0.0 collective-permute-start.14
  56.7 0.0 collective-permute-done.4.refs_3_
  56.8 0.5 collective-permute-start.17
  57.3 0.0 collective-permute-done.16.refs_12_
  57.3 0.1 collective-permute-start.15
  57.4 5.5 %collective-permute-done.7.refs_6_ = bf16[20,7,16,128]{3,2,1,0:T(8,128)(2,1)S(1)} collective-permute-done((bf16[20,7,16,128]{3,2,1,0:T(8,128)(2,1)S(1)}, bf16[20,7,16,128]{3,2,1,0:T(8,128)(2,1)S(1)}, u32[]{:S(2)}, u32[]{:S(2)}) %collective-permute-start.7) | collective-permute-done | bytes 573472 | tf_op jit(solution)/shard_map/ppermute | solution.py:53
  62.9 0.0 collective-permute-start.18
  62.9 1.1 collective-permute-done.8.refs_7_
  64.0 0.0 collective-permute-start.19
  64.0 0.0 copy-done.2
  64.0 1.0 temporal_blocks.1.refs_0_
  65.0 0.0 collective-permute-done.14.refs_10_
  65.0 1.6 %collective-permute-start.11 = (bf16[32,7,16,128]{3,2,1,0:T(8,128)(2,1)}, bf16[32,7,16,128]{3,2,1,0:T(8,128)(2,1)S(1)}, u32[]{:S(2)}, u32[]{:S(2)}) collective-permute-start(bf16[32,7,16,128]{3,2,1,0:T(8,128)(2,1)} %temporal_blocks.1.refs_0_), channel_id=1, source_target_pairs={{0,64},{1,65},{2,66},{3,67},{4,68},{5,69},{6,70},{7,71},{8,72},{9,... | collective-permute-start | bytes 2752520 | tf_op jit(solution)/shard_map/ppermute | solution.py:47
  66.6 0.0 collective-permute-done.17.refs_13_
  66.6 1.2 collective-permute-start.10
  67.8 0.0 collective-permute-done.15.refs_11_
  67.8 0.9 collective-permute-start.9
  68.6 0.0 collective-permute-done.18.refs_14_
  68.6 0.0 collective-permute-done.19.refs_15_
  68.6 4.9 %spatial.1 = (bf16[128,1280]{1,0:T(8,128)(2,1)S(1)}, bf16[128,5,2,128]{3,2,1,0:T(2,128)(2,1)}) custom-call(bf16[20,7,16,128]{3,2,1,0:T(8,128)(2,1)S(1)} %get-tuple-element.14.refs_0_, bf16[20,7,16,128]{3,2,1,0:T(8,128)(2,1)S(1)} %get-tuple-element.15.refs_1_, bf16[20,7,16,128]{3,2,1,0:T(8,128)(2,1)S(1)} %collective-permute-done.3.refs_2_, ...), custom_call_target="tpu_custom_call" | custom-call | flops 8999999488 | bytes 10490880 | tf_op jit(solution)/shard_map/spatial/pallas_call | solution.py:356
  73.5 9.6 %all-to-all-start.1 = ((bf16[128,5,2,128]{3,2,1,0:T(2,128)(2,1)}), bf16[128,5,2,128]{3,2,1,0:T(2,128)(2,1)S(1)}, u32[]{:S(2)}, u32[]{:S(2)}) async-start(bf16[128,5,2,128]{3,2,1,0:T(2,128)(2,1)} %get-tuple-element.16), calls=%async_computation.1 | async-start | bytes 655360 | tf_op jit(solution)/shard_map/all_to_all | solution.py:415
  83.1 0.1 collective-permute-start.20
  83.2 0.0 collective-permute-done.11.refs_2_
  83.2 8.3 %collective-permute-done.10.refs_1_ = bf16[32,7,16,128]{3,2,1,0:T(8,128)(2,1)S(1)} collective-permute-done((bf16[32,7,16,128]{3,2,1,0:T(8,128)(2,1)}, bf16[32,7,16,128]{3,2,1,0:T(8,128)(2,1)S(1)}, u32[]{:S(2)}, u32[]{:S(2)}) %collective-permute-start.10) | collective-permute-done | bytes 917536 | tf_op jit(solution)/shard_map/ppermute | solution.py:47
  91.5 1.1 collective-permute-done.9.refs_0_
  92.6 5.0 %all-to-all-done.1.refs_3_.refs_4_ = bf16[128,5,2,128]{3,2,1,0:T(2,128)(2,1)S(1)} async-done(((bf16[128,5,2,128]{3,2,1,0:T(2,128)(2,1)}), bf16[128,5,2,128]{3,2,1,0:T(2,128)(2,1)S(1)}, u32[]{:S(2)}, u32[]{:S(2)}) %all-to-all-start.1) | async-done | bytes 327712 | tf_op jit(solution)/shard_map/all_to_all | solution.py:415
  97.7 0.0 collective-permute-start.21
  97.7 0.5 collective-permute-start.22
  98.2 0.0 collective-permute-start.23
  98.2 2.3 %half.1 = (f32[2048,128]{1,0:T(8,128)S(1)}, bf16[128,640]{1,0:T(8,128)(2,1)S(1)}) custom-call(bf16[32,7,16,128]{3,2,1,0:T(8,128)(2,1)} %temporal_blocks.1.refs_0_, bf16[32,7,16,128]{3,2,1,0:T(8,128)(2,1)S(1)} %get-tuple-element.17.refs_1_, bf16[32,7,16,128]{3,2,1,0:T(8,128)(2,1)S(1)} %get-tuple-element.18.refs_2_, ...), custom_call_target="tpu_custom_call" | custom-call | flops 3000000000 | bytes 4685824 | tf_op jit(solution)/shard_map/half/pallas_call | solution.py:356
  100.5 0.0 collective-permute-done.20.refs_0_.refs_4_
  100.5 0.0 collective-permute-done.21.refs_1_.refs_5_
  100.5 1.0 collective-permute-done.22.refs_2_.refs_6_
  101.5 1.3 %collective-permute-done.23.refs_3_.refs_7_ = bf16[32,7,16,128]{3,2,1,0:T(8,128)(2,1)S(1)} collective-permute-done((bf16[32,7,16,128]{3,2,1,0:T(8,128)(2,1)S(1)}, bf16[32,7,16,128]{3,2,1,0:T(8,128)(2,1)S(1)}, u32[]{:S(2)}, u32[]{:S(2)}) %collective-permute-start.23) | collective-permute-done | bytes 917536 | tf_op jit(solution)/shard_map/ppermute | solution.py:63
  102.8 2.8 %temporal.1 = bf16[128,3,2,128]{3,2,1,0:T(2,128)(2,1)S(1)} custom-call(bf16[32,7,16,128]{3,2,1,0:T(8,128)(2,1)} %collective-permute-done.20.refs_0_.refs_4_, bf16[32,7,16,128]{3,2,1,0:T(8,128)(2,1)S(1)} %collective-permute-done.21.refs_1_.refs_5_, bf16[32,7,16,128]{3,2,1,0:T(8,128)(2,1)S(1)} %collective-permute-done.22.refs_2_.refs_6_, ...), custom_call_target="tpu_custom_call" | custom-call | flops 5000000000 | bytes 5079040 | tf_op jit(solution)/shard_map/temporal/pallas_call | solution.py:356
  105.6 19.9 %all_to_all.16.refs_8_ = bf16[128,3,2,128]{3,2,1,0:T(2,128)(2,1)S(1)} all-to-all(bf16[128,3,2,128]{3,2,1,0:T(2,128)(2,1)S(1)} %temporal.1), channel_id=1, replica_groups=mesh['clip'=2,'seq'=128] {'seq'}, dimensions={0} | all-to-all | bytes 393216 | tf_op jit(solution)/shard_map/all_to_all | solution.py:443
  125.5 2.9 %mixed.1 = bf16[128,1280]{1,0:T(8,128)(2,1)} custom-call(bf16[32,7,16,128]{3,2,1,0:T(8,128)(2,1)} %temporal_blocks.1.refs_0_, bf16[32,7,16,128]{3,2,1,0:T(8,128)(2,1)S(1)} %get-tuple-element.17.refs_1_, bf16[32,7,16,128]{3,2,1,0:T(8,128)(2,1)S(1)} %get-tuple-element.18.refs_2_, bf16[32,7,16,128]{3,2,1,0:T(8,128)(2,1)S(1)} %get-tuple-element.19.refs_3_, ...), custom_call_target="tpu_custom_call" | custom-call | flops 3000000000 | bytes 10000000 | tf_op jit(solution)/shard_map/mixed/pallas_call | solution.py:444
  (6 shorter events, 0.0 us)
Async XLA Ops:
  24.9 5.2 %copy-start.1 = (f32[1280]{0:T(1024)S(1)}, f32[1280]{0:T(1024)}, u32[]{:S(2)}) copy-start(f32[1280]{0:T(1024)} %param.10) | copy-start | bytes 15364
  24.9 5.2 %copy-start = (bf16[1,128,1280]{2,1,0:T(8,128)(2,1)S(1)}, bf16[1,128,1280]{2,1,0:T(8,128)(2,1)}, u32[]{:S(2)}) copy-start(bf16[1,128,1280]{2,1,0:T(8,128)(2,1)} %param.8) | copy-start | bytes 983044
  24.9 7.6 %collective-permute-start.2 = (bf16[8,7,16,128]{3,2,1,0:T(8,128)(2,1)S(1)}, bf16[8,7,16,128]{3,2,1,0:T(8,128)(2,1)S(1)}, u32[]{:S(2)}, u32[]{:S(2)}) collective-permute-start(bf16[8,7,16,128]{3,2,1,0:T(8,128)(2,1)S(1)} %slice.4), channel_id=1, source_target_pairs={{0,64},{1,65},{2,66},{3,67},{4,68},{5,69},{6,70},{7,71},{8,72},{9,... | collective-permute-start | bytes 688136 | tf_op jit(solution)/shard_map/ppermute | solution.py:47
  28.0 7.0 %collective-permute-start.1 = (bf16[8,7,16,128]{3,2,1,0:T(8,128)(2,1)S(1)}, bf16[8,7,16,128]{3,2,1,0:T(8,128)(2,1)S(1)}, u32[]{:S(2)}, u32[]{:S(2)}) collective-permute-start(bf16[8,7,16,128]{3,2,1,0:T(8,128)(2,1)S(1)} %slice.4), channel_id=1, source_target_pairs={{0,96},{1,97},{2,98},{3,99},{4,100},{5,101},{6,102},{7,103},{8,104... | collective-permute-start | bytes 688136 | tf_op jit(solution)/shard_map/ppermute | solution.py:47
  29.2 7.2 %collective-permute-start = (bf16[8,7,16,128]{3,2,1,0:T(8,128)(2,1)S(1)}, bf16[8,7,16,128]{3,2,1,0:T(8,128)(2,1)S(1)}, u32[]{:S(2)}, u32[]{:S(2)}) collective-permute-start(bf16[8,7,16,128]{3,2,1,0:T(8,128)(2,1)S(1)} %slice.4), channel_id=1, source_target_pairs={{0,32},{1,33},{2,34},{3,35},{4,36},{5,37},{6,38},{7,39},{8,40},{9,... | collective-permute-start | bytes 688136 | tf_op jit(solution)/shard_map/ppermute | solution.py:47
  36.4 27.6 %copy-start.2 = (f32[1280]{0:T(1024)S(1)}, f32[1280]{0:T(1024)}, u32[]{:S(2)}) copy-start(f32[1280]{0:T(1024)} %param.13) | copy-start | bytes 15364
  36.5 6.4 %collective-permute-start.12 = (bf16[20,7,16,128]{3,2,1,0:T(8,128)(2,1)S(1)}, bf16[20,7,16,128]{3,2,1,0:T(8,128)(2,1)S(1)}, u32[]{:S(2)}, u32[]{:S(2)}) collective-permute-start(bf16[20,7,16,128]{3,2,1,0:T(8,128)(2,1)S(1)} %get-tuple-element.14.refs_0_), channel_id=1, source_target_pairs={{0,128},{1,129},{2,130},{3,131},{4,132},{5,133},{6,134},{7,135},{8... | collective-permute-start | bytes 1720328 | tf_op jit(solution)/shard_map/ppermute | solution.py:63
  36.6 10.3 %collective-permute-start.5 = (bf16[20,7,16,128]{3,2,1,0:T(8,128)(2,1)S(1)}, bf16[20,7,16,128]{3,2,1,0:T(8,128)(2,1)S(1)}, u32[]{:S(2)}, u32[]{:S(2)}) collective-permute-start(bf16[20,7,16,128]{3,2,1,0:T(8,128)(2,1)S(1)} %get-tuple-element.14.refs_0_), channel_id=1, source_target_pairs={{0,3},{1,0},{2,1},{3,2},{4,7},{5,4},{6,5},{7,6},{8,11},{9,8},{10,9... | collective-permute-start | bytes 1720328 | tf_op jit(solution)/shard_map/ppermute | solution.py:53
  39.7 10.9 %collective-permute-start.3 = (bf16[20,7,16,128]{3,2,1,0:T(8,128)(2,1)S(1)}, bf16[20,7,16,128]{3,2,1,0:T(8,128)(2,1)S(1)}, u32[]{:S(2)}, u32[]{:S(2)}) collective-permute-start(bf16[20,7,16,128]{3,2,1,0:T(8,128)(2,1)S(1)} %get-tuple-element.14.refs_0_), channel_id=1, source_target_pairs={{0,1},{1,2},{2,3},{3,0},{4,5},{5,6},{6,7},{7,4},{8,9},{9,10},{10,1... | collective-permute-start | bytes 1720328 | tf_op jit(solution)/shard_map/ppermute | solution.py:53
  39.7 13.4 %collective-permute-start.6 = (bf16[20,7,16,128]{3,2,1,0:T(8,128)(2,1)S(1)}, bf16[20,7,16,128]{3,2,1,0:T(8,128)(2,1)S(1)}, u32[]{:S(2)}, u32[]{:S(2)}) collective-permute-start(bf16[20,7,16,128]{3,2,1,0:T(8,128)(2,1)S(1)} %get-tuple-element.15.refs_1_), channel_id=1, source_target_pairs={{0,3},{1,0},{2,1},{3,2},{4,7},{5,4},{6,5},{7,6},{8,11},{9,8},{10,9... | collective-permute-start | bytes 1720328 | tf_op jit(solution)/shard_map/ppermute | solution.py:53
  42.9 13.8 %collective-permute-start.13 = (bf16[20,7,16,128]{3,2,1,0:T(8,128)(2,1)S(1)}, bf16[20,7,16,128]{3,2,1,0:T(8,128)(2,1)S(1)}, u32[]{:S(2)}, u32[]{:S(2)}) collective-permute-start(bf16[20,7,16,128]{3,2,1,0:T(8,128)(2,1)S(1)} %get-tuple-element.15.refs_1_), channel_id=1, source_target_pairs={{0,128},{1,129},{2,130},{3,131},{4,132},{5,133},{6,134},{7,135},{8... | collective-permute-start | bytes 1720328 | tf_op jit(solution)/shard_map/ppermute | solution.py:63
  42.9 13.8 %collective-permute-start.4 = (bf16[20,7,16,128]{3,2,1,0:T(8,128)(2,1)S(1)}, bf16[20,7,16,128]{3,2,1,0:T(8,128)(2,1)S(1)}, u32[]{:S(2)}, u32[]{:S(2)}) collective-permute-start(bf16[20,7,16,128]{3,2,1,0:T(8,128)(2,1)S(1)} %get-tuple-element.15.refs_1_), channel_id=1, source_target_pairs={{0,1},{1,2},{2,3},{3,0},{4,5},{5,6},{6,7},{7,4},{8,9},{9,10},{10,1... | collective-permute-start | bytes 1720328 | tf_op jit(solution)/shard_map/ppermute | solution.py:53
  46.9 10.4 %collective-permute-start.16 = (bf16[20,7,16,128]{3,2,1,0:T(8,128)(2,1)S(1)}, bf16[20,7,16,128]{3,2,1,0:T(8,128)(2,1)S(1)}, u32[]{:S(2)}, u32[]{:S(2)}) collective-permute-start(bf16[20,7,16,128]{3,2,1,0:T(8,128)(2,1)S(1)} %collective-permute-done.5.refs_4_), channel_id=1, source_target_pairs={{0,128},{1,129},{2,130},{3,131},{4,132},{5,133},{6,134},{7,135},{8... | collective-permute-start | bytes 1720328 | tf_op jit(solution)/shard_map/ppermute | solution.py:63
  50.6 12.3 %collective-permute-start.7 = (bf16[20,7,16,128]{3,2,1,0:T(8,128)(2,1)S(1)}, bf16[20,7,16,128]{3,2,1,0:T(8,128)(2,1)S(1)}, u32[]{:S(2)}, u32[]{:S(2)}) collective-permute-start(bf16[20,7,16,128]{3,2,1,0:T(8,128)(2,1)S(1)} %collective-permute-done.3.refs_2_), channel_id=1, source_target_pairs={{0,1},{1,2},{2,3},{3,0},{4,5},{5,6},{6,7},{7,4},{8,9},{9,10},{10,1... | collective-permute-start | bytes 1720328 | tf_op jit(solution)/shard_map/ppermute | solution.py:53
  53.1 10.9 %collective-permute-start.8 = (bf16[20,7,16,128]{3,2,1,0:T(8,128)(2,1)S(1)}, bf16[20,7,16,128]{3,2,1,0:T(8,128)(2,1)S(1)}, u32[]{:S(2)}, u32[]{:S(2)}) collective-permute-start(bf16[20,7,16,128]{3,2,1,0:T(8,128)(2,1)S(1)} %collective-permute-done.6.refs_5_), channel_id=1, source_target_pairs={{0,3},{1,0},{2,1},{3,2},{4,7},{5,4},{6,5},{7,6},{8,11},{9,8},{10,9... | collective-permute-start | bytes 1720328 | tf_op jit(solution)/shard_map/ppermute | solution.py:53
  56.7 8.2 %collective-permute-start.14 = (bf16[20,7,16,128]{3,2,1,0:T(8,128)(2,1)S(1)}, bf16[20,7,16,128]{3,2,1,0:T(8,128)(2,1)S(1)}, u32[]{:S(2)}, u32[]{:S(2)}) collective-permute-start(bf16[20,7,16,128]{3,2,1,0:T(8,128)(2,1)S(1)} %collective-permute-done.3.refs_2_), channel_id=1, source_target_pairs={{0,128},{1,129},{2,130},{3,131},{4,132},{5,133},{6,134},{7,135},{8... | collective-permute-start | bytes 1720328 | tf_op jit(solution)/shard_map/ppermute | solution.py:63
  56.8 9.8 %collective-permute-start.17 = (bf16[20,7,16,128]{3,2,1,0:T(8,128)(2,1)S(1)}, bf16[20,7,16,128]{3,2,1,0:T(8,128)(2,1)S(1)}, u32[]{:S(2)}, u32[]{:S(2)}) collective-permute-start(bf16[20,7,16,128]{3,2,1,0:T(8,128)(2,1)S(1)} %collective-permute-done.6.refs_5_), channel_id=1, source_target_pairs={{0,128},{1,129},{2,130},{3,131},{4,132},{5,133},{6,134},{7,135},{8... | collective-permute-start | bytes 1720328 | tf_op jit(solution)/shard_map/ppermute | solution.py:63
  57.3 10.5 %collective-permute-start.15 = (bf16[20,7,16,128]{3,2,1,0:T(8,128)(2,1)S(1)}, bf16[20,7,16,128]{3,2,1,0:T(8,128)(2,1)S(1)}, u32[]{:S(2)}, u32[]{:S(2)}) collective-permute-start(bf16[20,7,16,128]{3,2,1,0:T(8,128)(2,1)S(1)} %collective-permute-done.4.refs_3_), channel_id=1, source_target_pairs={{0,128},{1,129},{2,130},{3,131},{4,132},{5,133},{6,134},{7,135},{8... | collective-permute-start | bytes 1720328 | tf_op jit(solution)/shard_map/ppermute | solution.py:63
  62.9 5.7 %collective-permute-start.18 = (bf16[20,7,16,128]{3,2,1,0:T(8,128)(2,1)S(1)}, bf16[20,7,16,128]{3,2,1,0:T(8,128)(2,1)S(1)}, u32[]{:S(2)}, u32[]{:S(2)}) collective-permute-start(bf16[20,7,16,128]{3,2,1,0:T(8,128)(2,1)S(1)} %collective-permute-done.7.refs_6_), channel_id=1, source_target_pairs={{0,128},{1,129},{2,130},{3,131},{4,132},{5,133},{6,134},{7,135},{8... | collective-permute-start | bytes 1720328 | tf_op jit(solution)/shard_map/ppermute | solution.py:63
  64.0 4.7 %collective-permute-start.19 = (bf16[20,7,16,128]{3,2,1,0:T(8,128)(2,1)S(1)}, bf16[20,7,16,128]{3,2,1,0:T(8,128)(2,1)S(1)}, u32[]{:S(2)}, u32[]{:S(2)}) collective-permute-start(bf16[20,7,16,128]{3,2,1,0:T(8,128)(2,1)S(1)} %collective-permute-done.8.refs_7_), channel_id=1, source_target_pairs={{0,128},{1,129},{2,130},{3,131},{4,132},{5,133},{6,134},{7,135},{8... | collective-permute-start | bytes 1720328 | tf_op jit(solution)/shard_map/ppermute | solution.py:63
  65.0 18.2 %collective-permute-start.11 = (bf16[32,7,16,128]{3,2,1,0:T(8,128)(2,1)}, bf16[32,7,16,128]{3,2,1,0:T(8,128)(2,1)S(1)}, u32[]{:S(2)}, u32[]{:S(2)}) collective-permute-start(bf16[32,7,16,128]{3,2,1,0:T(8,128)(2,1)} %temporal_blocks.1.refs_0_), channel_id=1, source_target_pairs={{0,64},{1,65},{2,66},{3,67},{4,68},{5,69},{6,70},{7,71},{8,72},{9,... | collective-permute-start | bytes 2752520 | tf_op jit(solution)/shard_map/ppermute | solution.py:47
  66.6 24.9 %collective-permute-start.10 = (bf16[32,7,16,128]{3,2,1,0:T(8,128)(2,1)}, bf16[32,7,16,128]{3,2,1,0:T(8,128)(2,1)S(1)}, u32[]{:S(2)}, u32[]{:S(2)}) collective-permute-start(bf16[32,7,16,128]{3,2,1,0:T(8,128)(2,1)} %temporal_blocks.1.refs_0_), channel_id=1, source_target_pairs={{0,96},{1,97},{2,98},{3,99},{4,100},{5,101},{6,102},{7,103},{8,104... | collective-permute-start | bytes 2752520 | tf_op jit(solution)/shard_map/ppermute | solution.py:47
  67.8 24.9 %collective-permute-start.9 = (bf16[32,7,16,128]{3,2,1,0:T(8,128)(2,1)}, bf16[32,7,16,128]{3,2,1,0:T(8,128)(2,1)S(1)}, u32[]{:S(2)}, u32[]{:S(2)}) collective-permute-start(bf16[32,7,16,128]{3,2,1,0:T(8,128)(2,1)} %temporal_blocks.1.refs_0_), channel_id=1, source_target_pairs={{0,32},{1,33},{2,34},{3,35},{4,36},{5,37},{6,38},{7,39},{8,40},{9,... | collective-permute-start | bytes 2752520 | tf_op jit(solution)/shard_map/ppermute | solution.py:47
  73.5 24.1 %all-to-all-start.1 = ((bf16[128,5,2,128]{3,2,1,0:T(2,128)(2,1)}), bf16[128,5,2,128]{3,2,1,0:T(2,128)(2,1)S(1)}, u32[]{:S(2)}, u32[]{:S(2)}) async-start(bf16[128,5,2,128]{3,2,1,0:T(2,128)(2,1)} %get-tuple-element.16), calls=%async_computation.1 | async-start | bytes 655360 | tf_op jit(solution)/shard_map/all_to_all | solution.py:415
  83.1 17.4 %collective-permute-start.20 = (bf16[32,7,16,128]{3,2,1,0:T(8,128)(2,1)}, bf16[32,7,16,128]{3,2,1,0:T(8,128)(2,1)}, u32[]{:S(2)}, u32[]{:S(2)}) collective-permute-start(bf16[32,7,16,128]{3,2,1,0:T(8,128)(2,1)} %temporal_blocks.1.refs_0_), channel_id=1, source_target_pairs={{0,128},{1,129},{2,130},{3,131},{4,132},{5,133},{6,134},{7,135},{8... | collective-permute-start | bytes 2752520 | tf_op jit(solution)/shard_map/ppermute | solution.py:63
  97.7 2.8 %collective-permute-start.21 = (bf16[32,7,16,128]{3,2,1,0:T(8,128)(2,1)S(1)}, bf16[32,7,16,128]{3,2,1,0:T(8,128)(2,1)S(1)}, u32[]{:S(2)}, u32[]{:S(2)}) collective-permute-start(bf16[32,7,16,128]{3,2,1,0:T(8,128)(2,1)S(1)} %get-tuple-element.17.refs_1_), channel_id=1, source_target_pairs={{0,128},{1,129},{2,130},{3,131},{4,132},{5,133},{6,134},{7,135},{8... | collective-permute-start | bytes 2752520 | tf_op jit(solution)/shard_map/ppermute | solution.py:63
  97.7 3.8 %collective-permute-start.22 = (bf16[32,7,16,128]{3,2,1,0:T(8,128)(2,1)S(1)}, bf16[32,7,16,128]{3,2,1,0:T(8,128)(2,1)S(1)}, u32[]{:S(2)}, u32[]{:S(2)}) collective-permute-start(bf16[32,7,16,128]{3,2,1,0:T(8,128)(2,1)S(1)} %get-tuple-element.18.refs_2_), channel_id=1, source_target_pairs={{0,128},{1,129},{2,130},{3,131},{4,132},{5,133},{6,134},{7,135},{8... | collective-permute-start | bytes 2752520 | tf_op jit(solution)/shard_map/ppermute | solution.py:63
  98.2 4.6 %collective-permute-start.23 = (bf16[32,7,16,128]{3,2,1,0:T(8,128)(2,1)S(1)}, bf16[32,7,16,128]{3,2,1,0:T(8,128)(2,1)S(1)}, u32[]{:S(2)}, u32[]{:S(2)}) collective-permute-start(bf16[32,7,16,128]{3,2,1,0:T(8,128)(2,1)S(1)} %get-tuple-element.19.refs_3_), channel_id=1, source_target_pairs={{0,128},{1,129},{2,130},{3,131},{4,132},{5,133},{6,134},{7,135},{8... | collective-permute-start | bytes 2752520 | tf_op jit(solution)/shard_map/ppermute | solution.py:63

commit v7 on v5

--- a/solution.py
+++ b/solution.py
@@ -266,11 +266,11 @@
 def heads(rows, scores, attn):
     keys = scores.shape[1]
     for h in range(HEADS):
-        q = rows[64 * h : 64 * (h + 1), 0:128].astype(BF)
+        q = (rows[64 * h : 64 * (h + 1), 0:128].astype(BF) * (HEAD**-0.5)).astype(BF)
         k = rows[640 + 64 * h : 640 + 64 * (h + 1), 0:keys].astype(BF)
         scores[h] = dot(k, q, (((0,), (0,)), ((), ())))
     for h in range(HEADS):
-        st = scores[h] * (HEAD**-0.5)
+        st = scores[h]
         e = jnp.exp(st - jnp.max(st, axis=0, keepdims=True))
         p = (e * (1.0 / jnp.sum(e, axis=0, keepdims=True))).astype(BF)
         v = rows[1280 + 64 * h : 1280 + 64 * (h + 1), 0:keys].astype(BF)

time: 129 us -> 129 us (level)
  no operation moved by 1% of the time
where the time goes in v7:
time: 129 us
  blocking collectives  42.9 us (33%)
  waiting for transfers between devices  40 us (31%)
  starting transfers between devices  29.7 us (23%)
  Pallas kernels  15.7 us (12%)
    all_to_all x1, blocking collectives, body(): lax.all_to_all(packed, 'seq', 0, 0, axis_index_groups=Z_GROUPS, tiled=True)  23.2 us
    all_to_all x1, blocking collectives, body(): back = lax.all_to_all(tattn, 'seq', 0, 0, tiled=True)  19.7 us
    ppermute x6, waiting for transfers between devices, shift(): return lax.ppermute(part, ('clip', 'seq'), ring_perm(k, stage))  16.7 us
    ppermute x6, waiting for transfers between devices, ring(): lax.ppermute(block, ('clip', 'seq'), ring_perm(k, stage))  15.5 us
    pallas_call x3, Pallas kernels, call(): pl.pallas_call(kernel, out_shape=shapes[0] if single else shapes, in_spec...  10 us
    ppermute x6, starting transfers between devices, shift(): return lax.ppermute(part, ('clip', 'seq'), ring_perm(k, stage))  10 us
    all_to_all x1, starting transfers between devices, body(): tokens = lax.all_to_all(tnormed, 'seq', 0, 0, tiled=True)  9.59 us
    ppermute x6, starting transfers between devices, ring(): lax.ppermute(block, ('clip', 'seq'), ring_perm(k, stage))  8.77 us
  transfers between devices with their start and end apart: 25, of which 13 were waited for; matrix products, arithmetic and copies ran while one was open for 0% of the time, Pallas kernels for 6%

profile of v7, /device:TPU:32, one launch (start us, length us, event | category | flops | bytes accessed | tf_op | source)
XLA Modules:
  0.0 128.7 jit_solution(10391263801964859165)
XLA Ops:
  0.0 1.7 %pack.1 = bf16[8,14,16,128]{3,2,1,0:T(8,128)(2,1)} custom-call(bf16[15,1280]{1,0:T(8,128)(2,1)} %bitcast.7, bf16[1,1280]{1,0:T(2,128)(2,1)} %ref_in.1, bf16[10,640]{1,0:T(8,128)(2,1)} %bitcast.9, bf16[15,1280]{1,0:T(8,128)(2,1)} %bitcast.8, bf16[10,640]{1,0:T(8,128)(2,1)} %bitcast.10), custom_call_target="tpu_custom_call" | custom-call | tf_op jit(solution)/shard_map/pack/pallas_call | solution.py:370
  1.7 23.2 %all_to_all.15.along_z = bf16[8,14,16,128]{3,2,1,0:T(8,128)(2,1)S(1)} all-to-all(bf16[8,14,16,128]{3,2,1,0:T(8,128)(2,1)} %pack.1), channel_id=1, replica_groups={{0,4,8,12,16,20,24,28},{1,5,9,13,17,21,25,29},{2,6,10,14,18,22,26,30},{..., dimensions={0} | all-to-all | bytes 917504 | tf_op jit(solution)/shard_map/all_to_all | solution.py:379
  24.9 3.1 %collective-permute-start.2 = (bf16[8,7,16,128]{3,2,1,0:T(8,128)(2,1)S(1)}, bf16[8,7,16,128]{3,2,1,0:T(8,128)(2,1)S(1)}, u32[]{:S(2)}, u32[]{:S(2)}) collective-permute-start(bf16[8,7,16,128]{3,2,1,0:T(8,128)(2,1)S(1)} %slice.4), channel_id=1, source_target_pairs={{0,64},{1,65},{2,66},{3,67},{4,68},{5,69},{6,70},{7,71},{8,72},{9,... | collective-permute-start | bytes 688136 | tf_op jit(solution)/shard_map/ppermute | solution.py:47
  28.0 1.1 collective-permute-start.1
  29.2 0.9 collective-permute-start
  30.1 2.5 %collective-permute-done.2.p3 = bf16[8,7,16,128]{3,2,1,0:T(8,128)(2,1)S(1)} collective-permute-done((bf16[8,7,16,128]{3,2,1,0:T(8,128)(2,1)S(1)}, bf16[8,7,16,128]{3,2,1,0:T(8,128)(2,1)S(1)}, u32[]{:S(2)}, u32[]{:S(2)}) %collective-permute-start.2) | collective-permute-done | bytes 229408 | tf_op jit(solution)/shard_map/ppermute | solution.py:47
  32.5 2.5 %collective-permute-done.1.p2 = bf16[8,7,16,128]{3,2,1,0:T(8,128)(2,1)S(1)} collective-permute-done((bf16[8,7,16,128]{3,2,1,0:T(8,128)(2,1)S(1)}, bf16[8,7,16,128]{3,2,1,0:T(8,128)(2,1)S(1)}, u32[]{:S(2)}, u32[]{:S(2)}) %collective-permute-start.1) | collective-permute-done | bytes 229408 | tf_op jit(solution)/shard_map/ppermute | solution.py:47
  35.1 1.3 %collective-permute-done.p1 = bf16[8,7,16,128]{3,2,1,0:T(8,128)(2,1)S(1)} collective-permute-done((bf16[8,7,16,128]{3,2,1,0:T(8,128)(2,1)S(1)}, bf16[8,7,16,128]{3,2,1,0:T(8,128)(2,1)S(1)}, u32[]{:S(2)}, u32[]{:S(2)}) %collective-permute-start) | collective-permute-done | bytes 229408 | tf_op jit(solution)/shard_map/ppermute | solution.py:47
  36.4 0.1 halves.1
  36.5 0.0 copy-start.2
  36.5 0.1 collective-permute-start.12
  36.6 3.1 %collective-permute-start.5 = (bf16[20,7,16,128]{3,2,1,0:T(8,128)(2,1)S(1)}, bf16[20,7,16,128]{3,2,1,0:T(8,128)(2,1)S(1)}, u32[]{:S(2)}, u32[]{:S(2)}) collective-permute-start(bf16[20,7,16,128]{3,2,1,0:T(8,128)(2,1)S(1)} %get-tuple-element.14.refs_0_), channel_id=1, source_target_pairs={{0,3},{1,0},{2,1},{3,2},{4,7},{5,4},{6,5},{7,6},{8,11},{9,8},{10,9... | collective-permute-start | bytes 1720328 | tf_op jit(solution)/shard_map/ppermute | solution.py:53
  39.7 0.0 collective-permute-start.3
  39.7 3.2 %collective-permute-start.6 = (bf16[20,7,16,128]{3,2,1,0:T(8,128)(2,1)S(1)}, bf16[20,7,16,128]{3,2,1,0:T(8,128)(2,1)S(1)}, u32[]{:S(2)}, u32[]{:S(2)}) collective-permute-start(bf16[20,7,16,128]{3,2,1,0:T(8,128)(2,1)S(1)} %get-tuple-element.15.refs_1_), channel_id=1, source_target_pairs={{0,3},{1,0},{2,1},{3,2},{4,7},{5,4},{6,5},{7,6},{8,11},{9,8},{10,9... | collective-permute-start | bytes 1720328 | tf_op jit(solution)/shard_map/ppermute | solution.py:53
  42.9 0.0 collective-permute-start.13
  42.9 0.0 collective-permute-done.12.refs_8_
  42.9 0.0 collective-permute-start.4
  42.9 4.0 %collective-permute-done.5.refs_4_ = bf16[20,7,16,128]{3,2,1,0:T(8,128)(2,1)S(1)} collective-permute-done((bf16[20,7,16,128]{3,2,1,0:T(8,128)(2,1)S(1)}, bf16[20,7,16,128]{3,2,1,0:T(8,128)(2,1)S(1)}, u32[]{:S(2)}, u32[]{:S(2)}) %collective-permute-start.5) | collective-permute-done | bytes 573472 | tf_op jit(solution)/shard_map/ppermute | solution.py:53
  46.9 0.0 collective-permute-start.16
  46.9 3.7 %collective-permute-done.3.refs_2_ = bf16[20,7,16,128]{3,2,1,0:T(8,128)(2,1)S(1)} collective-permute-done((bf16[20,7,16,128]{3,2,1,0:T(8,128)(2,1)S(1)}, bf16[20,7,16,128]{3,2,1,0:T(8,128)(2,1)S(1)}, u32[]{:S(2)}, u32[]{:S(2)}) %collective-permute-start.3) | collective-permute-done | bytes 573472 | tf_op jit(solution)/shard_map/ppermute | solution.py:53
  50.6 0.0 collective-permute-start.7
  50.6 2.4 %collective-permute-done.6.refs_5_ = bf16[20,7,16,128]{3,2,1,0:T(8,128)(2,1)S(1)} collective-permute-done((bf16[20,7,16,128]{3,2,1,0:T(8,128)(2,1)S(1)}, bf16[20,7,16,128]{3,2,1,0:T(8,128)(2,1)S(1)}, u32[]{:S(2)}, u32[]{:S(2)}) %collective-permute-start.6) | collective-permute-done | bytes 573472 | tf_op jit(solution)/shard_map/ppermute | solution.py:53
  53.1 3.7 %collective-permute-start.8 = (bf16[20,7,16,128]{3,2,1,0:T(8,128)(2,1)S(1)}, bf16[20,7,16,128]{3,2,1,0:T(8,128)(2,1)S(1)}, u32[]{:S(2)}, u32[]{:S(2)}) collective-permute-start(bf16[20,7,16,128]{3,2,1,0:T(8,128)(2,1)S(1)} %collective-permute-done.6.refs_5_), channel_id=1, source_target_pairs={{0,3},{1,0},{2,1},{3,2},{4,7},{5,4},{6,5},{7,6},{8,11},{9,8},{10,9... | collective-permute-start | bytes 1720328 | tf_op jit(solution)/shard_map/ppermute | solution.py:53
  56.8 0.0 collective-permute-done.13.refs_9_
  56.8 0.0 collective-permute-start.14
  56.8 0.0 collective-permute-done.4.refs_3_
  56.8 0.5 collective-permute-start.17
  57.3 0.0 collective-permute-done.16.refs_12_
  57.3 0.1 collective-permute-start.15
  57.4 5.5 %collective-permute-done.7.refs_6_ = bf16[20,7,16,128]{3,2,1,0:T(8,128)(2,1)S(1)} collective-permute-done((bf16[20,7,16,128]{3,2,1,0:T(8,128)(2,1)S(1)}, bf16[20,7,16,128]{3,2,1,0:T(8,128)(2,1)S(1)}, u32[]{:S(2)}, u32[]{:S(2)}) %collective-permute-start.7) | collective-permute-done | bytes 573472 | tf_op jit(solution)/shard_map/ppermute | solution.py:53
  62.9 0.0 collective-permute-start.18
  62.9 1.1 collective-permute-done.8.refs_7_
  64.0 0.0 collective-permute-start.19
  64.0 0.0 copy-done.1
  64.0 0.0 copy-done.2
  64.0 0.0 copy-start
  64.0 1.0 temporal_blocks.1.refs_0_
  65.0 0.0 collective-permute-done.14.refs_10_
  65.0 1.6 %collective-permute-start.11 = (bf16[32,7,16,128]{3,2,1,0:T(8,128)(2,1)}, bf16[32,7,16,128]{3,2,1,0:T(8,128)(2,1)S(1)}, u32[]{:S(2)}, u32[]{:S(2)}) collective-permute-start(bf16[32,7,16,128]{3,2,1,0:T(8,128)(2,1)} %temporal_blocks.1.refs_0_), channel_id=1, source_target_pairs={{0,64},{1,65},{2,66},{3,67},{4,68},{5,69},{6,70},{7,71},{8,72},{9,... | collective-permute-start | bytes 2752520 | tf_op jit(solution)/shard_map/ppermute | solution.py:47
  66.6 0.0 collective-permute-done.17.refs_13_
  66.6 1.2 collective-permute-start.10
  67.8 0.0 collective-permute-done.15.refs_11_
  67.8 0.9 collective-permute-start.9
  68.7 0.0 collective-permute-done.18.refs_14_
  68.7 0.0 collective-permute-done.19.refs_15_
  68.7 0.0 copy-done
  68.7 5.0 %spatial.1 = (bf16[128,1280]{1,0:T(8,128)(2,1)S(1)}, bf16[128,5,2,128]{3,2,1,0:T(2,128)(2,1)}) custom-call(bf16[20,7,16,128]{3,2,1,0:T(8,128)(2,1)S(1)} %get-tuple-element.14.refs_0_, bf16[20,7,16,128]{3,2,1,0:T(8,128)(2,1)S(1)} %get-tuple-element.15.refs_1_, bf16[20,7,16,128]{3,2,1,0:T(8,128)(2,1)S(1)} %collective-permute-done.3.refs_2_, ...), custom_call_target="tpu_custom_call" | custom-call | flops 8999999488 | bytes 10168320 | tf_op jit(solution)/shard_map/spatial/pallas_call | solution.py:353
  73.7 9.6 %all-to-all-start.1 = ((bf16[128,5,2,128]{3,2,1,0:T(2,128)(2,1)}), bf16[128,5,2,128]{3,2,1,0:T(2,128)(2,1)S(1)}, u32[]{:S(2)}, u32[]{:S(2)}) async-start(bf16[128,5,2,128]{3,2,1,0:T(2,128)(2,1)} %get-tuple-element.16), calls=%async_computation.1 | async-start | bytes 655360 | tf_op jit(solution)/shard_map/all_to_all | solution.py:410
  83.3 0.1 collective-permute-start.20
  83.4 0.0 collective-permute-done.11.refs_2_
  83.4 8.0 %collective-permute-done.10.refs_1_ = bf16[32,7,16,128]{3,2,1,0:T(8,128)(2,1)S(1)} collective-permute-done((bf16[32,7,16,128]{3,2,1,0:T(8,128)(2,1)}, bf16[32,7,16,128]{3,2,1,0:T(8,128)(2,1)S(1)}, u32[]{:S(2)}, u32[]{:S(2)}) %collective-permute-start.10) | collective-permute-done | bytes 917536 | tf_op jit(solution)/shard_map/ppermute | solution.py:47
  91.4 1.2 collective-permute-done.9.refs_0_
  92.6 5.4 %all-to-all-done.1.refs_3_.refs_4_ = bf16[128,5,2,128]{3,2,1,0:T(2,128)(2,1)S(1)} async-done(((bf16[128,5,2,128]{3,2,1,0:T(2,128)(2,1)}), bf16[128,5,2,128]{3,2,1,0:T(2,128)(2,1)S(1)}, u32[]{:S(2)}, u32[]{:S(2)}) %all-to-all-start.1) | async-done | bytes 327712 | tf_op jit(solution)/shard_map/all_to_all | solution.py:410
  98.0 0.0 collective-permute-start.21
  98.0 0.5 collective-permute-start.22
  98.5 0.0 collective-permute-start.23
  98.5 2.3 %half.1 = (f32[2048,128]{1,0:T(8,128)S(1)}, bf16[128,640]{1,0:T(8,128)(2,1)S(1)}) custom-call(bf16[32,7,16,128]{3,2,1,0:T(8,128)(2,1)} %temporal_blocks.1.refs_0_, bf16[32,7,16,128]{3,2,1,0:T(8,128)(2,1)S(1)} %get-tuple-element.17.refs_1_, bf16[32,7,16,128]{3,2,1,0:T(8,128)(2,1)S(1)} %get-tuple-element.18.refs_2_, ...), custom_call_target="tpu_custom_call" | custom-call | flops 3000000000 | bytes 4685824 | tf_op jit(solution)/shard_map/half/pallas_call | solution.py:353
  100.8 0.0 collective-permute-done.20.refs_0_.refs_4_
  100.8 0.0 collective-permute-done.21.refs_1_.refs_5_
  100.8 1.0 collective-permute-done.22.refs_2_.refs_6_
  101.8 1.3 %collective-permute-done.23.refs_3_.refs_7_ = bf16[32,7,16,128]{3,2,1,0:T(8,128)(2,1)S(1)} collective-permute-done((bf16[32,7,16,128]{3,2,1,0:T(8,128)(2,1)S(1)}, bf16[32,7,16,128]{3,2,1,0:T(8,128)(2,1)S(1)}, u32[]{:S(2)}, u32[]{:S(2)}) %collective-permute-start.23) | collective-permute-done | bytes 917536 | tf_op jit(solution)/shard_map/ppermute | solution.py:63
  103.1 2.8 %temporal.1 = bf16[128,3,2,128]{3,2,1,0:T(2,128)(2,1)S(1)} custom-call(bf16[32,7,16,128]{3,2,1,0:T(8,128)(2,1)} %collective-permute-done.20.refs_0_.refs_4_, bf16[32,7,16,128]{3,2,1,0:T(8,128)(2,1)S(1)} %collective-permute-done.21.refs_1_.refs_5_, bf16[32,7,16,128]{3,2,1,0:T(8,128)(2,1)S(1)} %collective-permute-done.22.refs_2_.refs_6_, ...), custom_call_target="tpu_custom_call" | custom-call | flops 5000000000 | bytes 5079040 | tf_op jit(solution)/shard_map/temporal/pallas_call | solution.py:353
  105.9 19.7 %all_to_all.16.refs_8_ = bf16[128,3,2,128]{3,2,1,0:T(2,128)(2,1)S(1)} all-to-all(bf16[128,3,2,128]{3,2,1,0:T(2,128)(2,1)S(1)} %temporal.1), channel_id=1, replica_groups=mesh['clip'=2,'seq'=128] {'seq'}, dimensions={0} | all-to-all | bytes 393216 | tf_op jit(solution)/shard_map/all_to_all | solution.py:438
  125.6 2.9 %mixed.1 = bf16[128,1280]{1,0:T(8,128)(2,1)} custom-call(bf16[32,7,16,128]{3,2,1,0:T(8,128)(2,1)} %temporal_blocks.1.refs_0_, bf16[32,7,16,128]{3,2,1,0:T(8,128)(2,1)S(1)} %get-tuple-element.17.refs_1_, bf16[32,7,16,128]{3,2,1,0:T(8,128)(2,1)S(1)} %get-tuple-element.18.refs_2_, bf16[32,7,16,128]{3,2,1,0:T(8,128)(2,1)S(1)} %get-tuple-element.19.refs_3_, ...), custom_call_target="tpu_custom_call" | custom-call | flops 3000000000 | bytes 10000000 | tf_op jit(solution)/shard_map/mixed/pallas_call | solution.py:439
  (5 shorter events, 0.0 us)
Async XLA Ops:
  24.9 7.6 %collective-permute-start.2 = (bf16[8,7,16,128]{3,2,1,0:T(8,128)(2,1)S(1)}, bf16[8,7,16,128]{3,2,1,0:T(8,128)(2,1)S(1)}, u32[]{:S(2)}, u32[]{:S(2)}) collective-permute-start(bf16[8,7,16,128]{3,2,1,0:T(8,128)(2,1)S(1)} %slice.4), channel_id=1, source_target_pairs={{0,64},{1,65},{2,66},{3,67},{4,68},{5,69},{6,70},{7,71},{8,72},{9,... | collective-permute-start | bytes 688136 | tf_op jit(solution)/shard_map/ppermute | solution.py:47
  28.0 7.0 %collective-permute-start.1 = (bf16[8,7,16,128]{3,2,1,0:T(8,128)(2,1)S(1)}, bf16[8,7,16,128]{3,2,1,0:T(8,128)(2,1)S(1)}, u32[]{:S(2)}, u32[]{:S(2)}) collective-permute-start(bf16[8,7,16,128]{3,2,1,0:T(8,128)(2,1)S(1)} %slice.4), channel_id=1, source_target_pairs={{0,96},{1,97},{2,98},{3,99},{4,100},{5,101},{6,102},{7,103},{8,104... | collective-permute-start | bytes 688136 | tf_op jit(solution)/shard_map/ppermute | solution.py:47
  29.2 7.2 %collective-permute-start = (bf16[8,7,16,128]{3,2,1,0:T(8,128)(2,1)S(1)}, bf16[8,7,16,128]{3,2,1,0:T(8,128)(2,1)S(1)}, u32[]{:S(2)}, u32[]{:S(2)}) collective-permute-start(bf16[8,7,16,128]{3,2,1,0:T(8,128)(2,1)S(1)} %slice.4), channel_id=1, source_target_pairs={{0,32},{1,33},{2,34},{3,35},{4,36},{5,37},{6,38},{7,39},{8,40},{9,... | collective-permute-start | bytes 688136 | tf_op jit(solution)/shard_map/ppermute | solution.py:47
  36.4 27.6 %copy-start.1 = (f32[1280]{0:T(1024)S(1)}, f32[1280]{0:T(1024)}, u32[]{:S(2)}) copy-start(f32[1280]{0:T(1024)} %param.10) | copy-start | bytes 15364
  36.5 27.5 %copy-start.2 = (f32[1280]{0:T(1024)S(1)}, f32[1280]{0:T(1024)}, u32[]{:S(2)}) copy-start(f32[1280]{0:T(1024)} %param.13) | copy-start | bytes 15364
  36.5 6.4 %collective-permute-start.12 = (bf16[20,7,16,128]{3,2,1,0:T(8,128)(2,1)S(1)}, bf16[20,7,16,128]{3,2,1,0:T(8,128)(2,1)S(1)}, u32[]{:S(2)}, u32[]{:S(2)}) collective-permute-start(bf16[20,7,16,128]{3,2,1,0:T(8,128)(2,1)S(1)} %get-tuple-element.14.refs_0_), channel_id=1, source_target_pairs={{0,128},{1,129},{2,130},{3,131},{4,132},{5,133},{6,134},{7,135},{8... | collective-permute-start | bytes 1720328 | tf_op jit(solution)/shard_map/ppermute | solution.py:63
  36.6 10.3 %collective-permute-start.5 = (bf16[20,7,16,128]{3,2,1,0:T(8,128)(2,1)S(1)}, bf16[20,7,16,128]{3,2,1,0:T(8,128)(2,1)S(1)}, u32[]{:S(2)}, u32[]{:S(2)}) collective-permute-start(bf16[20,7,16,128]{3,2,1,0:T(8,128)(2,1)S(1)} %get-tuple-element.14.refs_0_), channel_id=1, source_target_pairs={{0,3},{1,0},{2,1},{3,2},{4,7},{5,4},{6,5},{7,6},{8,11},{9,8},{10,9... | collective-permute-start | bytes 1720328 | tf_op jit(solution)/shard_map/ppermute | solution.py:53
  39.7 10.9 %collective-permute-start.3 = (bf16[20,7,16,128]{3,2,1,0:T(8,128)(2,1)S(1)}, bf16[20,7,16,128]{3,2,1,0:T(8,128)(2,1)S(1)}, u32[]{:S(2)}, u32[]{:S(2)}) collective-permute-start(bf16[20,7,16,128]{3,2,1,0:T(8,128)(2,1)S(1)} %get-tuple-element.14.refs_0_), channel_id=1, source_target_pairs={{0,1},{1,2},{2,3},{3,0},{4,5},{5,6},{6,7},{7,4},{8,9},{9,10},{10,1... | collective-permute-start | bytes 1720328 | tf_op jit(solution)/shard_map/ppermute | solution.py:53
  39.7 13.4 %collective-permute-start.6 = (bf16[20,7,16,128]{3,2,1,0:T(8,128)(2,1)S(1)}, bf16[20,7,16,128]{3,2,1,0:T(8,128)(2,1)S(1)}, u32[]{:S(2)}, u32[]{:S(2)}) collective-permute-start(bf16[20,7,16,128]{3,2,1,0:T(8,128)(2,1)S(1)} %get-tuple-element.15.refs_1_), channel_id=1, source_target_pairs={{0,3},{1,0},{2,1},{3,2},{4,7},{5,4},{6,5},{7,6},{8,11},{9,8},{10,9... | collective-permute-start | bytes 1720328 | tf_op jit(solution)/shard_map/ppermute | solution.py:53
  42.9 13.8 %collective-permute-start.13 = (bf16[20,7,16,128]{3,2,1,0:T(8,128)(2,1)S(1)}, bf16[20,7,16,128]{3,2,1,0:T(8,128)(2,1)S(1)}, u32[]{:S(2)}, u32[]{:S(2)}) collective-permute-start(bf16[20,7,16,128]{3,2,1,0:T(8,128)(2,1)S(1)} %get-tuple-element.15.refs_1_), channel_id=1, source_target_pairs={{0,128},{1,129},{2,130},{3,131},{4,132},{5,133},{6,134},{7,135},{8... | collective-permute-start | bytes 1720328 | tf_op jit(solution)/shard_map/ppermute | solution.py:63
  42.9 13.8 %collective-permute-start.4 = (bf16[20,7,16,128]{3,2,1,0:T(8,128)(2,1)S(1)}, bf16[20,7,16,128]{3,2,1,0:T(8,128)(2,1)S(1)}, u32[]{:S(2)}, u32[]{:S(2)}) collective-permute-start(bf16[20,7,16,128]{3,2,1,0:T(8,128)(2,1)S(1)} %get-tuple-element.15.refs_1_), channel_id=1, source_target_pairs={{0,1},{1,2},{2,3},{3,0},{4,5},{5,6},{6,7},{7,4},{8,9},{9,10},{10,1... | collective-permute-start | bytes 1720328 | tf_op jit(solution)/shard_map/ppermute | solution.py:53
  46.9 10.4 %collective-permute-start.16 = (bf16[20,7,16,128]{3,2,1,0:T(8,128)(2,1)S(1)}, bf16[20,7,16,128]{3,2,1,0:T(8,128)(2,1)S(1)}, u32[]{:S(2)}, u32[]{:S(2)}) collective-permute-start(bf16[20,7,16,128]{3,2,1,0:T(8,128)(2,1)S(1)} %collective-permute-done.5.refs_4_), channel_id=1, source_target_pairs={{0,128},{1,129},{2,130},{3,131},{4,132},{5,133},{6,134},{7,135},{8... | collective-permute-start | bytes 1720328 | tf_op jit(solution)/shard_map/ppermute | solution.py:63
  50.6 12.3 %collective-permute-start.7 = (bf16[20,7,16,128]{3,2,1,0:T(8,128)(2,1)S(1)}, bf16[20,7,16,128]{3,2,1,0:T(8,128)(2,1)S(1)}, u32[]{:S(2)}, u32[]{:S(2)}) collective-permute-start(bf16[20,7,16,128]{3,2,1,0:T(8,128)(2,1)S(1)} %collective-permute-done.3.refs_2_), channel_id=1, source_target_pairs={{0,1},{1,2},{2,3},{3,0},{4,5},{5,6},{6,7},{7,4},{8,9},{9,10},{10,1... | collective-permute-start | bytes 1720328 | tf_op jit(solution)/shard_map/ppermute | solution.py:53
  53.1 10.9 %collective-permute-start.8 = (bf16[20,7,16,128]{3,2,1,0:T(8,128)(2,1)S(1)}, bf16[20,7,16,128]{3,2,1,0:T(8,128)(2,1)S(1)}, u32[]{:S(2)}, u32[]{:S(2)}) collective-permute-start(bf16[20,7,16,128]{3,2,1,0:T(8,128)(2,1)S(1)} %collective-permute-done.6.refs_5_), channel_id=1, source_target_pairs={{0,3},{1,0},{2,1},{3,2},{4,7},{5,4},{6,5},{7,6},{8,11},{9,8},{10,9... | collective-permute-start | bytes 1720328 | tf_op jit(solution)/shard_map/ppermute | solution.py:53
  56.8 8.3 %collective-permute-start.14 = (bf16[20,7,16,128]{3,2,1,0:T(8,128)(2,1)S(1)}, bf16[20,7,16,128]{3,2,1,0:T(8,128)(2,1)S(1)}, u32[]{:S(2)}, u32[]{:S(2)}) collective-permute-start(bf16[20,7,16,128]{3,2,1,0:T(8,128)(2,1)S(1)} %collective-permute-done.3.refs_2_), channel_id=1, source_target_pairs={{0,128},{1,129},{2,130},{3,131},{4,132},{5,133},{6,134},{7,135},{8... | collective-permute-start | bytes 1720328 | tf_op jit(solution)/shard_map/ppermute | solution.py:63
  56.8 9.9 %collective-permute-start.17 = (bf16[20,7,16,128]{3,2,1,0:T(8,128)(2,1)S(1)}, bf16[20,7,16,128]{3,2,1,0:T(8,128)(2,1)S(1)}, u32[]{:S(2)}, u32[]{:S(2)}) collective-permute-start(bf16[20,7,16,128]{3,2,1,0:T(8,128)(2,1)S(1)} %collective-permute-done.6.refs_5_), channel_id=1, source_target_pairs={{0,128},{1,129},{2,130},{3,131},{4,132},{5,133},{6,134},{7,135},{8... | collective-permute-start | bytes 1720328 | tf_op jit(solution)/shard_map/ppermute | solution.py:63
  57.3 10.5 %collective-permute-start.15 = (bf16[20,7,16,128]{3,2,1,0:T(8,128)(2,1)S(1)}, bf16[20,7,16,128]{3,2,1,0:T(8,128)(2,1)S(1)}, u32[]{:S(2)}, u32[]{:S(2)}) collective-permute-start(bf16[20,7,16,128]{3,2,1,0:T(8,128)(2,1)S(1)} %collective-permute-done.4.refs_3_), channel_id=1, source_target_pairs={{0,128},{1,129},{2,130},{3,131},{4,132},{5,133},{6,134},{7,135},{8... | collective-permute-start | bytes 1720328 | tf_op jit(solution)/shard_map/ppermute | solution.py:63
  62.9 5.8 %collective-permute-start.18 = (bf16[20,7,16,128]{3,2,1,0:T(8,128)(2,1)S(1)}, bf16[20,7,16,128]{3,2,1,0:T(8,128)(2,1)S(1)}, u32[]{:S(2)}, u32[]{:S(2)}) collective-permute-start(bf16[20,7,16,128]{3,2,1,0:T(8,128)(2,1)S(1)} %collective-permute-done.7.refs_6_), channel_id=1, source_target_pairs={{0,128},{1,129},{2,130},{3,131},{4,132},{5,133},{6,134},{7,135},{8... | collective-permute-start | bytes 1720328 | tf_op jit(solution)/shard_map/ppermute | solution.py:63
  64.0 4.7 %collective-permute-start.19 = (bf16[20,7,16,128]{3,2,1,0:T(8,128)(2,1)S(1)}, bf16[20,7,16,128]{3,2,1,0:T(8,128)(2,1)S(1)}, u32[]{:S(2)}, u32[]{:S(2)}) collective-permute-start(bf16[20,7,16,128]{3,2,1,0:T(8,128)(2,1)S(1)} %collective-permute-done.8.refs_7_), channel_id=1, source_target_pairs={{0,128},{1,129},{2,130},{3,131},{4,132},{5,133},{6,134},{7,135},{8... | collective-permute-start | bytes 1720328 | tf_op jit(solution)/shard_map/ppermute | solution.py:63
  64.0 4.7 %copy-start = (bf16[1,128,1280]{2,1,0:T(8,128)(2,1)S(1)}, bf16[1,128,1280]{2,1,0:T(8,128)(2,1)}, u32[]{:S(2)}) copy-start(bf16[1,128,1280]{2,1,0:T(8,128)(2,1)} %param.8) | copy-start | bytes 983044
  65.0 18.4 %collective-permute-start.11 = (bf16[32,7,16,128]{3,2,1,0:T(8,128)(2,1)}, bf16[32,7,16,128]{3,2,1,0:T(8,128)(2,1)S(1)}, u32[]{:S(2)}, u32[]{:S(2)}) collective-permute-start(bf16[32,7,16,128]{3,2,1,0:T(8,128)(2,1)} %temporal_blocks.1.refs_0_), channel_id=1, source_target_pairs={{0,64},{1,65},{2,66},{3,67},{4,68},{5,69},{6,70},{7,71},{8,72},{9,... | collective-permute-start | bytes 2752520 | tf_op jit(solution)/shard_map/ppermute | solution.py:47
  66.6 24.8 %collective-permute-start.10 = (bf16[32,7,16,128]{3,2,1,0:T(8,128)(2,1)}, bf16[32,7,16,128]{3,2,1,0:T(8,128)(2,1)S(1)}, u32[]{:S(2)}, u32[]{:S(2)}) collective-permute-start(bf16[32,7,16,128]{3,2,1,0:T(8,128)(2,1)} %temporal_blocks.1.refs_0_), channel_id=1, source_target_pairs={{0,96},{1,97},{2,98},{3,99},{4,100},{5,101},{6,102},{7,103},{8,104... | collective-permute-start | bytes 2752520 | tf_op jit(solution)/shard_map/ppermute | solution.py:47
  67.8 24.8 %collective-permute-start.9 = (bf16[32,7,16,128]{3,2,1,0:T(8,128)(2,1)}, bf16[32,7,16,128]{3,2,1,0:T(8,128)(2,1)S(1)}, u32[]{:S(2)}, u32[]{:S(2)}) collective-permute-start(bf16[32,7,16,128]{3,2,1,0:T(8,128)(2,1)} %temporal_blocks.1.refs_0_), channel_id=1, source_target_pairs={{0,32},{1,33},{2,34},{3,35},{4,36},{5,37},{6,38},{7,39},{8,40},{9,... | collective-permute-start | bytes 2752520 | tf_op jit(solution)/shard_map/ppermute | solution.py:47
  73.7 24.3 %all-to-all-start.1 = ((bf16[128,5,2,128]{3,2,1,0:T(2,128)(2,1)}), bf16[128,5,2,128]{3,2,1,0:T(2,128)(2,1)S(1)}, u32[]{:S(2)}, u32[]{:S(2)}) async-start(bf16[128,5,2,128]{3,2,1,0:T(2,128)(2,1)} %get-tuple-element.16), calls=%async_computation.1 | async-start | bytes 655360 | tf_op jit(solution)/shard_map/all_to_all | solution.py:410
  83.3 17.5 %collective-permute-start.20 = (bf16[32,7,16,128]{3,2,1,0:T(8,128)(2,1)}, bf16[32,7,16,128]{3,2,1,0:T(8,128)(2,1)}, u32[]{:S(2)}, u32[]{:S(2)}) collective-permute-start(bf16[32,7,16,128]{3,2,1,0:T(8,128)(2,1)} %temporal_blocks.1.refs_0_), channel_id=1, source_target_pairs={{0,128},{1,129},{2,130},{3,131},{4,132},{5,133},{6,134},{7,135},{8... | collective-permute-start | bytes 2752520 | tf_op jit(solution)/shard_map/ppermute | solution.py:63
  98.0 2.8 %collective-permute-start.21 = (bf16[32,7,16,128]{3,2,1,0:T(8,128)(2,1)S(1)}, bf16[32,7,16,128]{3,2,1,0:T(8,128)(2,1)S(1)}, u32[]{:S(2)}, u32[]{:S(2)}) collective-permute-start(bf16[32,7,16,128]{3,2,1,0:T(8,128)(2,1)S(1)} %get-tuple-element.17.refs_1_), channel_id=1, source_target_pairs={{0,128},{1,129},{2,130},{3,131},{4,132},{5,133},{6,134},{7,135},{8... | collective-permute-start | bytes 2752520 | tf_op jit(solution)/shard_map/ppermute | solution.py:63
  98.0 3.8 %collective-permute-start.22 = (bf16[32,7,16,128]{3,2,1,0:T(8,128)(2,1)S(1)}, bf16[32,7,16,128]{3,2,1,0:T(8,128)(2,1)S(1)}, u32[]{:S(2)}, u32[]{:S(2)}) collective-permute-start(bf16[32,7,16,128]{3,2,1,0:T(8,128)(2,1)S(1)} %get-tuple-element.18.refs_2_), channel_id=1, source_target_pairs={{0,128},{1,129},{2,130},{3,131},{4,132},{5,133},{6,134},{7,135},{8... | collective-permute-start | bytes 2752520 | tf_op jit(solution)/shard_map/ppermute | solution.py:63
  98.5 4.6 %collective-permute-start.23 = (bf16[32,7,16,128]{3,2,1,0:T(8,128)(2,1)S(1)}, bf16[32,7,16,128]{3,2,1,0:T(8,128)(2,1)S(1)}, u32[]{:S(2)}, u32[]{:S(2)}) collective-permute-start(bf16[32,7,16,128]{3,2,1,0:T(8,128)(2,1)S(1)} %get-tuple-element.19.refs_3_), channel_id=1, source_target_pairs={{0,128},{1,129},{2,130},{3,131},{4,132},{5,133},{6,134},{7,135},{8... | collective-permute-start | bytes 2752520 | tf_op jit(solution)/shard_map/ppermute | solution.py:63
